TPU v7x, 768 devices: a whole 4x8x12 slice. The times are simulated.
768 devices in a mesh: wide: 24 (over y, z_lo), narrow: 32 (over x, z_hi, core).
Axes of the slice: x: 4, y: 8, z: 12 (z_hi: 4, z_lo: 3; z = z_hi * 3 + z_lo), core: 2. Of those that a mesh axis runs over, the one named last changes fastest.
Arguments:
- integrals: float32 [12288, 24576], P('wide', 'narrow'), may hold values from -0.125 to 0.125
- amplitudes: float32 [24576, 1024], P(('narrow', 'wide')), may hold values from -6 to 6
- row_irrep: int32 [96], P('wide'), may hold values from 0 to 3
- col_irrep: int32 [192], P('narrow'), may hold values from 0 to 3
- partner: int32 [32], replicated, may hold values from 0 to 31, as said below
Outputs:
- ladder: float32 [12288, 1024], P(('wide', 'narrow'))
Inputs may be any that keep to these rules, and one draw needn't show every extreme that they name: partner is an involution without fixed points: partner[partner[n]] == n and partner[n] != n; at least one index n has partner n + 16.
All inputs are finite; a program needn't handle non-finite values.
Results may differ from a plain program's by a relative error of at most 0.0003.
Values sent between devices are 32-bit elements; how exact they have to be, the bound alone decides.
No kernel may reach another device: no remote copies, remote signals or barrier semaphores. Data moves between devices by JAX's collectives and lax.ppermute only.
A program may use at most 32 MiB of HBM per device.

v0:
```python
import jax
import jax.numpy as jnp
from jax import lax
from jax.sharding import PartitionSpec as P

BW = 128
NO = 32


def local(integrals, amplitudes, row_irrep, col_irrep, partner):
    local_rows = amplitudes.shape[0]
    pair_cols = amplitudes.shape[1]
    my_index = lax.axis_index("narrow")
    partner_index = partner[my_index]
    piece = lax.all_gather(amplitudes, "narrow", axis=0, tiled=True)
    count = piece.shape[0]
    offset = partner_index * local_rows
    inside = (offset >= 0) & (offset < count)
    taken = lax.dynamic_slice_in_dim(piece, jnp.clip(offset, 0, count - local_rows), local_rows, 0)
    fetched = jnp.where(inside, taken, jnp.zeros_like(taken))
    swapped = jnp.swapaxes(fetched.reshape(local_rows, NO, NO), 1, 2).reshape(local_rows, pair_cols)
    symmetric = amplitudes + swapped
    tile_rows = integrals.shape[0]
    matches = jnp.repeat(row_irrep, BW)[:, None] == jnp.repeat(col_irrep, BW)[None, :]
    masked = jnp.where(matches, integrals, jnp.zeros_like(integrals))
    partial_sum = jnp.dot(
        masked,
        lax.all_gather(symmetric, "wide", axis=0, tiled=True),
        precision=lax.Precision.HIGHEST,
        preferred_element_type=jnp.float32,
    )
    share_rows = tile_rows // lax.axis_size("narrow")
    summed = lax.psum(partial_sum, "narrow")
    return lax.dynamic_slice_in_dim(summed, my_index * share_rows, share_rows, 0)


def solution(mesh):
    return jax.shard_map(
        local,
        mesh=mesh,
        in_specs=(P("wide", "narrow"), P(("narrow", "wide"), None), P("wide"), P("narrow"), P()),
        out_specs=P(("wide", "narrow"), None),
        check_vma=False,
    )
```

profile of v0, /device:TPU:1, one launch (start us, length us, event | category | flops | bytes accessed | tf_op | source)
XLA Modules:
  0.0 579.8 jit_solution(13682755834590292038)
XLA Ops:
  6.5 0.0 copy-start
  6.5 0.0 copy-start.2
  6.5 0.0 copy-start.3
  6.5 0.0 copy-start.1
  6.5 0.0 all-gather.3.cloned.1.call-start
  6.6 0.7 all-gather.3.cloned.1.call-update
  7.3 0.0 all-gather.5.cloned.1.call-start
  7.3 1.2 dynamic_slice.9
  9.2 94.3 %all-gather.3.cloned.1.call-done = f32[1024,1024]{1,0:T(8,128)} async-done(((f32[32,1024]{1,0:T(8,128)}), f32[1024,1024]{1,0:T(8,128)}) %all-gather.3.cloned.1.call-update) | async-done | bytes 4194320 | tf_op jit(solution)/shard_map/all_gather | solution.py:15
  103.5 0.9 dynamic-slice_select_fusion
  104.4 0.2 reshape.19
  104.6 0.2 copy.6
  104.8 0.2 reshape.20
  105.1 0.0 copy-done.2
  105.1 0.7 add.13
  105.7 0.0 all-gather.5.cloned.1.call-update
  105.8 0.0 all-reduce.2.cloned.1.call-start
  105.8 0.0 copy-done.3
  105.8 0.1 broadcast_bitcast_fusion.1
  105.9 0.0 copy-done
  105.9 0.1 broadcast_bitcast_fusion
  106.0 104.4 %all-gather.5.cloned.1.call-done = f32[768,1024]{1,0:T(8,128)} async-done(((f32[32,1024]{1,0:T(8,128)}), f32[768,1024]{1,0:T(8,128)}) %all-gather.5.cloned.1.call-update) | async-done | bytes 3145744 | tf_op jit(solution)/shard_map/all_gather | solution.py:28
  210.4 0.0 copy-done.1
  210.4 8.0 %fusion = f32[512,1024]{1,0:T(8,128)} fusion(f32[768,1024]{1,0:T(8,128)} %all-gather.5.cloned.1.call-done, f32[512,768]{1,0:T(8,128)S(1)} %copy-done.1, s32[768]{0:T(1024)S(1)} %broadcast_bitcast_fusion, s32[512]{0:T(512)S(1)} %broadcast_bitcast_fusion.1), kind=kOutput, calls=%fused_computation | convolution fusion | flops 4832624640 | bytes 6820864 | tf_op jit(solution)/shard_map/dot_general | solution.py:26
  218.4 0.0 all-reduce.2.cloned.1.call-update
  218.5 353.3 %all-reduce.2.cloned.1.call-done = f32[512,1024]{1,0:T(8,128)} async-done(((f32[512,1024]{1,0:T(8,128)}), f32[512,1024]{1,0:T(8,128)}) %all-reduce.2.cloned.1.call-update) | async-done | bytes 2097168 | tf_op jit(solution)/shard_map/psum | solution.py:33
  571.8 1.5 constant_dynamic-slice_fusion
Async XLA Ops:
  6.5 99.4 %copy-start = (s32[6]{0:T(128)S(1)}, s32[6]{0:T(128)}, u32[]{:S(2)}) copy-start(s32[6]{0:T(128)} %param.8) | copy-start | bytes 76
  6.5 98.5 %copy-start.2 = (f32[32,1024]{1,0:T(8,128)S(1)}, f32[32,1024]{1,0:T(8,128)}, u32[]{:S(2)}) copy-start(f32[32,1024]{1,0:T(8,128)} %param.6) | copy-start | bytes 393220
  6.5 99.3 %copy-start.3 = (s32[4]{0:T(128)S(1)}, s32[4]{0:T(128)}, u32[]{:S(2)}) copy-start(s32[4]{0:T(128)} %param.7) | copy-start | bytes 52
  6.5 203.9 %copy-start.1 = (f32[512,768]{1,0:T(8,128)S(1)}, f32[512,768]{1,0:T(8,128)}, u32[]{:S(2)}) copy-start(f32[512,768]{1,0:T(8,128)} %param.5) | copy-start | bytes 4718596
  6.5 97.0 %all-gather.3.cloned.1.call-start = ((), (), s32[]{:S(2)}) async-start(), calls=%async_computation | async-start | bytes 4325376 | tf_op jit(solution)/shard_map/all_gather | solution.py:15
  7.3 203.1 %all-gather.5.cloned.1.call-start = ((), (), s32[]{:S(2)}) async-start(), calls=%async_computation.1 | async-start | bytes 3276800 | tf_op jit(solution)/shard_map/all_gather | solution.py:28
  105.8 466.0 %all-reduce.2.cloned.1.call-start = ((), (), s32[]{:S(2)}) async-start(), calls=%async_computation.2 | async-start | bytes 4194304 | tf_op jit(solution)/shard_map/psum | solution.py:33
Sparse Core Ops, SparseCore 0:
  11.1 92.3 all-gather.2
  105.9 104.4 all-gather.4
  218.6 353.1 all-reduce.1
where the time goes:
time: 580 us
  waiting for transfers between devices  553 us (95%)
  between operations  13.8 us (2%)
  matrix products  8.03 us (1%)
    psum x1, waiting for transfers between devices, local(): summed = lax.psum(partial_sum, 'narrow')  353 us
    all_gather x1, waiting for transfers between devices, local(): lax.all_gather(symmetric, 'wide', axis=0, tiled=True)  104 us
    all_gather x1, waiting for transfers between devices, local(): piece = lax.all_gather(amplitudes, 'narrow', axis=0, tiled=True)  94.3 us
  transfers between devices with their start and end apart: 3, of which 3 were waited for; matrix products, arithmetic and copies ran while one was open for 0% of the time, Pallas kernels for 0%

commit v1 on v0

v1 whole, which is shorter than its diff:
```python
import jax
import jax.numpy as jnp
from jax import lax
from jax.sharding import PartitionSpec as P

BW = 128
NO = 32
NX, NY, NZH, NZL = 4, 8, 4, 3
WIDE, NARROW = NY * NZL, NX * NZH * 2

X_GROUPS = [[x * 8 + rest for x in range(NX)] for rest in range(8)]
ZH_GROUPS = [[x * 8 + zh * 2 + c for zh in range(NZH)] for x in range(NX) for c in range(2)]
ZL_GROUPS = [[y * NZL + zl for zl in range(NZL)] for y in range(NY)]
CORE_SWAP = [(n, n ^ 1) for n in range(NARROW)]


def y_shift(step):
    return [(y * NZL + zl, (y + step) % NY * NZL + zl) for y in range(NY) for zl in range(NZL)]


def swap_ij(rows):
    count, cols = rows.shape
    return jnp.swapaxes(rows.reshape(count, NO, NO), 1, 2).reshape(count, cols)


def symmetrize(amplitudes, partner):
    pieces = lax.all_to_all(amplitudes, "narrow", 0, 0, tiled=True)
    pick = (partner[:, None] == jnp.arange(NARROW, dtype=jnp.int32)[None, :]).astype(jnp.float32)
    taken = jnp.dot(pick, swap_ij(pieces), precision=lax.Precision.HIGHEST)
    return lax.all_to_all(pieces + taken, "narrow", 0, 0, tiled=True)


def gather_wide(block):
    block = lax.all_gather(block, "wide", axis=0, tiled=True, axis_index_groups=ZL_GROUPS)
    up, down = block, block
    found = {0: block}
    for step in (1, 2, 3):
        up = lax.ppermute(up, "wide", y_shift(1))
        down = lax.ppermute(down, "wide", y_shift(-1))
        found[NY - step], found[step] = up, down
    found[4] = lax.ppermute(up, "wide", y_shift(1))
    return jnp.concatenate([found[d] for d in range(NY)], axis=0)


def local(integrals, amplitudes, row_irrep, col_irrep, partner):
    rows, depth = integrals.shape
    y = lax.axis_index("wide") // NZL
    core = lax.axis_index("narrow") % 2
    matches = jnp.repeat(row_irrep, BW)[:, None] == jnp.repeat(col_irrep, BW)[None, :]
    masked = jnp.where(matches, integrals, jnp.zeros_like(integrals))
    shift = y * (depth // NY)
    masked = lax.dynamic_slice_in_dim(jnp.concatenate([masked, masked], axis=1), shift, depth, 1)
    symmetric = gather_wide(symmetrize(amplitudes, partner))
    partial_sum = jnp.dot(masked, symmetric, precision=lax.Precision.HIGH, preferred_element_type=jnp.float32)
    halves = partial_sum.reshape(NX * NZH, 2, rows // NARROW, -1)
    mine = lax.dynamic_index_in_dim(halves, core, 1, keepdims=False)
    other = lax.dynamic_index_in_dim(halves, 1 - core, 1, keepdims=False)
    chip = mine + lax.ppermute(other, "narrow", CORE_SWAP)
    over_x = lax.all_to_all(chip, "narrow", 0, 0, tiled=True, axis_index_groups=X_GROUPS)
    chip = over_x.reshape((NX, NZH) + chip.shape[1:]).sum(0)
    over_z = lax.all_to_all(chip, "narrow", 0, 0, tiled=True, axis_index_groups=ZH_GROUPS)
    return over_z.sum(0)


def solution(mesh):
    return jax.shard_map(
        local,
        mesh=mesh,
        in_specs=(P("wide", "narrow"), P(("narrow", "wide"), None), P("wide"), P("narrow"), P()),
        out_specs=P(("wide", "narrow"), None),
        check_vma=False,
    )
```

time: 580 us -> 160 us (0.28)
  the two profiles are of different devices: /device:TPU:1 before, /device:TPU:2 now
where the time goes in v1:
time: 160 us
  blocking collectives  99.6 us (62%)
  starting transfers between devices  25.2 us (16%)
  waiting for transfers between devices  24.1 us (15%)
  local copies, waits for them, and re-layouts  4.45 us (3%)
  matrix products  3.54 us (2%)
  other arithmetic  2.58 us (2%)
    all_to_all x1, blocking collectives, symmetrize(): pieces = lax.all_to_all(amplitudes, 'narrow', 0, 0, tiled=True)  29.1 us
    all_to_all x1, blocking collectives, local(): lax.all_to_all(chip, 'narrow', 0, 0, tiled=True, axis_index_groups=ZH_GRO...  21.2 us
    all_to_all x1, blocking collectives, local(): lax.all_to_all(chip, 'narrow', 0, 0, tiled=True, axis_index_groups=X_GROUPS)  18.1 us
    all_to_all x1, blocking collectives, symmetrize(): return lax.all_to_all(pieces + taken, 'narrow', 0, 0, tiled=True)  17.6 us
    ppermute x3, starting transfers between devices, gather_wide(): down = lax.ppermute(down, 'wide', y_shift(-1))  14.1 us
    all_gather x1, blocking collectives, gather_wide(): lax.all_gather(block, 'wide', axis=0, tiled=True, axis_index_groups=ZL_GR...  13.6 us
    ppermute x3, waiting for transfers between devices, gather_wide(): up = lax.ppermute(up, 'wide', y_shift(1))  13.3 us
    ppermute x1, waiting for transfers between devices, gather_wide(): found[4] = lax.ppermute(up, 'wide', y_shift(1))  7.97 us
  transfers between devices with their start and end apart: 8, of which 5 were waited for; matrix products, arithmetic and copies ran while one was open for 1% of the time, Pallas kernels for 0%

profile of v1, /device:TPU:2, one launch (start us, length us, event | category | flops | bytes accessed | tf_op | source)
XLA Modules:
  0.0 159.7 jit_solution(9708100325901693397)
XLA Ops:
  0.0 0.0 copy-start
  0.0 0.0 copy-start.2
  0.0 0.0 copy-start.3
  0.0 0.0 copy-start.1
  0.0 1.1 all_to_all.22
  1.1 29.1 %all_to_all.34 = f32[32,1,1024]{2,1,0:T(1,128)S(1)} all-to-all(f32[32,1,1024]{2,1,0:T(1,128)S(1)} %all_to_all.22), channel_id=1, replica_groups=mesh['wide'=24,'narrow'=32] {'narrow'}, dimensions={0} | all-to-all | bytes 262144 | tf_op jit(solution)/shard_map/all_to_all | solution.py:27
  30.2 0.3 reduce
  30.5 0.2 reshape.20
  30.7 0.2 copy.11
  30.9 0.2 reshape.21
  31.2 0.0 copy-done.2
  31.2 0.3 fusion.3
  31.4 0.1 copy.12
  31.6 17.6 %all_to_all.35 = f32[32,1,1024]{2,1,0:T(1,128)S(1)} all-to-all(f32[32,1,1024]{2,1,0:T(1,128)S(1)} %copy.12), channel_id=1, replica_groups=mesh['wide'=24,'narrow'=32] {'narrow'}, dimensions={0} | all-to-all | bytes 262144 | tf_op jit(solution)/shard_map/all_to_all | solution.py:30
  49.2 13.6 %all-gather = f32[96,1,1024]{2,1,0:T(1,128)S(1)} all-gather(f32[32,1,1024]{2,1,0:T(1,128)S(1)} %all_to_all.35), channel_id=2, replica_groups={{0,32,64},{96,128,160},{192,224,256},{288,320,352},{384,416,448},{480,5..., dimensions={0}, use_global_device_ids=true | all-gather | bytes 524288 | tf_op jit(solution)/shard_map/all_gather | solution.py:34
  62.8 0.1 copy.19
  62.9 3.5 %collective-permute-start.3 = (f32[96,1024]{1,0:T(8,128)S(1)}, f32[96,1024]{1,0:T(8,128)S(1)}, u32[]{:S(2)}, u32[]{:S(2)}) collective-permute-start(f32[96,1024]{1,0:T(8,128)S(1)} %bitcast.26), channel_id=1, source_target_pairs={{0,96},{32,128},{64,160},{96,192},{128,224},{160,256},{192,288},{2... | collective-permute-start | bytes 1179656 | tf_op jit(solution)/shard_map/ppermute | solution.py:38
  66.4 3.8 %collective-permute-start = (f32[96,1024]{1,0:T(8,128)S(1)}, f32[96,1024]{1,0:T(8,128)S(1)}, u32[]{:S(2)}, u32[]{:S(2)}) collective-permute-start(f32[96,1024]{1,0:T(8,128)S(1)} %bitcast.27), channel_id=1, source_target_pairs={{0,672},{32,704},{64,736},{96,0},{128,32},{160,64},{192,96},{224,1... | collective-permute-start | bytes 1179656 | tf_op jit(solution)/shard_map/ppermute | solution.py:39
  70.2 5.3 %collective-permute-done.3 = f32[96,1024]{1,0:T(8,128)S(1)} collective-permute-done((f32[96,1024]{1,0:T(8,128)S(1)}, f32[96,1024]{1,0:T(8,128)S(1)}, u32[]{:S(2)}, u32[]{:S(2)}) %collective-permute-start.3) | collective-permute-done | bytes 393248 | tf_op jit(solution)/shard_map/ppermute | solution.py:38
  75.5 1.9 %collective-permute-start.4 = (f32[96,1024]{1,0:T(8,128)S(1)}, f32[96,1024]{1,0:T(8,128)S(1)}, u32[]{:S(2)}, u32[]{:S(2)}) collective-permute-start(f32[96,1024]{1,0:T(8,128)S(1)} %collective-permute-done.3), channel_id=1, source_target_pairs={{0,96},{32,128},{64,160},{96,192},{128,224},{160,256},{192,288},{2... | collective-permute-start | bytes 1179656 | tf_op jit(solution)/shard_map/ppermute | solution.py:38
  77.4 0.0 copy-done
  77.4 0.1 broadcast_bitcast_fusion
  77.5 0.0 collective-permute-done
  77.5 5.1 %collective-permute-start.1 = (f32[96,1024]{1,0:T(8,128)S(1)}, f32[96,1024]{1,0:T(8,128)}, u32[]{:S(2)}, u32[]{:S(2)}) collective-permute-start(f32[96,1024]{1,0:T(8,128)S(1)} %collective-permute-done), channel_id=1, source_target_pairs={{0,672},{32,704},{64,736},{96,0},{128,32},{160,64},{192,96},{224,1... | collective-permute-start | bytes 1179656 | tf_op jit(solution)/shard_map/ppermute | solution.py:39
  82.7 4.3 %collective-permute-done.4 = f32[96,1024]{1,0:T(8,128)S(1)} collective-permute-done((f32[96,1024]{1,0:T(8,128)S(1)}, f32[96,1024]{1,0:T(8,128)S(1)}, u32[]{:S(2)}, u32[]{:S(2)}) %collective-permute-start.4) | collective-permute-done | bytes 393248 | tf_op jit(solution)/shard_map/ppermute | solution.py:38
  87.0 1.9 %collective-permute-start.5 = (f32[96,1024]{1,0:T(8,128)S(1)}, f32[96,1024]{1,0:T(8,128)}, u32[]{:S(2)}, u32[]{:S(2)}) collective-permute-start(f32[96,1024]{1,0:T(8,128)S(1)} %collective-permute-done.4), channel_id=1, source_target_pairs={{0,96},{32,128},{64,160},{96,192},{128,224},{160,256},{192,288},{2... | collective-permute-start | bytes 1179656 | tf_op jit(solution)/shard_map/ppermute | solution.py:38
  88.9 0.0 copy-done.3
  88.9 0.1 broadcast_bitcast_fusion.1
  89.0 0.0 copy-done.1
  89.0 0.2 compare_select_fusion
  89.2 0.0 collective-permute-done.1
  89.2 5.1 %collective-permute-start.2 = (f32[96,1024]{1,0:T(8,128)}, f32[96,1024]{1,0:T(8,128)S(1)}, u32[]{:S(2)}, u32[]{:S(2)}) collective-permute-start(f32[96,1024]{1,0:T(8,128)} %collective-permute-done.1), channel_id=1, source_target_pairs={{0,672},{32,704},{64,736},{96,0},{128,32},{160,64},{192,96},{224,1... | collective-permute-start | bytes 1179656 | tf_op jit(solution)/shard_map/ppermute | solution.py:39
  94.3 3.6 %collective-permute-done.5 = f32[96,1024]{1,0:T(8,128)} collective-permute-done((f32[96,1024]{1,0:T(8,128)S(1)}, f32[96,1024]{1,0:T(8,128)}, u32[]{:S(2)}, u32[]{:S(2)}) %collective-permute-start.5) | collective-permute-done | bytes 393248 | tf_op jit(solution)/shard_map/ppermute | solution.py:38
  98.0 1.9 %collective-permute-start.6 = (f32[96,1024]{1,0:T(8,128)}, f32[96,1024]{1,0:T(8,128)S(1)}, u32[]{:S(2)}, u32[]{:S(2)}) collective-permute-start(f32[96,1024]{1,0:T(8,128)} %collective-permute-done.5), channel_id=1, source_target_pairs={{0,96},{32,128},{64,160},{96,192},{128,224},{160,256},{192,288},{2... | collective-permute-start | bytes 1179656 | tf_op jit(solution)/shard_map/ppermute | solution.py:41
  99.9 0.1 constant_dynamic-update-slice_fusion.7
  100.0 1.0 constant_dynamic-update-slice_fusion.5
  101.0 0.0 collective-permute-done.2
  101.1 8.0 %collective-permute-done.6 = f32[96,1024]{1,0:T(8,128)S(1)} collective-permute-done((f32[96,1024]{1,0:T(8,128)}, f32[96,1024]{1,0:T(8,128)S(1)}, u32[]{:S(2)}, u32[]{:S(2)}) %collective-permute-start.6) | collective-permute-done | bytes 393248 | tf_op jit(solution)/shard_map/ppermute | solution.py:41
  109.1 1.0 constant_dynamic-update-slice_fusion.2
  110.2 3.3 %fusion.1 = f32[512,1024]{1,0:T(8,128)S(1)} fusion(f32[768,1024]{1,0:T(8,128)S(1)} %constant_dynamic-update-slice_fusion, s32[]{:T(128)S(6)} %select_n.27, f32[512,768]{1,0:T(8,128)S(1)} %compare_select_fusion), kind=kOutput, calls=%fused_computation.3 | convolution fusion | flops 2416312320 | bytes 6815748 | tf_op jit(solution)/shard_map/dot_general | solution.py:54
  113.5 0.1 dynamic-slice_bitcast_fusion
  113.6 1.9 %collective-permute-start.7 = (f32[16,16,1024]{2,1,0:T(8,128)S(1)}, f32[16,16,1024]{2,1,0:T(8,128)}, u32[]{:S(2)}, u32[]{:S(2)}) collective-permute-start(f32[16,16,1024]{2,1,0:T(8,128)S(1)} %dynamic-slice_bitcast_fusion), channel_id=1, source_target_pairs={{0,1},{1,0},{2,3},{3,2},{4,5},{5,4},{6,7},{7,6},{8,9},{9,8},{10,11... | collective-permute-start | bytes 3145736 | tf_op jit(solution)/shard_map/ppermute | solution.py:58
  115.5 2.8 %collective-permute-done.7 = f32[16,16,1024]{2,1,0:T(8,128)} collective-permute-done((f32[16,16,1024]{2,1,0:T(8,128)S(1)}, f32[16,16,1024]{2,1,0:T(8,128)}, u32[]{:S(2)}, u32[]{:S(2)}) %collective-permute-start.7) | collective-permute-done | bytes 1048608 | tf_op jit(solution)/shard_map/ppermute | solution.py:58
  118.3 1.4 bitcast_add_fusion
  119.7 18.1 %all_to_all.36 = f32[16,16,1024]{2,1,0:T(8,128)S(1)} all-to-all(f32[16,16,1024]{2,1,0:T(8,128)S(1)} %bitcast_add_fusion), channel_id=1, replica_groups={{0,8,16,24},{1,9,17,25},{2,10,18,26},{3,11,19,27},{4,12,20,28},{5,13,21..., dimensions={0} | all-to-all | bytes 2097152 | tf_op jit(solution)/shard_map/all_to_all | solution.py:59
  137.8 0.1 reduce_sum.18
  137.9 21.2 %all_to_all.37 = f32[4,16,1024]{2,1,0:T(8,128)S(1)} all-to-all(f32[4,16,1024]{2,1,0:T(8,128)S(1)} %reduce_sum.18), channel_id=1, replica_groups={{0,2,4,6},{1,3,5,7},{8,10,12,14},{9,11,13,15},{16,18,20,22},{17,19,21,2..., dimensions={0} | all-to-all | bytes 524288 | tf_op jit(solution)/shard_map/all_to_all | solution.py:61
  159.0 0.6 reduce_sum.19
  (5 shorter events, 0.1 us)
Async XLA Ops:
  0.0 77.4 %copy-start = (s32[6]{0:T(128)S(1)}, s32[6]{0:T(128)}, u32[]{:S(2)}) copy-start(s32[6]{0:T(128)} %param.8) | copy-start | bytes 76
  0.0 31.2 %copy-start.2 = (s32[32]{0:T(128)S(1)}, s32[32]{0:T(128)}, u32[]{:S(2)}) copy-start(s32[32]{0:T(128)} %param.9) | copy-start | bytes 388
  0.0 88.9 %copy-start.3 = (s32[4]{0:T(128)S(1)}, s32[4]{0:T(128)}, u32[]{:S(2)}) copy-start(s32[4]{0:T(128)} %param.7) | copy-start | bytes 52
  0.0 89.0 %copy-start.1 = (f32[512,768]{1,0:T(8,128)S(1)}, f32[512,768]{1,0:T(8,128)}, u32[]{:S(2)}) copy-start(f32[512,768]{1,0:T(8,128)} %param.5) | copy-start | bytes 4718596
  62.9 12.6 %collective-permute-start.3 = (f32[96,1024]{1,0:T(8,128)S(1)}, f32[96,1024]{1,0:T(8,128)S(1)}, u32[]{:S(2)}, u32[]{:S(2)}) collective-permute-start(f32[96,1024]{1,0:T(8,128)S(1)} %bitcast.26), channel_id=1, source_target_pairs={{0,96},{32,128},{64,160},{96,192},{128,224},{160,256},{192,288},{2... | collective-permute-start | bytes 1179656 | tf_op jit(solution)/shard_map/ppermute | solution.py:38
  66.4 11.2 %collective-permute-start = (f32[96,1024]{1,0:T(8,128)S(1)}, f32[96,1024]{1,0:T(8,128)S(1)}, u32[]{:S(2)}, u32[]{:S(2)}) collective-permute-start(f32[96,1024]{1,0:T(8,128)S(1)} %bitcast.27), channel_id=1, source_target_pairs={{0,672},{32,704},{64,736},{96,0},{128,32},{160,64},{192,96},{224,1... | collective-permute-start | bytes 1179656 | tf_op jit(solution)/shard_map/ppermute | solution.py:39
  75.5 11.5 %collective-permute-start.4 = (f32[96,1024]{1,0:T(8,128)S(1)}, f32[96,1024]{1,0:T(8,128)S(1)}, u32[]{:S(2)}, u32[]{:S(2)}) collective-permute-start(f32[96,1024]{1,0:T(8,128)S(1)} %collective-permute-done.3), channel_id=1, source_target_pairs={{0,96},{32,128},{64,160},{96,192},{128,224},{160,256},{192,288},{2... | collective-permute-start | bytes 1179656 | tf_op jit(solution)/shard_map/ppermute | solution.py:38
  77.5 11.7 %collective-permute-start.1 = (f32[96,1024]{1,0:T(8,128)S(1)}, f32[96,1024]{1,0:T(8,128)}, u32[]{:S(2)}, u32[]{:S(2)}) collective-permute-start(f32[96,1024]{1,0:T(8,128)S(1)} %collective-permute-done), channel_id=1, source_target_pairs={{0,672},{32,704},{64,736},{96,0},{128,32},{160,64},{192,96},{224,1... | collective-permute-start | bytes 1179656 | tf_op jit(solution)/shard_map/ppermute | solution.py:39
  87.0 11.0 %collective-permute-start.5 = (f32[96,1024]{1,0:T(8,128)S(1)}, f32[96,1024]{1,0:T(8,128)}, u32[]{:S(2)}, u32[]{:S(2)}) collective-permute-start(f32[96,1024]{1,0:T(8,128)S(1)} %collective-permute-done.4), channel_id=1, source_target_pairs={{0,96},{32,128},{64,160},{96,192},{128,224},{160,256},{192,288},{2... | collective-permute-start | bytes 1179656 | tf_op jit(solution)/shard_map/ppermute | solution.py:38
  89.2 11.8 %collective-permute-start.2 = (f32[96,1024]{1,0:T(8,128)}, f32[96,1024]{1,0:T(8,128)S(1)}, u32[]{:S(2)}, u32[]{:S(2)}) collective-permute-start(f32[96,1024]{1,0:T(8,128)} %collective-permute-done.1), channel_id=1, source_target_pairs={{0,672},{32,704},{64,736},{96,0},{128,32},{160,64},{192,96},{224,1... | collective-permute-start | bytes 1179656 | tf_op jit(solution)/shard_map/ppermute | solution.py:39
  98.0 11.1 %collective-permute-start.6 = (f32[96,1024]{1,0:T(8,128)}, f32[96,1024]{1,0:T(8,128)S(1)}, u32[]{:S(2)}, u32[]{:S(2)}) collective-permute-start(f32[96,1024]{1,0:T(8,128)} %collective-permute-done.5), channel_id=1, source_target_pairs={{0,96},{32,128},{64,160},{96,192},{128,224},{160,256},{192,288},{2... | collective-permute-start | bytes 1179656 | tf_op jit(solution)/shard_map/ppermute | solution.py:41
  113.6 4.7 %collective-permute-start.7 = (f32[16,16,1024]{2,1,0:T(8,128)S(1)}, f32[16,16,1024]{2,1,0:T(8,128)}, u32[]{:S(2)}, u32[]{:S(2)}) collective-permute-start(f32[16,16,1024]{2,1,0:T(8,128)S(1)} %dynamic-slice_bitcast_fusion), channel_id=1, source_target_pairs={{0,1},{1,0},{2,3},{3,2},{4,5},{5,4},{6,7},{7,6},{8,9},{9,8},{10,11... | collective-permute-start | bytes 3145736 | tf_op jit(solution)/shard_map/ppermute | solution.py:58

commit v2 on v1

v2 whole, which is shorter than its diff:
```python
import jax
import jax.numpy as jnp
from jax import lax
from jax.experimental import pallas as pl
from jax.experimental.pallas import tpu as pltpu
from jax.sharding import PartitionSpec as P

BW = 128
NO = 32
NX, NY, NZH, NZL, NC = 4, 8, 4, 3, 2
WIDE, NARROW = NY * NZL, NX * NZH * NC
LR = 32
SLAB = 512
DEPTH = 768
QC = 256
OUT = 16

X_GROUPS = [[x * 8 + rest for x in range(NX)] for rest in range(8)]
ZH_GROUPS = [[x * 8 + zh * 2 + c for zh in range(NZH)] for x in range(NX) for c in range(NC)]
ZL_GROUPS = [[y * NZL + zl for zl in range(NZL)] for y in range(NY)]
CORE_SWAP = [(n, n ^ 1) for n in range(NARROW)]
VMEM = pl.BlockSpec(memory_space=pltpu.VMEM)
SMEM = pl.BlockSpec(memory_space=pltpu.SMEM)


def y_shift(step):
    return [(y * NZL + zl, (y + step) % NY * NZL + zl) for y in range(NY) for zl in range(NZL)]


def swap_ij(rows):
    count, cols = rows.shape
    return jnp.swapaxes(rows.reshape(count, NO, NO), 1, 2).reshape(count, cols)


def select_kernel(partner, place, pieces, own, other, out):
    rest = place[0] % 8
    core = rest % 2
    for x in range(NX):
        p = partner[x * 8 + rest]
        at = (p // 2) % NZH * NX + p // 8

        @pl.when(p % 2 == core)
        def _():
            out[x] = pieces[x, 0] + own[at]

        @pl.when(p % 2 != core)
        def _():
            out[x] = pieces[x, 0] + other[at]


def split_kernel(place, block, high, low):
    core = place[0] % 2
    for away in range(2):
        for zh in range(NZH):
            for x in range(NX):
                start = pl.multiple_of(x * BW + zh * LR + lax.bitwise_xor(core, away) * OUT, OUT)
                values = block[0, pl.ds(start, OUT), :]
                top = values.astype(jnp.bfloat16)
                to = away * (SLAB // 2) + zh * NX * OUT + x * OUT
                high[to : to + OUT, :] = top
                low[to : to + OUT, :] = (values - top.astype(jnp.float32)).astype(jnp.bfloat16)


def multiply_kernel(place, high, low, *refs):
    blocks, (own, other, s_high, s_low) = refs[:NY], refs[NY:]
    y = place[1] // NZL
    for step in range(NY):
        at = lax.rem(y + step, NY) * (NZL * LR)
        for zl in range(NZL):
            for x in range(NX):
                to = pl.ds(pl.multiple_of(x * DEPTH + at + zl * LR, LR), LR)
                values = blocks[step][zl, x]
                top = values.astype(jnp.bfloat16)
                s_high[to, :] = top
                s_low[to, :] = (values - top.astype(jnp.float32)).astype(jnp.bfloat16)
    half = SLAB // 2
    for away, out in ((1, other), (0, own)):
        rows = slice(away * half, (away + 1) * half)
        total = jnp.dot(low[rows, :], s_high[...], preferred_element_type=jnp.float32)
        total += jnp.dot(high[rows, :], s_low[...], preferred_element_type=jnp.float32)
        total += jnp.dot(high[rows, :], s_high[...], preferred_element_type=jnp.float32)
        out[...] = total


def local(integrals, amplitudes, row_irrep, col_irrep, partner):
    place = jnp.stack([lax.axis_index("narrow"), lax.axis_index("wide")]).astype(jnp.int32)

    both = jnp.stack([amplitudes, swap_ij(amplitudes)]).reshape(2, LR, NX, QC)
    pieces = lax.all_to_all(both.transpose(2, 0, 1, 3), "narrow", 0, 0, tiled=True, axis_index_groups=X_GROUPS)

    matches = jnp.repeat(row_irrep, BW)[:, None] == jnp.repeat(col_irrep, BW)[None, :]
    masked = jnp.where(matches, integrals, jnp.zeros_like(integrals))
    masked, pieces = lax.optimization_barrier((masked, pieces))
    all_integrals = lax.all_gather(masked, "narrow", axis=0, tiled=False, axis_index_groups=X_GROUPS)

    own = lax.all_gather(pieces[:, 1], "narrow", axis=0, tiled=True, axis_index_groups=ZH_GROUPS)
    other = lax.ppermute(own, "narrow", CORE_SWAP)
    symmetric = pl.pallas_call(
        select_kernel,
        out_shape=jax.ShapeDtypeStruct((NX, LR, QC), jnp.float32),
        in_specs=[SMEM, SMEM, VMEM, VMEM, VMEM],
        out_specs=VMEM,
    )(partner, place, pieces, own, other)

    block = lax.all_gather(symmetric, "wide", axis=0, tiled=False, axis_index_groups=ZL_GROUPS)
    up, down = block, block
    found = {0: block}
    for step in (1, 2, 3):
        up = lax.ppermute(up, "wide", y_shift(1))
        down = lax.ppermute(down, "wide", y_shift(-1))
        found[NY - step], found[step] = up, down
    found[4] = lax.ppermute(up, "wide", y_shift(1))

    high, low = pl.pallas_call(
        split_kernel,
        grid=(NX,),
        out_shape=[jax.ShapeDtypeStruct((SLAB, NX * DEPTH), jnp.bfloat16)] * 2,
        in_specs=[SMEM, pl.BlockSpec((1, SLAB, DEPTH), lambda i: (i, 0, 0))],
        out_specs=[pl.BlockSpec((SLAB, DEPTH), lambda i: (0, i))] * 2,
        compiler_params=pltpu.CompilerParams(vmem_limit_bytes=24 << 20),
        cost_estimate=pl.CostEstimate(flops=0, bytes_accessed=12 << 20, transcendentals=0),
    )(place, all_integrals)

    scratch = pltpu.VMEM((NX * DEPTH, QC), jnp.bfloat16)
    mine, theirs = pl.pallas_call(
        multiply_kernel,
        out_shape=[jax.ShapeDtypeStruct((SLAB // 2, QC), jnp.float32)] * 2,
        in_specs=[SMEM] + [VMEM] * (2 + NY),
        out_specs=[VMEM] * 2,
        scratch_shapes=[scratch, scratch],
        compiler_params=pltpu.CompilerParams(vmem_limit_bytes=40 << 20),
        cost_estimate=pl.CostEstimate(flops=6 * SLAB * NX * DEPTH * QC, bytes_accessed=10 << 20, transcendentals=0),
    )(place, high, low, *[found[d] for d in range(NY)])

    chip = mine + lax.ppermute(theirs, "narrow", CORE_SWAP)
    over_z = lax.all_to_all(chip, "narrow", 0, 0, tiled=True, axis_index_groups=ZH_GROUPS)
    reduced = over_z.reshape(NZH, NX, OUT, QC).sum(0)
    planes = lax.all_to_all(reduced, "narrow", 0, 0, tiled=True, axis_index_groups=X_GROUPS)
    return planes.transpose(1, 0, 2).reshape(OUT, NX * QC)


def solution(mesh):
    return jax.shard_map(
        local,
        mesh=mesh,
        in_specs=(P("wide", "narrow"), P(("narrow", "wide"), None), P("wide"), P("narrow"), P()),
        out_specs=P(("wide", "narrow"), None),
        check_vma=False,
    )
```

time: 160 us -> 162 us (1.012)
  blocking collectives: 99.6 us -> 66.5 us
  starting transfers between devices: 25.2 us -> 40 us
  between operations: 0.26 us -> 13.6 us
  Pallas kernels: 0 us -> 7.49 us
  matrix products: 3.54 us -> 0 us
  local copies, waits for them, and re-layouts: 4.45 us -> 7.64 us
    all_to_all x3 -> x1, blocking collectives: 64.8 us -> 9.22 us  [local(): lax.all_to_all(reduced, 'narrow', 0, 0, tiled=True, axis_index_groups=X_G...]
    all_gather x1 -> x2, blocking collectives: 13.6 us -> 33.8 us  [the longest x1 20.5 us: local(): lax.all_gather(pieces[:, 1], 'narrow', axis=0, tiled=True, axis_index_gro...]
    all_to_all x0 -> x1, starting transfers between devices: none -> 12.9 us  [local(): lax.all_to_all(both.transpose(2, 0, 1, 3), 'narrow', 0, 0, tiled=True, ax...]
    pallas_call x0 -> x3, Pallas kernels: none -> 7.49 us  [the longest x1 3.61 us: local(): pl.pallas_call(multiply_kernel, out_shape=[jax.ShapeDtypeStruct((SLAB //...]
    all_to_all x0 -> x1, waiting for transfers between devices: none -> 3.76 us  [local(): lax.all_to_all(both.transpose(2, 0, 1, 3), 'narrow', 0, 0, tiled=True, ax...]
    ppermute x8 -> x9, waiting for transfers between devices: 24.1 us -> 20.5 us  [the longest x3 13.5 us: local(): up = lax.ppermute(up, 'wide', y_shift(1))]
    dot_general x2 -> x0, matrix products: 3.54 us -> none  [the longest x1 3.28 us: local(): jnp.dot(masked, symmetric, precision=lax.Precision.HIGH, preferred_elemen...]
    all_to_all x1, blocking collectives: 21.2 us -> 23.5 us  [local(): lax.all_to_all(chip, 'narrow', 0, 0, tiled=True, axis_index_groups=ZH_GRO...]
  transfers between devices with their start and end apart: 8 -> 11, of which waited for: 5 -> 7; matrix products, arithmetic and copies ran while one was open for 1% -> 1% of each run, Pallas kernels for 0% -> 2%
where the time goes in v2:
time: 162 us
  blocking collectives  66.5 us (41%)
  starting transfers between devices  40 us (25%)
  waiting for transfers between devices  24.3 us (15%)
  between operations  13.6 us (8%)
  local copies, waits for them, and re-layouts  7.64 us (5%)
  Pallas kernels  7.49 us (5%)
  other arithmetic  2.07 us (1%)
    all_to_all x1, blocking collectives, local(): lax.all_to_all(chip, 'narrow', 0, 0, tiled=True, axis_index_groups=ZH_GRO...  23.5 us
    all_gather x1, blocking collectives, local(): lax.all_gather(pieces[:, 1], 'narrow', axis=0, tiled=True, axis_index_gro...  20.5 us
    ppermute x3, starting transfers between devices, local(): down = lax.ppermute(down, 'wide', y_shift(-1))  14.1 us
    ppermute x3, waiting for transfers between devices, local(): up = lax.ppermute(up, 'wide', y_shift(1))  13.5 us
    all_gather x1, blocking collectives, local(): lax.all_gather(symmetric, 'wide', axis=0, tiled=False, axis_index_groups=...  13.2 us
    all_to_all x1, starting transfers between devices, local(): lax.all_to_all(both.transpose(2, 0, 1, 3), 'narrow', 0, 0, tiled=True, ax...  12.9 us
    all_to_all x1, blocking collectives, local(): lax.all_to_all(reduced, 'narrow', 0, 0, tiled=True, axis_index_groups=X_G...  9.22 us
    ppermute x3, starting transfers between devices, local(): up = lax.ppermute(up, 'wide', y_shift(1))  7.29 us
  transfers between devices with their start and end apart: 11, of which 7 were waited for; matrix products, arithmetic and copies ran while one was open for 1% of the time, Pallas kernels for 2%

profile of v2, /device:TPU:2, one launch (start us, length us, event | category | flops | bytes accessed | tf_op | source)
XLA Modules:
  0.0 161.6 jit_solution(13812369670534971126)
XLA Ops:
  6.5 0.0 copy-start
  6.5 1.0 stack.20
  7.5 1.1 reshape.18
  8.6 0.0 copy-start.7
  8.6 0.0 copy-start.5
  8.6 0.2 copy.16
  8.8 0.2 stack.21
  9.0 0.1 maximum_bitcast_fusion
  9.1 0.7 copy.17
  9.8 12.9 %all-to-all-start = ((f32[4,2,32,256]{3,2,1,0:T(8,128)}), f32[4,2,32,256]{3,2,1,0:T(8,128)S(1)}, u32[]{:S(2)}, u32[]{:S(2)}) async-start(f32[4,2,32,256]{3,2,1,0:T(8,128)} %copy.17), calls=%async_computation | async-start | bytes 524288 | tf_op jit(solution)/shard_map/all_to_all | solution.py:89
  22.8 0.0 all-gather.5.cloned.1.call-start
  22.8 0.1 broadcast_bitcast_fusion.1
  22.8 0.1 broadcast_bitcast_fusion
  22.9 0.0 copy-done.5
  22.9 1.3 compare_select_fusion
  24.2 3.8 %all-to-all-done.pieces = f32[4,2,32,256]{3,2,1,0:T(8,128)S(1)} async-done(((f32[4,2,32,256]{3,2,1,0:T(8,128)}), f32[4,2,32,256]{3,2,1,0:T(8,128)S(1)}, u32[]{:S(2)}, u32[]{:S(2)}) %all-to-all-start) | async-done | bytes 262176 | tf_op jit(solution)/shard_map/all_to_all | solution.py:89
  28.0 0.0 all-gather.5.cloned.1.call-update
  28.0 20.5 %all-gather.1 = f32[16,1,32,256]{3,2,1,0:T(8,128)S(1)} all-gather(f32[4,1,32,256]{3,2,1,0:T(8,128)S(1)} %slice.3), channel_id=3, replica_groups={{0,2,4,6},{1,3,5,7},{8,10,12,14},{9,11,13,15},{16,18,20,22},{17,19,21,2..., dimensions={0}, use_global_device_ids=true | all-gather | bytes 655360 | tf_op jit(solution)/shard_map/all_gather | solution.py:96
  48.6 1.9 %collective-permute-start = (f32[16,32,256]{2,1,0:T(8,128)S(1)}, f32[16,32,256]{2,1,0:T(8,128)S(1)}, u32[]{:S(2)}, u32[]{:S(2)}) collective-permute-start(f32[16,32,256]{2,1,0:T(8,128)S(1)} %bitcast.21), channel_id=1, source_target_pairs={{0,1},{1,0},{2,3},{3,2},{4,5},{5,4},{6,7},{7,6},{8,9},{9,8},{10,11... | collective-permute-start | bytes 1572872 | tf_op jit(solution)/shard_map/ppermute | solution.py:97
  50.5 0.6 pad_add_fusion.place
  51.1 1.2 collective-permute-done.other
  52.4 0.0 copy-done.3
  52.4 0.9 copy-done.6
  53.2 2.1 %shard_map.56 = f32[4,32,256]{2,1,0:T(8,128)} custom-call(s32[32]{0:T(128)} %partner.1, s32[2]{0:T(128)} %pad_add_fusion.place, f32[4,2,32,256]{3,2,1,0:T(8,128)} %copy-done.4, f32[16,32,256]{2,1,0:T(8,128)} %bitcast.22, f32[16,32,256]{2,1,0:T(8,128)} %copy-done.6), custom_call_target="tpu_custom_call" | custom-call | tf_op jit(solution)/shard_map/pallas_call | solution.py:98
  55.3 13.2 %all-gather.2 = f32[12,32,256]{2,1,0:T(8,128)S(1)} all-gather(f32[4,32,256]{2,1,0:T(8,128)} %shard_map.56), channel_id=4, replica_groups={{0,32,64},{96,128,160},{192,224,256},{288,320,352},{384,416,448},{480,5..., dimensions={0}, use_global_device_ids=true | all-gather | bytes 524288 | tf_op jit(solution)/shard_map/all_gather | solution.py:105
  68.5 3.5 %collective-permute-start.4 = (f32[3,4,32,256]{3,2,1,0:T(8,128)S(1)}, f32[3,4,32,256]{3,2,1,0:T(8,128)S(1)}, u32[]{:S(2)}, u32[]{:S(2)}) collective-permute-start(f32[3,4,32,256]{3,2,1,0:T(8,128)S(1)} %bitcast.18), channel_id=1, source_target_pairs={{0,96},{32,128},{64,160},{96,192},{128,224},{160,256},{192,288},{2... | collective-permute-start | bytes 1179656 | tf_op jit(solution)/shard_map/ppermute | solution.py:109
  72.0 3.8 %collective-permute-start.1 = (f32[3,4,32,256]{3,2,1,0:T(8,128)S(1)}, f32[3,4,32,256]{3,2,1,0:T(8,128)S(1)}, u32[]{:S(2)}, u32[]{:S(2)}) collective-permute-start(f32[3,4,32,256]{3,2,1,0:T(8,128)S(1)} %bitcast.19), channel_id=1, source_target_pairs={{0,672},{32,704},{64,736},{96,0},{128,32},{160,64},{192,96},{224,1... | collective-permute-start | bytes 1179656 | tf_op jit(solution)/shard_map/ppermute | solution.py:110
  75.9 5.3 %collective-permute-done.4.refs_7_ = f32[3,4,32,256]{3,2,1,0:T(8,128)S(1)} collective-permute-done((f32[3,4,32,256]{3,2,1,0:T(8,128)S(1)}, f32[3,4,32,256]{3,2,1,0:T(8,128)S(1)}, u32[]{:S(2)}, u32[]{:S(2)}) %collective-permute-start.4) | collective-permute-done | bytes 393248 | tf_op jit(solution)/shard_map/ppermute | solution.py:109
  81.2 1.9 %collective-permute-start.5 = (f32[3,4,32,256]{3,2,1,0:T(8,128)S(1)}, f32[3,4,32,256]{3,2,1,0:T(8,128)S(1)}, u32[]{:S(2)}, u32[]{:S(2)}) collective-permute-start(f32[3,4,32,256]{3,2,1,0:T(8,128)S(1)} %collective-permute-done.4.refs_7_), channel_id=1, source_target_pairs={{0,96},{32,128},{64,160},{96,192},{128,224},{160,256},{192,288},{2... | collective-permute-start | bytes 1179656 | tf_op jit(solution)/shard_map/ppermute | solution.py:109
  83.1 0.0 collective-permute-done.1.refs_1_
  83.1 5.1 %collective-permute-start.2 = (f32[3,4,32,256]{3,2,1,0:T(8,128)S(1)}, f32[3,4,32,256]{3,2,1,0:T(8,128)S(1)}, u32[]{:S(2)}, u32[]{:S(2)}) collective-permute-start(f32[3,4,32,256]{3,2,1,0:T(8,128)S(1)} %collective-permute-done.1.refs_1_), channel_id=1, source_target_pairs={{0,672},{32,704},{64,736},{96,0},{128,32},{160,64},{192,96},{224,1... | collective-permute-start | bytes 1179656 | tf_op jit(solution)/shard_map/ppermute | solution.py:110
  88.2 4.4 %collective-permute-done.5.refs_6_ = f32[3,4,32,256]{3,2,1,0:T(8,128)S(1)} collective-permute-done((f32[3,4,32,256]{3,2,1,0:T(8,128)S(1)}, f32[3,4,32,256]{3,2,1,0:T(8,128)S(1)}, u32[]{:S(2)}, u32[]{:S(2)}) %collective-permute-start.5) | collective-permute-done | bytes 393248 | tf_op jit(solution)/shard_map/ppermute | solution.py:109
  92.6 1.9 %collective-permute-start.6 = (f32[3,4,32,256]{3,2,1,0:T(8,128)S(1)}, f32[3,4,32,256]{3,2,1,0:T(8,128)S(1)}, u32[]{:S(2)}, u32[]{:S(2)}) collective-permute-start(f32[3,4,32,256]{3,2,1,0:T(8,128)S(1)} %collective-permute-done.5.refs_6_), channel_id=1, source_target_pairs={{0,96},{32,128},{64,160},{96,192},{128,224},{160,256},{192,288},{2... | collective-permute-start | bytes 1179656 | tf_op jit(solution)/shard_map/ppermute | solution.py:109
  94.5 0.0 collective-permute-done.2.refs_2_
  94.5 5.1 %collective-permute-start.3 = (f32[3,4,32,256]{3,2,1,0:T(8,128)S(1)}, f32[3,4,32,256]{3,2,1,0:T(8,128)S(1)}, u32[]{:S(2)}, u32[]{:S(2)}) collective-permute-start(f32[3,4,32,256]{3,2,1,0:T(8,128)S(1)} %collective-permute-done.2.refs_2_), channel_id=1, source_target_pairs={{0,672},{32,704},{64,736},{96,0},{128,32},{160,64},{192,96},{224,1... | collective-permute-start | bytes 1179656 | tf_op jit(solution)/shard_map/ppermute | solution.py:110
  99.7 3.8 %collective-permute-done.6.refs_5_ = f32[3,4,32,256]{3,2,1,0:T(8,128)S(1)} collective-permute-done((f32[3,4,32,256]{3,2,1,0:T(8,128)S(1)}, f32[3,4,32,256]{3,2,1,0:T(8,128)S(1)}, u32[]{:S(2)}, u32[]{:S(2)}) %collective-permute-start.6) | collective-permute-done | bytes 393248 | tf_op jit(solution)/shard_map/ppermute | solution.py:109
  103.5 1.9 %collective-permute-start.7 = (f32[3,4,32,256]{3,2,1,0:T(8,128)S(1)}, f32[3,4,32,256]{3,2,1,0:T(8,128)S(1)}, u32[]{:S(2)}, u32[]{:S(2)}) collective-permute-start(f32[3,4,32,256]{3,2,1,0:T(8,128)S(1)} %collective-permute-done.6.refs_5_), channel_id=1, source_target_pairs={{0,96},{32,128},{64,160},{96,192},{128,224},{160,256},{192,288},{2... | collective-permute-start | bytes 1179656 | tf_op jit(solution)/shard_map/ppermute | solution.py:112
  105.4 0.0 all-gather.5.cloned.1.call-done
  105.4 2.8 %copy-done.1 = f32[2048,768]{1,0:T(8,128)S(1)} copy-done((f32[2048,768]{1,0:T(8,128)S(1)}, f32[2048,768]{1,0:T(8,128)}, u32[]{:S(2)}) %copy-start.1) | copy-done | bytes 6291480
  108.2 1.8 %shard_map.55 = (bf16[512,3072]{1,0:T(8,128)(2,1)S(1)}, bf16[512,3072]{1,0:T(8,128)(2,1)S(1)}) custom-call(s32[2]{0:T(128)S(1)} %copy-done.2, f32[4,512,768]{2,1,0:T(8,128)S(1)} %bitcast.17), custom_call_target="tpu_custom_call" | custom-call | bytes 12582912 | tf_op jit(solution)/shard_map/pallas_call | solution.py:114
  110.0 0.0 collective-permute-done.3.refs_3_
  110.0 4.3 %collective-permute-done.7.refs_4_ = f32[3,4,32,256]{3,2,1,0:T(8,128)S(1)} collective-permute-done((f32[3,4,32,256]{3,2,1,0:T(8,128)S(1)}, f32[3,4,32,256]{3,2,1,0:T(8,128)S(1)}, u32[]{:S(2)}, u32[]{:S(2)}) %collective-permute-start.7) | collective-permute-done | bytes 393248 | tf_op jit(solution)/shard_map/ppermute | solution.py:112
  114.3 3.6 %shard_map.57 = (f32[256,256]{1,0:T(8,128)S(1)}, f32[256,256]{1,0:T(8,128)S(1)}) custom-call(s32[2]{0:T(128)S(1)} %copy-done.2, bf16[512,3072]{1,0:T(8,128)(2,1)S(1)} %get-tuple-element.12.high, bf16[512,3072]{1,0:T(8,128)(2,1)S(1)} %get-tuple-element.13.low, f32[3,4,32,256]{3,2,1,0:T(8,128)S(1)} %bitcast.20, ...), custom_call_target="tpu_custom_call" | custom-call | flops 2415919104 | bytes 10485760 | tf_op jit(solution)/shard_map/pallas_call | solution.py:125
  117.9 1.9 %collective-permute-start.8 = (f32[256,256]{1,0:T(8,128)S(1)}, f32[256,256]{1,0:T(8,128)S(1)}, u32[]{:S(2)}, u32[]{:S(2)}) collective-permute-start(f32[256,256]{1,0:T(8,128)S(1)} %get-tuple-element.16), channel_id=1, source_target_pairs={{0,1},{1,0},{2,3},{3,2},{4,5},{5,4},{6,7},{7,6},{8,9},{9,8},{10,11... | collective-permute-start | bytes 786440 | tf_op jit(solution)/shard_map/ppermute | solution.py:135
  119.9 1.5 collective-permute-done.8
  121.4 23.5 %all_to_all.19 = f32[4,64,256]{2,1,0:T(8,128)S(1)} all-to-all(f32[4,64,256]{2,1,0:T(8,128)S(1)} %bitcast.24), channel_id=1, replica_groups={{0,2,4,6},{1,3,5,7},{8,10,12,14},{9,11,13,15},{16,18,20,22},{17,19,21,2..., dimensions={0} | all-to-all | bytes 524288 | tf_op jit(solution)/shard_map/all_to_all | solution.py:136
  144.9 9.2 %all_to_all.20 = f32[4,16,256]{2,1,0:T(8,128)S(1)} all-to-all(f32[4,16,256]{2,1,0:T(8,128)S(1)} %bitcast.25), channel_id=1, replica_groups={{0,8,16,24},{1,9,17,25},{2,10,18,26},{3,11,19,27},{4,12,20,28},{5,13,21..., dimensions={0} | all-to-all | bytes 131072 | tf_op jit(solution)/shard_map/all_to_all | solution.py:138
  154.1 0.6 copy.19
  (12 shorter events, 0.1 us)
Async XLA Ops:
  6.5 16.3 %copy-start = (s32[6]{0:T(128)S(1)}, s32[6]{0:T(128)}, u32[]{:S(2)}) copy-start(s32[6]{0:T(128)} %param.8) | copy-start | bytes 76
  8.6 14.2 %copy-start.7 = (s32[4]{0:T(128)S(1)}, s32[4]{0:T(128)}, u32[]{:S(2)}) copy-start(s32[4]{0:T(128)} %param.7) | copy-start | bytes 52
  8.6 14.3 %copy-start.5 = (f32[512,768]{1,0:T(8,128)S(1)}, f32[512,768]{1,0:T(8,128)}, u32[]{:S(2)}) copy-start(f32[512,768]{1,0:T(8,128)} %param.5) | copy-start | bytes 4718596
  9.8 18.1 %all-to-all-start = ((f32[4,2,32,256]{3,2,1,0:T(8,128)}), f32[4,2,32,256]{3,2,1,0:T(8,128)S(1)}, u32[]{:S(2)}, u32[]{:S(2)}) async-start(f32[4,2,32,256]{3,2,1,0:T(8,128)} %copy.17), calls=%async_computation | async-start | bytes 524288 | tf_op jit(solution)/shard_map/all_to_all | solution.py:89
  22.8 82.6 %all-gather.5.cloned.1.call-start = ((), (), s32[]{:S(2)}) async-start(), calls=%async_computation.3 | async-start | bytes 7864320 | tf_op jit(solution)/shard_map/all_gather | solution.py:94
  28.0 24.4 %copy-start.4 = (f32[4,2,32,256]{3,2,1,0:T(8,128)}, f32[4,2,32,256]{3,2,1,0:T(8,128)S(1)}, u32[]{:S(2)}) copy-start(f32[4,2,32,256]{3,2,1,0:T(8,128)S(1)} %all-to-all-done.pieces) | copy-start | bytes 786436
  48.6 3.8 %copy-start.3 = (f32[16,1,32,256]{3,2,1,0:T(8,128)}, f32[16,1,32,256]{3,2,1,0:T(8,128)S(1)}, u32[]{:S(2)}) copy-start(f32[16,1,32,256]{3,2,1,0:T(8,128)S(1)} %all-gather.1) | copy-start | bytes 1572868
  48.6 3.8 %collective-permute-start = (f32[16,32,256]{2,1,0:T(8,128)S(1)}, f32[16,32,256]{2,1,0:T(8,128)S(1)}, u32[]{:S(2)}, u32[]{:S(2)}) collective-permute-start(f32[16,32,256]{2,1,0:T(8,128)S(1)} %bitcast.21), channel_id=1, source_target_pairs={{0,1},{1,0},{2,3},{3,2},{4,5},{5,4},{6,7},{7,6},{8,9},{9,8},{10,11... | collective-permute-start | bytes 1572872 | tf_op jit(solution)/shard_map/ppermute | solution.py:97
  51.1 54.3 %copy-start.2 = (s32[2]{0:T(128)S(1)}, s32[2]{0:T(128)}, u32[]{:S(2)}) copy-start(s32[2]{0:T(128)} %pad_add_fusion.place) | copy-start | bytes 28
  52.4 0.9 copy-start.6
  68.5 12.6 %collective-permute-start.4 = (f32[3,4,32,256]{3,2,1,0:T(8,128)S(1)}, f32[3,4,32,256]{3,2,1,0:T(8,128)S(1)}, u32[]{:S(2)}, u32[]{:S(2)}) collective-permute-start(f32[3,4,32,256]{3,2,1,0:T(8,128)S(1)} %bitcast.18), channel_id=1, source_target_pairs={{0,96},{32,128},{64,160},{96,192},{128,224},{160,256},{192,288},{2... | collective-permute-start | bytes 1179656 | tf_op jit(solution)/shard_map/ppermute | solution.py:109
  72.0 11.0 %collective-permute-start.1 = (f32[3,4,32,256]{3,2,1,0:T(8,128)S(1)}, f32[3,4,32,256]{3,2,1,0:T(8,128)S(1)}, u32[]{:S(2)}, u32[]{:S(2)}) collective-permute-start(f32[3,4,32,256]{3,2,1,0:T(8,128)S(1)} %bitcast.19), channel_id=1, source_target_pairs={{0,672},{32,704},{64,736},{96,0},{128,32},{160,64},{192,96},{224,1... | collective-permute-start | bytes 1179656 | tf_op jit(solution)/shard_map/ppermute | solution.py:110
  81.2 11.4 %collective-permute-start.5 = (f32[3,4,32,256]{3,2,1,0:T(8,128)S(1)}, f32[3,4,32,256]{3,2,1,0:T(8,128)S(1)}, u32[]{:S(2)}, u32[]{:S(2)}) collective-permute-start(f32[3,4,32,256]{3,2,1,0:T(8,128)S(1)} %collective-permute-done.4.refs_7_), channel_id=1, source_target_pairs={{0,96},{32,128},{64,160},{96,192},{128,224},{160,256},{192,288},{2... | collective-permute-start | bytes 1179656 | tf_op jit(solution)/shard_map/ppermute | solution.py:109
  83.1 11.4 %collective-permute-start.2 = (f32[3,4,32,256]{3,2,1,0:T(8,128)S(1)}, f32[3,4,32,256]{3,2,1,0:T(8,128)S(1)}, u32[]{:S(2)}, u32[]{:S(2)}) collective-permute-start(f32[3,4,32,256]{3,2,1,0:T(8,128)S(1)} %collective-permute-done.1.refs_1_), channel_id=1, source_target_pairs={{0,672},{32,704},{64,736},{96,0},{128,32},{160,64},{192,96},{224,1... | collective-permute-start | bytes 1179656 | tf_op jit(solution)/shard_map/ppermute | solution.py:110
  92.6 10.9 %collective-permute-start.6 = (f32[3,4,32,256]{3,2,1,0:T(8,128)S(1)}, f32[3,4,32,256]{3,2,1,0:T(8,128)S(1)}, u32[]{:S(2)}, u32[]{:S(2)}) collective-permute-start(f32[3,4,32,256]{3,2,1,0:T(8,128)S(1)} %collective-permute-done.5.refs_6_), channel_id=1, source_target_pairs={{0,96},{32,128},{64,160},{96,192},{128,224},{160,256},{192,288},{2... | collective-permute-start | bytes 1179656 | tf_op jit(solution)/shard_map/ppermute | solution.py:109
  94.5 15.5 %collective-permute-start.3 = (f32[3,4,32,256]{3,2,1,0:T(8,128)S(1)}, f32[3,4,32,256]{3,2,1,0:T(8,128)S(1)}, u32[]{:S(2)}, u32[]{:S(2)}) collective-permute-start(f32[3,4,32,256]{3,2,1,0:T(8,128)S(1)} %collective-permute-done.2.refs_2_), channel_id=1, source_target_pairs={{0,672},{32,704},{64,736},{96,0},{128,32},{160,64},{192,96},{224,1... | collective-permute-start | bytes 1179656 | tf_op jit(solution)/shard_map/ppermute | solution.py:110
  103.5 10.9 %collective-permute-start.7 = (f32[3,4,32,256]{3,2,1,0:T(8,128)S(1)}, f32[3,4,32,256]{3,2,1,0:T(8,128)S(1)}, u32[]{:S(2)}, u32[]{:S(2)}) collective-permute-start(f32[3,4,32,256]{3,2,1,0:T(8,128)S(1)} %collective-permute-done.6.refs_5_), channel_id=1, source_target_pairs={{0,96},{32,128},{64,160},{96,192},{128,224},{160,256},{192,288},{2... | collective-permute-start | bytes 1179656 | tf_op jit(solution)/shard_map/ppermute | solution.py:112
  105.4 2.8 %copy-start.1 = (f32[2048,768]{1,0:T(8,128)S(1)}, f32[2048,768]{1,0:T(8,128)}, u32[]{:S(2)}) copy-start(f32[2048,768]{1,0:T(8,128)} %all-gather.5.cloned.1.call-done) | copy-start | bytes 18874372
  117.9 3.4 %collective-permute-start.8 = (f32[256,256]{1,0:T(8,128)S(1)}, f32[256,256]{1,0:T(8,128)S(1)}, u32[]{:S(2)}, u32[]{:S(2)}) collective-permute-start(f32[256,256]{1,0:T(8,128)S(1)} %get-tuple-element.16), channel_id=1, source_target_pairs={{0,1},{1,0},{2,3},{3,2},{4,5},{5,4},{6,7},{7,6},{8,9},{9,8},{10,11... | collective-permute-start | bytes 786440 | tf_op jit(solution)/shard_map/ppermute | solution.py:135
Sparse Core Ops, SparseCore 0:
  28.1 71.1 all-gather.4

commit v3 on v1

v3 whole, which is shorter than its diff:
```python
import functools

import jax
import jax.numpy as jnp
from jax import lax
from jax.experimental import pallas as pl
from jax.experimental.pallas import tpu as pltpu
from jax.sharding import PartitionSpec as P

BW = 128
NO = 32
NX, NY, NZH, NZL, NC = 4, 8, 4, 3, 2
WIDE, NARROW = NY * NZL, NX * NZH * NC
LR = 32
SLAB = 512
DEPTH = 768
COLS = 1024
OUT = 16
HALF = SLAB // 2

X_GROUPS = [[x * 8 + rest for x in range(NX)] for rest in range(8)]
ZH_GROUPS = [[x * 8 + zh * 2 + c for zh in range(NZH)] for x in range(NX) for c in range(NC)]
XZ_GROUPS = [[n for n in range(NARROW) if n % 2 == c] for c in range(NC)]
CORE_SWAP = [(n, n ^ 1) for n in range(NARROW)]
VMEM = pl.BlockSpec(memory_space=pltpu.VMEM)
SMEM = pl.BlockSpec(memory_space=pltpu.SMEM)


def y_shift(step):
    return [(y * NZL + zl, (y + step) % NY * NZL + zl) for y in range(NY) for zl in range(NZL)]


def zl_shift(step):
    return [(y * NZL + zl, y * NZL + (zl + step) % NZL) for y in range(NY) for zl in range(NZL)]


def swap_ij(rows):
    count, cols = rows.shape
    return jnp.swapaxes(rows.reshape(count, NO, NO), 1, 2).reshape(count, cols)


def symmetrize(amplitudes, partner, core):
    pieces = lax.all_to_all(amplitudes, "narrow", 0, 0, tiled=True, axis_index_groups=XZ_GROUPS)
    swapped = swap_ij(pieces)
    other = lax.ppermute(swapped, "narrow", CORE_SWAP)
    pairs = jnp.arange(LR, dtype=jnp.int32)
    mine = jnp.where(core == 0, partner[0::2], partner[1::2])
    wanted = jnp.repeat(mine, 2)[:, None]
    same_row = (pairs % 2)[:, None] == (pairs % 2)[None, :]
    held = [(wanted == (pairs // 2 * 2 + lax.bitwise_xor(core, away))[None, :]) & same_row for away in range(2)]
    pick = jnp.concatenate(held, axis=1).astype(jnp.float32)
    taken = jnp.dot(pick, jnp.concatenate([swapped, other], axis=0), precision=lax.Precision.HIGHEST)
    return lax.all_to_all(pieces + taken, "narrow", 0, 0, tiled=True, axis_index_groups=XZ_GROUPS)


def gather_wide(block):
    near = lax.ppermute(block, "wide", zl_shift(1))
    far = lax.ppermute(block, "wide", zl_shift(-1))
    up = lax.ppermute(block, "wide", y_shift(1))
    down = lax.ppermute(block, "wide", y_shift(-1))
    near, far, up, down = lax.optimization_barrier((near, far, up, down))
    rest = jnp.concatenate([near, far], axis=0)
    up_rest = lax.ppermute(rest, "wide", y_shift(1))
    down_rest = lax.ppermute(rest, "wide", y_shift(-1))
    up = jnp.concatenate([up, up_rest], axis=0)
    down = jnp.concatenate([down, down_rest], axis=0)
    found = [(0, 0, block), (0, LR, rest), (NY - 1, 0, up), (1, 0, down)]
    for step in (2, 3):
        up = lax.ppermute(up, "wide", y_shift(1))
        down = lax.ppermute(down, "wide", y_shift(-1))
        found += [(NY - step, 0, up), (step, 0, down)]
    cut = LR * NZL // 2
    found.append((4, 0, lax.ppermute(up[:cut], "wide", y_shift(1))))
    found.append((4, cut, lax.ppermute(down[cut:], "wide", y_shift(-1))))
    return found


def split_kernel(place, row_irrep, col_irrep, block, high, low):
    core = place[0] % 2
    for x in range(NX):
        for col in range(DEPTH // BW):
            keep = row_irrep[x] == col_irrep[col]
            lanes = slice(col * BW, (col + 1) * BW)
            for zh in range(NZH):
                for away in range(2):
                    start = pl.multiple_of(x * BW + zh * LR + lax.bitwise_xor(core, away) * OUT, OUT)
                    values = jnp.where(keep, block[pl.ds(start, OUT), lanes], 0.0)
                    top = values.astype(jnp.bfloat16)
                    to = away * HALF + x * NZH * OUT + zh * OUT
                    high[to : to + OUT, lanes] = top
                    low[to : to + OUT, lanes] = (values - top.astype(jnp.float32)).astype(jnp.bfloat16)


def three_pass(high, low, s_high, s_low, rows):
    total = jnp.dot(low[rows, :], s_high[...], preferred_element_type=jnp.float32)
    total += jnp.dot(high[rows, :], s_low[...], preferred_element_type=jnp.float32)
    return total + jnp.dot(high[rows, :], s_high[...], preferred_element_type=jnp.float32)


def first_kernel(where, place, high, low, *refs):
    blocks, (other, s_high, s_low) = refs[: len(where)], refs[len(where) :]
    y, zl = place[1] // NZL, lax.rem(place[1], NZL)
    for (step, first), block in zip(where, blocks):
        at = lax.rem(y + step, NY) * (NZL * LR)
        rows = block.shape[0]
        begin = 0
        while begin < rows:
            slot = (first + begin) // LR
            inside = (first + begin) % LR
            count = min(LR - inside, rows - begin)
            owner = lax.rem(zl + (0, NZL - 1, 1)[slot], NZL)
            to = pl.ds(pl.multiple_of(at + owner * LR + inside, 16), count)
            values = block[begin : begin + count, :]
            top = values.astype(jnp.bfloat16)
            s_high[to, :] = top
            s_low[to, :] = (values - top.astype(jnp.float32)).astype(jnp.bfloat16)
            begin += count
    other[...] = three_pass(high, low, s_high, s_low, slice(HALF, SLAB))


def second_kernel(high, low, s_high, s_low, own):
    own[...] = three_pass(high, low, s_high, s_low, slice(0, HALF))


def local(integrals, amplitudes, row_irrep, col_irrep, partner):
    narrow, wide = lax.axis_index("narrow"), lax.axis_index("wide")
    place = jnp.stack([narrow, wide]).astype(jnp.int32)
    symmetric = symmetrize(amplitudes, partner, narrow % 2)
    found = gather_wide(symmetric)

    high, low = pl.pallas_call(
        split_kernel,
        out_shape=[jax.ShapeDtypeStruct((SLAB, DEPTH), jnp.bfloat16)] * 2,
        in_specs=[SMEM, SMEM, SMEM, VMEM],
        out_specs=[VMEM] * 2,
        compiler_params=pltpu.CompilerParams(vmem_limit_bytes=16 << 20),
        cost_estimate=pl.CostEstimate(flops=0, bytes_accessed=3 << 20, transcendentals=0),
    )(place, row_irrep, col_irrep, integrals)

    where = [(step, first) for step, first, _ in found]
    product = jax.ShapeDtypeStruct((HALF, COLS), jnp.float32)
    flops = 6 * HALF * DEPTH * COLS
    theirs, s_high, s_low = pl.pallas_call(
        functools.partial(first_kernel, where),
        out_shape=[product] + [jax.ShapeDtypeStruct((DEPTH, COLS), jnp.bfloat16)] * 2,
        in_specs=[SMEM] + [VMEM] * (2 + len(where)),
        out_specs=[VMEM] * 3,
        compiler_params=pltpu.CompilerParams(vmem_limit_bytes=32 << 20),
        cost_estimate=pl.CostEstimate(flops=flops, bytes_accessed=6 << 20, transcendentals=0),
    )(place, high, low, *[block for _, _, block in found])
    arrived = lax.ppermute(theirs, "narrow", CORE_SWAP)
    mine = pl.pallas_call(
        second_kernel,
        out_shape=product,
        in_specs=[VMEM] * 4,
        out_specs=VMEM,
        compiler_params=pltpu.CompilerParams(vmem_limit_bytes=32 << 20),
        cost_estimate=pl.CostEstimate(flops=flops, bytes_accessed=6 << 20, transcendentals=0),
    )(high, low, s_high, s_low)
    chip = mine + arrived
    over_x = lax.all_to_all(chip, "narrow", 0, 0, tiled=True, axis_index_groups=X_GROUPS)
    reduced = over_x.reshape(NX, NZH * OUT, COLS).sum(0)
    over_z = lax.all_to_all(reduced, "narrow", 0, 0, tiled=True, axis_index_groups=ZH_GROUPS)
    return over_z.reshape(NZH, OUT, COLS).sum(0)


def solution(mesh):
    return jax.shard_map(
        local,
        mesh=mesh,
        in_specs=(P("wide", "narrow"), P(("narrow", "wide"), None), P("wide"), P("narrow"), P()),
        out_specs=P(("wide", "narrow"), None),
        check_vma=False,
    )
```

time: 160 us -> 167 us (1.044)
  blocking collectives: 99.6 us -> 55.5 us
  starting transfers between devices: 25.2 us -> 64.6 us
  waiting for transfers between devices: 24.1 us -> 33.2 us
  Pallas kernels: 0 us -> 5.08 us
  matrix products: 3.54 us -> 0.26 us
    all_to_all x3 -> x2, blocking collectives: 67.9 us -> 37.2 us  [the longest x1 19.8 us: local(): lax.all_to_all(reduced, 'narrow', 0, 0, tiled=True, axis_index_groups=ZH_...]
    ppermute x2 -> x10, starting transfers between devices: 3.83 us -> 32 us  [the longest x1 5.59 us: gather_wide(): found.append((4, cut, lax.ppermute(down[cut:], 'wide', y_shift(-1))))]
    all_to_all x0 -> x1, starting transfers between devices: none -> 17.5 us  [symmetrize(): lax.all_to_all(amplitudes, 'narrow', 0, 0, tiled=True, axis_index_groups=...]
    all_gather x1 -> x0, blocking collectives: 13.6 us -> none  [gather_wide(): lax.all_gather(block, 'wide', axis=0, tiled=True, axis_index_groups=ZL_GR...]
    ppermute x3 -> x2, waiting for transfers between devices: 13.3 us -> 0.33 us  [gather_wide(): up = lax.ppermute(up, 'wide', y_shift(1))]
    all_to_all x0 -> x1, waiting for transfers between devices: none -> 10 us  [symmetrize(): lax.all_to_all(amplitudes, 'narrow', 0, 0, tiled=True, axis_index_groups=...]
    ppermute x3 -> x2, waiting for transfers between devices: 0.01 us -> 6.55 us  [gather_wide(): down = lax.ppermute(down, 'wide', y_shift(-1))]
    ppermute x2 -> x10, waiting for transfers between devices: 10.7 us -> 16.3 us  [the longest x1 6.21 us: gather_wide(): found.append((4, 0, lax.ppermute(up[:cut], 'wide', y_shift(1))))]
  transfers between devices with their start and end apart: 8 -> 15, of which waited for: 5 -> 10; matrix products, arithmetic and copies ran while one was open for 1% -> 2% of each run, Pallas kernels for 0% -> 1%
where the time goes in v3:
time: 167 us; the launch traced here: 166 us
  starting transfers between devices  64.6 us (39%)
  blocking collectives  55.5 us (33%)
  waiting for transfers between devices  33.2 us (20%)
  local copies, waits for them, and re-layouts  5.69 us (3%)
  Pallas kernels  5.08 us (3%)
    all_to_all x1, blocking collectives, local(): lax.all_to_all(reduced, 'narrow', 0, 0, tiled=True, axis_index_groups=ZH_...  19.8 us
    all_to_all x1, blocking collectives, local(): lax.all_to_all(chip, 'narrow', 0, 0, tiled=True, axis_index_groups=X_GROUPS)  18.3 us
    all_to_all x1, starting transfers between devices, symmetrize(): lax.all_to_all(amplitudes, 'narrow', 0, 0, tiled=True, axis_index_groups=...  17.5 us
    all_to_all x1, blocking collectives, symmetrize(): lax.all_to_all(pieces + taken, 'narrow', 0, 0, tiled=True, axis_index_gro...  17.4 us
    ppermute x2, starting transfers between devices, gather_wide(): down = lax.ppermute(down, 'wide', y_shift(-1))  11.2 us
    all_to_all x1, waiting for transfers between devices, symmetrize(): lax.all_to_all(amplitudes, 'narrow', 0, 0, tiled=True, axis_index_groups=...  10 us
    ppermute x2, waiting for transfers between devices, gather_wide(): down = lax.ppermute(down, 'wide', y_shift(-1))  6.55 us
    ppermute x1, waiting for transfers between devices, gather_wide(): found.append((4, 0, lax.ppermute(up[:cut], 'wide', y_shift(1))))  6.21 us
  transfers between devices with their start and end apart: 15, of which 10 were waited for; matrix products, arithmetic and copies ran while one was open for 2% of the time, Pallas kernels for 1%

profile of v3, /device:TPU:2, one launch (start us, length us, event | category | flops | bytes accessed | tf_op | source)
XLA Modules:
  0.0 165.8 jit_solution(10504705634677298165)
XLA Ops:
  0.0 1.6 all_to_all.27
  1.6 17.5 %all-to-all-start = ((f32[16,2,1024]{2,1,0:T(2,128)}), f32[16,2,1024]{2,1,0:T(2,128)S(1)}, u32[]{:S(2)}, u32[]{:S(2)}) async-start(f32[16,2,1024]{2,1,0:T(2,128)} %all_to_all.27), calls=%async_computation | async-start | bytes 262144 | tf_op jit(solution)/shard_map/all_to_all | solution.py:43
  19.1 0.7 slice.13
  19.9 0.8 slice.12
  20.7 0.1 eq.54
  20.8 10.0 %all-to-all-done = f32[16,2,1024]{2,1,0:T(2,128)S(1)} async-done(((f32[16,2,1024]{2,1,0:T(2,128)}), f32[16,2,1024]{2,1,0:T(2,128)S(1)}, u32[]{:S(2)}, u32[]{:S(2)}) %all-to-all-start) | async-done | bytes 131104 | tf_op jit(solution)/shard_map/all_to_all | solution.py:43
  30.9 0.2 reshape.56
  31.1 0.2 copy.7
  31.3 0.2 reshape.57
  31.6 1.9 %collective-permute-start = (f32[32,1024]{1,0:T(8,128)S(1)}, f32[32,1024]{1,0:T(8,128)S(1)}, u32[]{:S(2)}, u32[]{:S(2)}) collective-permute-start(f32[32,1024]{1,0:T(8,128)S(1)} %reshape.57), channel_id=1, source_target_pairs={{0,1},{1,0},{2,3},{3,2},{4,5},{5,4},{6,7},{7,6},{8,9},{9,8},{10,11... | collective-permute-start | bytes 393224 | tf_op jit(solution)/shard_map/ppermute | solution.py:45
  33.5 0.1 compare_and_fusion.1
  33.6 0.1 all_to_all.29
  33.7 1.1 collective-permute-done
  34.8 0.3 convolution_add_fusion
  35.1 0.1 all_to_all.30
  35.2 17.4 %all_to_all.41 = f32[16,2,1024]{2,1,0:T(2,128)S(1)} all-to-all(f32[16,2,1024]{2,1,0:T(2,128)S(1)} %all_to_all.30), channel_id=1, replica_groups={{0,2,4,6,8,10,12,14,16,18,20,22,24,26,28,30},{1,3,5,7,9,11,13,15,17,19,..., dimensions={0} | all-to-all | bytes 262144 | tf_op jit(solution)/shard_map/all_to_all | solution.py:53
  52.6 0.1 all_to_all.32.refs_0_
  52.7 5.5 %collective-permute-start.4 = (f32[32,1024]{1,0:T(8,128)S(1)}, f32[32,1024]{1,0:T(8,128)S(1)}, u32[]{:S(2)}, u32[]{:S(2)}) collective-permute-start(f32[32,1024]{1,0:T(8,128)S(1)} %all_to_all.32.refs_0_), channel_id=1, source_target_pairs={{0,672},{32,704},{64,736},{96,0},{128,32},{160,64},{192,96},{224,1... | collective-permute-start | bytes 393224 | tf_op jit(solution)/shard_map/ppermute | solution.py:60
  58.2 1.9 %collective-permute-start.3 = (f32[32,1024]{1,0:T(8,128)S(1)}, f32[32,1024]{1,0:T(8,128)S(1)}, u32[]{:S(2)}, u32[]{:S(2)}) collective-permute-start(f32[32,1024]{1,0:T(8,128)S(1)} %all_to_all.32.refs_0_), channel_id=1, source_target_pairs={{0,96},{32,128},{64,160},{96,192},{128,224},{160,256},{192,288},{2... | collective-permute-start | bytes 393224 | tf_op jit(solution)/shard_map/ppermute | solution.py:59
  60.1 4.3 %collective-permute-start.2 = (f32[32,1024]{1,0:T(8,128)S(1)}, f32[32,1024]{1,0:T(8,128)S(1)}, u32[]{:S(2)}, u32[]{:S(2)}) collective-permute-start(f32[32,1024]{1,0:T(8,128)S(1)} %all_to_all.32.refs_0_), channel_id=1, source_target_pairs={{0,64},{32,0},{64,32},{96,160},{128,96},{160,128},{192,256},{224,1... | collective-permute-start | bytes 393224 | tf_op jit(solution)/shard_map/ppermute | solution.py:58
  64.4 1.9 %collective-permute-start.1 = (f32[32,1024]{1,0:T(8,128)S(1)}, f32[32,1024]{1,0:T(8,128)S(1)}, u32[]{:S(2)}, u32[]{:S(2)}) collective-permute-start(f32[32,1024]{1,0:T(8,128)S(1)} %all_to_all.32.refs_0_), channel_id=1, source_target_pairs={{0,32},{32,64},{64,0},{96,128},{128,160},{160,96},{192,224},{224,2... | collective-permute-start | bytes 393224 | tf_op jit(solution)/shard_map/ppermute | solution.py:57
  66.4 1.1 collective-permute-done.2
  67.5 4.7 %collective-permute-done.1 = f32[32,1024]{1,0:T(8,128)S(1)} collective-permute-done((f32[32,1024]{1,0:T(8,128)S(1)}, f32[32,1024]{1,0:T(8,128)S(1)}, u32[]{:S(2)}, u32[]{:S(2)}) %collective-permute-start.1) | collective-permute-done | bytes 131104 | tf_op jit(solution)/shard_map/ppermute | solution.py:57
  72.2 5.1 %collective-permute-start.6 = (f32[64,1024]{1,0:T(8,128)S(1)}, f32[64,1024]{1,0:T(8,128)S(1)}, u32[]{:S(2)}, u32[]{:S(2)}) collective-permute-start(f32[64,1024]{1,0:T(8,128)S(1)} %constant_dynamic-update-slice_fusion.refs_1_), channel_id=1, source_target_pairs={{0,672},{32,704},{64,736},{96,0},{128,32},{160,64},{192,96},{224,1... | collective-permute-start | bytes 786440 | tf_op jit(solution)/shard_map/ppermute | solution.py:64
  77.3 1.9 %collective-permute-start.5 = (f32[64,1024]{1,0:T(8,128)S(1)}, f32[64,1024]{1,0:T(8,128)S(1)}, u32[]{:S(2)}, u32[]{:S(2)}) collective-permute-start(f32[64,1024]{1,0:T(8,128)S(1)} %constant_dynamic-update-slice_fusion.refs_1_), channel_id=1, source_target_pairs={{0,96},{32,128},{64,160},{96,192},{128,224},{160,256},{192,288},{2... | collective-permute-start | bytes 786440 | tf_op jit(solution)/shard_map/ppermute | solution.py:63
  79.3 1.9 %collective-permute-done.6 = f32[64,1024]{1,0:T(8,128)S(1)} collective-permute-done((f32[64,1024]{1,0:T(8,128)S(1)}, f32[64,1024]{1,0:T(8,128)S(1)}, u32[]{:S(2)}, u32[]{:S(2)}) %collective-permute-start.6) | collective-permute-done | bytes 262176 | tf_op jit(solution)/shard_map/ppermute | solution.py:64
  81.2 5.6 %collective-permute-start.8 = (f32[96,1024]{1,0:T(8,128)S(1)}, f32[96,1024]{1,0:T(8,128)S(1)}, u32[]{:S(2)}, u32[]{:S(2)}) collective-permute-start(f32[96,1024]{1,0:T(8,128)S(1)} %constant_dynamic-update-slice_fusion.4.refs_3_), channel_id=1, source_target_pairs={{0,672},{32,704},{64,736},{96,0},{128,32},{160,64},{192,96},{224,1... | collective-permute-start | bytes 1179656 | tf_op jit(solution)/shard_map/ppermute | solution.py:70
  86.9 1.9 %collective-permute-start.7 = (f32[96,1024]{1,0:T(8,128)S(1)}, f32[96,1024]{1,0:T(8,128)S(1)}, u32[]{:S(2)}, u32[]{:S(2)}) collective-permute-start(f32[96,1024]{1,0:T(8,128)S(1)} %constant_dynamic-update-slice_fusion.2.refs_2_), channel_id=1, source_target_pairs={{0,96},{32,128},{64,160},{96,192},{128,224},{160,256},{192,288},{2... | collective-permute-start | bytes 1179656 | tf_op jit(solution)/shard_map/ppermute | solution.py:69
  88.8 3.3 %collective-permute-done.8.refs_5_ = f32[96,1024]{1,0:T(8,128)S(1)} collective-permute-done((f32[96,1024]{1,0:T(8,128)S(1)}, f32[96,1024]{1,0:T(8,128)S(1)}, u32[]{:S(2)}, u32[]{:S(2)}) %collective-permute-start.8) | collective-permute-done | bytes 393248 | tf_op jit(solution)/shard_map/ppermute | solution.py:70
  92.1 5.6 %collective-permute-start.10 = (f32[96,1024]{1,0:T(8,128)S(1)}, f32[96,1024]{1,0:T(8,128)S(1)}, u32[]{:S(2)}, u32[]{:S(2)}) collective-permute-start(f32[96,1024]{1,0:T(8,128)S(1)} %collective-permute-done.8.refs_5_), channel_id=1, source_target_pairs={{0,672},{32,704},{64,736},{96,0},{128,32},{160,64},{192,96},{224,1... | collective-permute-start | bytes 1179656 | tf_op jit(solution)/shard_map/ppermute | solution.py:70
  97.7 0.3 collective-permute-done.7.refs_4_
  98.1 1.9 %collective-permute-start.9 = (f32[96,1024]{1,0:T(8,128)S(1)}, f32[96,1024]{1,0:T(8,128)S(1)}, u32[]{:S(2)}, u32[]{:S(2)}) collective-permute-start(f32[96,1024]{1,0:T(8,128)S(1)} %collective-permute-done.7.refs_4_), channel_id=1, source_target_pairs={{0,96},{32,128},{64,160},{96,192},{128,224},{160,256},{192,288},{2... | collective-permute-start | bytes 1179656 | tf_op jit(solution)/shard_map/ppermute | solution.py:69
  100.0 3.2 %collective-permute-done.10.refs_7_ = f32[96,1024]{1,0:T(8,128)S(1)} collective-permute-done((f32[96,1024]{1,0:T(8,128)S(1)}, f32[96,1024]{1,0:T(8,128)S(1)}, u32[]{:S(2)}, u32[]{:S(2)}) %collective-permute-start.10) | collective-permute-done | bytes 393248 | tf_op jit(solution)/shard_map/ppermute | solution.py:70
  103.2 0.7 slice.17
  103.9 5.6 %collective-permute-start.12 = (f32[48,1024]{1,0:T(8,128)}, f32[48,1024]{1,0:T(8,128)}, u32[]{:S(2)}, u32[]{:S(2)}) collective-permute-start(f32[48,1024]{1,0:T(8,128)} %slice.17), channel_id=1, source_target_pairs={{0,672},{32,704},{64,736},{96,0},{128,32},{160,64},{192,96},{224,1... | collective-permute-start | bytes 589832 | tf_op jit(solution)/shard_map/ppermute | solution.py:74
  109.5 0.7 slice.16
  110.2 1.9 %collective-permute-start.11 = (f32[48,1024]{1,0:T(8,128)}, f32[48,1024]{1,0:T(8,128)}, u32[]{:S(2)}, u32[]{:S(2)}) collective-permute-start(f32[48,1024]{1,0:T(8,128)} %slice.16), channel_id=1, source_target_pairs={{0,96},{32,128},{64,160},{96,192},{128,224},{160,256},{192,288},{2... | collective-permute-start | bytes 589832 | tf_op jit(solution)/shard_map/ppermute | solution.py:73
  112.2 0.1 pad_add_fusion.place
  112.3 0.8 shard_map.55
  113.1 6.2 %collective-permute-done.11.refs_8_ = f32[48,1024]{1,0:T(8,128)} collective-permute-done((f32[48,1024]{1,0:T(8,128)}, f32[48,1024]{1,0:T(8,128)}, u32[]{:S(2)}, u32[]{:S(2)}) %collective-permute-start.11) | collective-permute-done | bytes 196640 | tf_op jit(solution)/shard_map/ppermute | solution.py:73
  119.3 2.9 %shard_map.56 = (f32[256,1024]{1,0:T(8,128)S(1)}, bf16[768,1024]{1,0:T(8,128)(2,1)S(1)}, bf16[768,1024]{1,0:T(8,128)(2,1)S(1)}) custom-call(s32[2]{0:T(128)S(1)} %pad_add_fusion.place, bf16[512,768]{1,0:T(8,128)(2,1)S(1)} %get-tuple-element.14.high, bf16[512,768]{1,0:T(8,128)(2,1)S(1)} %get-tuple-element.15.low, f32[32,1024]{1,0:T(8,128)S(1)} %all_to_all.32.refs_0_, ...), custom_call_target="tpu_custom_call" | custom-call | flops 1207959552 | bytes 6291456 | tf_op jit(solution)/shard_map/pallas_call | solution.py:143
  122.2 1.9 %collective-permute-start.13 = (f32[256,1024]{1,0:T(8,128)S(1)}, f32[256,1024]{1,0:T(8,128)S(1)}, u32[]{:S(2)}, u32[]{:S(2)}) collective-permute-start(f32[256,1024]{1,0:T(8,128)S(1)} %get-tuple-element.22), channel_id=1, source_target_pairs={{0,1},{1,0},{2,3},{3,2},{4,5},{5,4},{6,7},{7,6},{8,9},{9,8},{10,11... | collective-permute-start | bytes 3145736 | tf_op jit(solution)/shard_map/ppermute | solution.py:151
  124.1 1.4 shard_map.57
  125.5 1.2 collective-permute-done.13
  126.8 0.2 add.63
  126.9 18.3 %all_to_all.42 = f32[4,64,1024]{2,1,0:T(8,128)S(1)} all-to-all(f32[4,64,1024]{2,1,0:T(8,128)S(1)} %bitcast.5), channel_id=1, replica_groups={{0,8,16,24},{1,9,17,25},{2,10,18,26},{3,11,19,27},{4,12,20,28},{5,13,21..., dimensions={0} | all-to-all | bytes 2097152 | tf_op jit(solution)/shard_map/all_to_all | solution.py:161
  145.3 19.8 %all_to_all.43 = f32[4,16,1024]{2,1,0:T(8,128)S(1)} all-to-all(f32[4,16,1024]{2,1,0:T(8,128)S(1)} %bitcast.7), channel_id=1, replica_groups={{0,2,4,6},{1,3,5,7},{8,10,12,14},{9,11,13,15},{16,18,20,22},{17,19,21,2..., dimensions={0} | all-to-all | bytes 524288 | tf_op jit(solution)/shard_map/all_to_all | solution.py:163
  165.1 0.6 reduce_sum.19
  (30 shorter events, 0.3 us)
Async XLA Ops:
  1.6 29.3 %all-to-all-start = ((f32[16,2,1024]{2,1,0:T(2,128)}), f32[16,2,1024]{2,1,0:T(2,128)S(1)}, u32[]{:S(2)}, u32[]{:S(2)}) async-start(f32[16,2,1024]{2,1,0:T(2,128)} %all_to_all.27), calls=%async_computation | async-start | bytes 262144 | tf_op jit(solution)/shard_map/all_to_all | solution.py:43
  31.6 3.2 %collective-permute-start = (f32[32,1024]{1,0:T(8,128)S(1)}, f32[32,1024]{1,0:T(8,128)S(1)}, u32[]{:S(2)}, u32[]{:S(2)}) collective-permute-start(f32[32,1024]{1,0:T(8,128)S(1)} %reshape.57), channel_id=1, source_target_pairs={{0,1},{1,0},{2,3},{3,2},{4,5},{5,4},{6,7},{7,6},{8,9},{9,8},{10,11... | collective-permute-start | bytes 393224 | tf_op jit(solution)/shard_map/ppermute | solution.py:45
  52.6 59.7 %copy-start = (f32[512,768]{1,0:T(8,128)S(1)}, f32[512,768]{1,0:T(8,128)}, u32[]{:S(2)}) copy-start(f32[512,768]{1,0:T(8,128)} %block.1) | copy-start | bytes 4718596
  52.6 59.7 %copy-start.5 = (s32[4]{0:T(128)S(1)}, s32[4]{0:T(128)}, u32[]{:S(2)}) copy-start(s32[4]{0:T(128)} %row_irrep.1) | copy-start | bytes 52
  52.6 59.7 %copy-start.6 = (s32[6]{0:T(128)S(1)}, s32[6]{0:T(128)}, u32[]{:S(2)}) copy-start(s32[6]{0:T(128)} %col_irrep.1) | copy-start | bytes 76
  52.7 13.7 %collective-permute-start.4 = (f32[32,1024]{1,0:T(8,128)S(1)}, f32[32,1024]{1,0:T(8,128)S(1)}, u32[]{:S(2)}, u32[]{:S(2)}) collective-permute-start(f32[32,1024]{1,0:T(8,128)S(1)} %all_to_all.32.refs_0_), channel_id=1, source_target_pairs={{0,672},{32,704},{64,736},{96,0},{128,32},{160,64},{192,96},{224,1... | collective-permute-start | bytes 393224 | tf_op jit(solution)/shard_map/ppermute | solution.py:60
  58.2 8.2 %collective-permute-start.3 = (f32[32,1024]{1,0:T(8,128)S(1)}, f32[32,1024]{1,0:T(8,128)S(1)}, u32[]{:S(2)}, u32[]{:S(2)}) collective-permute-start(f32[32,1024]{1,0:T(8,128)S(1)} %all_to_all.32.refs_0_), channel_id=1, source_target_pairs={{0,96},{32,128},{64,160},{96,192},{128,224},{160,256},{192,288},{2... | collective-permute-start | bytes 393224 | tf_op jit(solution)/shard_map/ppermute | solution.py:59
  60.1 7.3 %collective-permute-start.2 = (f32[32,1024]{1,0:T(8,128)S(1)}, f32[32,1024]{1,0:T(8,128)S(1)}, u32[]{:S(2)}, u32[]{:S(2)}) collective-permute-start(f32[32,1024]{1,0:T(8,128)S(1)} %all_to_all.32.refs_0_), channel_id=1, source_target_pairs={{0,64},{32,0},{64,32},{96,160},{128,96},{160,128},{192,256},{224,1... | collective-permute-start | bytes 393224 | tf_op jit(solution)/shard_map/ppermute | solution.py:58
  64.4 7.8 %collective-permute-start.1 = (f32[32,1024]{1,0:T(8,128)S(1)}, f32[32,1024]{1,0:T(8,128)S(1)}, u32[]{:S(2)}, u32[]{:S(2)}) collective-permute-start(f32[32,1024]{1,0:T(8,128)S(1)} %all_to_all.32.refs_0_), channel_id=1, source_target_pairs={{0,32},{32,64},{64,0},{96,128},{128,160},{160,96},{192,224},{224,2... | collective-permute-start | bytes 393224 | tf_op jit(solution)/shard_map/ppermute | solution.py:57
  72.2 9.0 %collective-permute-start.6 = (f32[64,1024]{1,0:T(8,128)S(1)}, f32[64,1024]{1,0:T(8,128)S(1)}, u32[]{:S(2)}, u32[]{:S(2)}) collective-permute-start(f32[64,1024]{1,0:T(8,128)S(1)} %constant_dynamic-update-slice_fusion.refs_1_), channel_id=1, source_target_pairs={{0,672},{32,704},{64,736},{96,0},{128,32},{160,64},{192,96},{224,1... | collective-permute-start | bytes 786440 | tf_op jit(solution)/shard_map/ppermute | solution.py:64
  77.3 9.5 %collective-permute-start.5 = (f32[64,1024]{1,0:T(8,128)S(1)}, f32[64,1024]{1,0:T(8,128)S(1)}, u32[]{:S(2)}, u32[]{:S(2)}) collective-permute-start(f32[64,1024]{1,0:T(8,128)S(1)} %constant_dynamic-update-slice_fusion.refs_1_), channel_id=1, source_target_pairs={{0,96},{32,128},{64,160},{96,192},{128,224},{160,256},{192,288},{2... | collective-permute-start | bytes 786440 | tf_op jit(solution)/shard_map/ppermute | solution.py:63
  81.2 10.9 %collective-permute-start.8 = (f32[96,1024]{1,0:T(8,128)S(1)}, f32[96,1024]{1,0:T(8,128)S(1)}, u32[]{:S(2)}, u32[]{:S(2)}) collective-permute-start(f32[96,1024]{1,0:T(8,128)S(1)} %constant_dynamic-update-slice_fusion.4.refs_3_), channel_id=1, source_target_pairs={{0,672},{32,704},{64,736},{96,0},{128,32},{160,64},{192,96},{224,1... | collective-permute-start | bytes 1179656 | tf_op jit(solution)/shard_map/ppermute | solution.py:70
  86.9 11.2 %collective-permute-start.7 = (f32[96,1024]{1,0:T(8,128)S(1)}, f32[96,1024]{1,0:T(8,128)S(1)}, u32[]{:S(2)}, u32[]{:S(2)}) collective-permute-start(f32[96,1024]{1,0:T(8,128)S(1)} %constant_dynamic-update-slice_fusion.2.refs_2_), channel_id=1, source_target_pairs={{0,96},{32,128},{64,160},{96,192},{128,224},{160,256},{192,288},{2... | collective-permute-start | bytes 1179656 | tf_op jit(solution)/shard_map/ppermute | solution.py:69
  92.1 17.4 %copy-start.1 = (f32[96,1024]{1,0:T(8,128)}, f32[96,1024]{1,0:T(8,128)S(1)}, u32[]{:S(2)}) copy-start(f32[96,1024]{1,0:T(8,128)S(1)} %collective-permute-done.8.refs_5_) | copy-start | bytes 1179652
  92.1 11.1 %collective-permute-start.10 = (f32[96,1024]{1,0:T(8,128)S(1)}, f32[96,1024]{1,0:T(8,128)S(1)}, u32[]{:S(2)}, u32[]{:S(2)}) collective-permute-start(f32[96,1024]{1,0:T(8,128)S(1)} %collective-permute-done.8.refs_5_), channel_id=1, source_target_pairs={{0,672},{32,704},{64,736},{96,0},{128,32},{160,64},{192,96},{224,1... | collective-permute-start | bytes 1179656 | tf_op jit(solution)/shard_map/ppermute | solution.py:70
  98.1 12.2 %copy-start.3 = (f32[96,1024]{1,0:T(8,128)}, f32[96,1024]{1,0:T(8,128)S(1)}, u32[]{:S(2)}) copy-start(f32[96,1024]{1,0:T(8,128)S(1)} %collective-permute-done.7.refs_4_) | copy-start | bytes 1179652
  98.1 11.4 %collective-permute-start.9 = (f32[96,1024]{1,0:T(8,128)S(1)}, f32[96,1024]{1,0:T(8,128)S(1)}, u32[]{:S(2)}, u32[]{:S(2)}) collective-permute-start(f32[96,1024]{1,0:T(8,128)S(1)} %collective-permute-done.7.refs_4_), channel_id=1, source_target_pairs={{0,96},{32,128},{64,160},{96,192},{128,224},{160,256},{192,288},{2... | collective-permute-start | bytes 1179656 | tf_op jit(solution)/shard_map/ppermute | solution.py:69
  103.9 9.2 %collective-permute-start.12 = (f32[48,1024]{1,0:T(8,128)}, f32[48,1024]{1,0:T(8,128)}, u32[]{:S(2)}, u32[]{:S(2)}) collective-permute-start(f32[48,1024]{1,0:T(8,128)} %slice.17), channel_id=1, source_target_pairs={{0,672},{32,704},{64,736},{96,0},{128,32},{160,64},{192,96},{224,1... | collective-permute-start | bytes 589832 | tf_op jit(solution)/shard_map/ppermute | solution.py:74
  110.2 9.1 %collective-permute-start.11 = (f32[48,1024]{1,0:T(8,128)}, f32[48,1024]{1,0:T(8,128)}, u32[]{:S(2)}, u32[]{:S(2)}) collective-permute-start(f32[48,1024]{1,0:T(8,128)} %slice.16), channel_id=1, source_target_pairs={{0,96},{32,128},{64,160},{96,192},{128,224},{160,256},{192,288},{2... | collective-permute-start | bytes 589832 | tf_op jit(solution)/shard_map/ppermute | solution.py:73
  112.1 7.2 %copy-start.2 = (f32[96,1024]{1,0:T(8,128)S(1)}, f32[96,1024]{1,0:T(8,128)}, u32[]{:S(2)}) copy-start(f32[96,1024]{1,0:T(8,128)} %copy-done.1) | copy-start | bytes 1179652
  112.2 7.1 %copy-start.4 = (f32[96,1024]{1,0:T(8,128)S(1)}, f32[96,1024]{1,0:T(8,128)}, u32[]{:S(2)}) copy-start(f32[96,1024]{1,0:T(8,128)} %copy-done.3) | copy-start | bytes 1179652
  122.2 4.6 %collective-permute-start.13 = (f32[256,1024]{1,0:T(8,128)S(1)}, f32[256,1024]{1,0:T(8,128)S(1)}, u32[]{:S(2)}, u32[]{:S(2)}) collective-permute-start(f32[256,1024]{1,0:T(8,128)S(1)} %get-tuple-element.22), channel_id=1, source_target_pairs={{0,1},{1,0},{2,3},{3,2},{4,5},{5,4},{6,7},{7,6},{8,9},{9,8},{10,11... | collective-permute-start | bytes 3145736 | tf_op jit(solution)/shard_map/ppermute | solution.py:151

commit v4 on v1

v4 whole, which is shorter than its diff:
```python
import jax
import jax.numpy as jnp
from jax import lax
from jax.experimental import pallas as pl
from jax.experimental.pallas import tpu as pltpu
from jax.sharding import PartitionSpec as P

BW = 128
NO = 32
NX, NY, NZH, NZL, NC = 4, 8, 4, 3, 2
WIDE, NARROW = NY * NZL, NX * NZH * NC
LR = 32
SLAB = 512
DEPTH = 768
COLS = 1024
OUT = 16
HALF = SLAB // 2

X_GROUPS = [[x * 8 + rest for x in range(NX)] for rest in range(8)]
ZH_GROUPS = [[x * 8 + zh * 2 + c for zh in range(NZH)] for x in range(NX) for c in range(NC)]
ZL_GROUPS = [[y * NZL + zl for zl in range(NZL)] for y in range(NY)]
CORE_SWAP = [(n, n ^ 1) for n in range(NARROW)]
VMEM = pl.BlockSpec(memory_space=pltpu.VMEM)
SMEM = pl.BlockSpec(memory_space=pltpu.SMEM)


def y_shift(step):
    return [(y * NZL + zl, (y + step) % NY * NZL + zl) for y in range(NY) for zl in range(NZL)]


def swap_ij(rows):
    count, cols = rows.shape
    return jnp.swapaxes(rows.reshape(count, NO, NO), 1, 2).reshape(count, cols)


def pieces_kernel(row_irrep, col_irrep, block, out, turned):
    for x in range(NX):
        lanes = slice(x * BW, (x + 1) * BW)
        for col in range(DEPTH // BW):
            keep = row_irrep[x] == col_irrep[col]
            values = jnp.where(keep, block[lanes, col * BW : (col + 1) * BW], 0.0)
            turned[col * BW : (col + 1) * BW, :] = values.T
        for r in range(LR):
            out[r, :, lanes] = turned[pl.ds(r, WIDE, stride=LR), :]


def split_kernel(place, pieces, high, low, turned):
    core = place[0] % 2
    for group in range(DEPTH // BW):
        lanes = slice(group * BW, (group + 1) * BW)
        for x in range(NX):
            cols = slice(x * BW, (x + 1) * BW)
            tile = jnp.concatenate([pieces[:, group * 4 + i, cols] for i in range(4)], axis=0)
            turned[cols, :] = tile.T
        for x in range(NX):
            for zh in range(NZH):
                for away in range(2):
                    start = pl.multiple_of(x * BW + zh * LR + lax.bitwise_xor(core, away) * OUT, OUT)
                    values = turned[pl.ds(start, OUT), :]
                    top = values.astype(jnp.bfloat16)
                    to = away * HALF + x * NZH * OUT + zh * OUT
                    high[to : to + OUT, lanes] = top
                    low[to : to + OUT, lanes] = (values - top.astype(jnp.float32)).astype(jnp.bfloat16)


def three_pass(high, low, s_high, s_low, rows):
    total = jnp.dot(low[rows, :], s_high[...], preferred_element_type=jnp.float32)
    total += jnp.dot(high[rows, :], s_low[...], preferred_element_type=jnp.float32)
    return total + jnp.dot(high[rows, :], s_high[...], preferred_element_type=jnp.float32)


def first_kernel(place, high, low, *refs):
    blocks, (other, s_high, s_low) = refs[:NY], refs[NY:]
    y = place[1] // NZL
    count = NZL * LR
    for step, block in enumerate(blocks):
        to = pl.ds(pl.multiple_of(lax.rem(y + step, NY) * count, LR), count)
        values = block[...]
        top = values.astype(jnp.bfloat16)
        s_high[to, :] = top
        s_low[to, :] = (values - top.astype(jnp.float32)).astype(jnp.bfloat16)
    other[...] = three_pass(high, low, s_high, s_low, slice(HALF, SLAB))


def second_kernel(high, low, s_high, s_low, own):
    own[...] = three_pass(high, low, s_high, s_low, slice(0, HALF))


def call(kernel, out_shape, in_specs, args, flops, moved, scratch=()):
    outs = out_shape if isinstance(out_shape, list) else [out_shape]
    found = pl.pallas_call(
        kernel,
        out_shape=outs,
        in_specs=in_specs,
        out_specs=[VMEM] * len(outs),
        scratch_shapes=list(scratch),
        compiler_params=pltpu.CompilerParams(vmem_limit_bytes=32 << 20),
        cost_estimate=pl.CostEstimate(flops=flops, bytes_accessed=moved, transcendentals=0),
    )(*args)
    return found if isinstance(out_shape, list) else found[0]


def gather_y(block):
    up, down = block, block
    found = {0: block}
    for step in (1, 2, 3):
        up = lax.ppermute(up, "wide", y_shift(1))
        down = lax.ppermute(down, "wide", y_shift(-1))
        found[NY - step], found[step] = up, down
    found[4] = lax.ppermute(up, "wide", y_shift(1))
    return [found[d] for d in range(NY)]


def local(integrals, amplitudes, row_irrep, col_irrep, partner):
    place = jnp.stack([lax.axis_index("narrow"), lax.axis_index("wide")]).astype(jnp.int32)

    rows = lax.all_to_all(amplitudes, "narrow", 0, 0, tiled=True)
    pieces = call(
        pieces_kernel,
        jax.ShapeDtypeStruct((LR, WIDE, SLAB), jnp.float32),
        [SMEM, SMEM, VMEM],
        (row_irrep, col_irrep, integrals),
        0,
        3 << 20,
        [pltpu.VMEM((DEPTH, BW), jnp.float32)],
    )
    pick = (partner[:, None] == jnp.arange(NARROW, dtype=jnp.int32)[None, :]).astype(jnp.float32)
    symmetric = rows + jnp.dot(pick, swap_ij(rows), precision=lax.Precision.HIGHEST)
    block = lax.all_gather(symmetric, "wide", axis=0, tiled=True, axis_index_groups=ZL_GROUPS)

    pieces, block = lax.optimization_barrier((pieces, block))
    pieces = lax.all_to_all(pieces, "narrow", 0, 0, tiled=True)
    found = gather_y(block)
    high, low = call(
        split_kernel,
        [jax.ShapeDtypeStruct((SLAB, DEPTH), jnp.bfloat16)] * 2,
        [SMEM, VMEM],
        (place, pieces),
        0,
        3 << 20,
        [pltpu.VMEM((SLAB, BW), jnp.float32)],
    )

    product = jax.ShapeDtypeStruct((HALF, COLS), jnp.float32)
    flops = 6 * HALF * DEPTH * COLS
    theirs, s_high, s_low = call(
        first_kernel,
        [product] + [jax.ShapeDtypeStruct((DEPTH, COLS), jnp.bfloat16)] * 2,
        [SMEM] + [VMEM] * (2 + NY),
        (place, high, low, *found),
        flops,
        6 << 20,
    )
    arrived = lax.ppermute(theirs, "narrow", CORE_SWAP)
    mine = call(second_kernel, product, [VMEM] * 4, (high, low, s_high, s_low), flops, 6 << 20)
    chip = mine + arrived
    over_x = lax.all_to_all(chip, "narrow", 0, 0, tiled=True, axis_index_groups=X_GROUPS)
    reduced = over_x.reshape(NX, NZH * OUT, COLS).sum(0)
    over_z = lax.all_to_all(reduced, "narrow", 0, 0, tiled=True, axis_index_groups=ZH_GROUPS)
    return over_z.reshape(NZH, OUT, COLS).sum(0)


def solution(mesh):
    return jax.shard_map(
        local,
        mesh=mesh,
        in_specs=(P("wide", "narrow"), P(("narrow", "wide"), None), P("wide"), P("narrow"), P()),
        out_specs=P(("wide", "narrow"), None),
        check_vma=False,
    )
```

time: 160 us -> 158 us (0.988)
  the two profiles are of different devices: /device:TPU:2 before, /device:TPU:32 now
where the time goes in v4:
time: 158 us; the launch traced here: 157 us
  blocking collectives  54 us (34%)
  starting transfers between devices  47.3 us (30%)
  waiting for transfers between devices  40.5 us (26%)
  Pallas kernels  9.06 us (6%)
  local copies, waits for them, and re-layouts  4.97 us (3%)
    all_to_all x1, blocking collectives, local(): lax.all_to_all(reduced, 'narrow', 0, 0, tiled=True, axis_index_groups=ZH_...  22.1 us
    ppermute x3, waiting for transfers between devices, gather_y(): up = lax.ppermute(up, 'wide', y_shift(1))  19.5 us
    all_to_all x1, blocking collectives, local(): lax.all_to_all(chip, 'narrow', 0, 0, tiled=True, axis_index_groups=X_GROUPS)  18.7 us
    all_to_all x1, starting transfers between devices, local(): rows = lax.all_to_all(amplitudes, 'narrow', 0, 0, tiled=True)  17.4 us
    ppermute x3, starting transfers between devices, gather_y(): down = lax.ppermute(down, 'wide', y_shift(-1))  14.8 us
    all_gather x1, blocking collectives, local(): lax.all_gather(symmetric, 'wide', axis=0, tiled=True, axis_index_groups=Z...  13.2 us
    all_to_all x1, waiting for transfers between devices, local(): pieces = lax.all_to_all(pieces, 'narrow', 0, 0, tiled=True)  12.5 us
    pallas_call x4, Pallas kernels, call(): pl.pallas_call(kernel, out_shape=outs, in_specs=in_specs, out_specs=[VMEM...  9.06 us
  transfers between devices with their start and end apart: 10, of which 6 were waited for; matrix products, arithmetic and copies ran while one was open for 0% of the time, Pallas kernels for 4%

profile of v4, /device:TPU:32, one launch (start us, length us, event | category | flops | bytes accessed | tf_op | source)
XLA Modules:
  0.0 157.5 jit_solution(10594471459579146936)
XLA Ops:
  0.0 1.6 %all_to_all.23 = f32[32,1,1024]{2,1,0:T(1,128)} reshape(f32[32,1024]{1,0:T(8,128)} %param.6) | data formatting | bytes 262144 | tf_op jit(solution)/shard_map/all_to_all | solution.py:117
  1.7 17.4 %all-to-all-start = ((f32[32,1,1024]{2,1,0:T(1,128)}), f32[32,1,1024]{2,1,0:T(1,128)S(1)}, u32[]{:S(2)}, u32[]{:S(2)}) async-start(f32[32,1,1024]{2,1,0:T(1,128)} %all_to_all.23), calls=%async_computation | async-start | bytes 262144 | tf_op jit(solution)/shard_map/all_to_all | solution.py:117
  19.0 0.0 copy-start
  19.0 1.4 copy-done
  20.4 0.0 copy-start.1
  20.4 0.7 copy-done.1
  21.1 0.0 copy-start.2
  21.1 0.7 copy-done.2
  21.7 2.9 %shard_map.55 = f32[32,24,512]{2,1,0:T(8,128)} custom-call(s32[4]{0:T(128)S(1)} %copy-done.1, s32[6]{0:T(128)S(1)} %copy-done.2, f32[512,768]{1,0:T(8,128)S(1)} %copy-done), custom_call_target="tpu_custom_call" | custom-call | bytes 3145728 | tf_op jit(solution)/shard_map/pallas_call | solution.py:91
  24.6 0.0 copy-start.3
  24.6 7.2 %all-to-all-done = f32[32,1,1024]{2,1,0:T(1,128)S(1)} async-done(((f32[32,1,1024]{2,1,0:T(1,128)}), f32[32,1,1024]{2,1,0:T(1,128)S(1)}, u32[]{:S(2)}, u32[]{:S(2)}) %all-to-all-start) | async-done | bytes 131104 | tf_op jit(solution)/shard_map/all_to_all | solution.py:117
  31.8 0.3 reduce.2
  32.1 0.2 reshape.18
  32.3 0.2 copy.8
  32.5 0.2 reshape.19
  32.7 0.0 copy-done.3
  32.7 0.3 convolution_add_fusion
  33.0 13.2 %all_gather.3.refs_0_ = f32[96,1024]{1,0:T(8,128)S(1)} all-gather(f32[32,1024]{1,0:T(8,128)S(1)} %convolution_add_fusion), channel_id=1, replica_groups={{0,32,64},{96,128,160},{192,224,256},{288,320,352},{384,416,448},{480,5..., dimensions={0}, use_global_device_ids=true | all-gather | bytes 524288 | tf_op jit(solution)/shard_map/all_gather | solution.py:129
  46.2 4.9 %all-to-all-start.1 = ((f32[32,24,512]{2,1,0:T(8,128)}), f32[32,24,512]{2,1,0:T(8,128)S(1)}, u32[]{:S(2)}, u32[]{:S(2)}) async-start(f32[32,24,512]{2,1,0:T(8,128)} %shard_map.55), calls=%async_computation.1 | async-start | bytes 3145728 | tf_op jit(solution)/shard_map/all_to_all | solution.py:132
  51.1 2.6 %collective-permute-start.3 = (f32[96,1024]{1,0:T(8,128)S(1)}, f32[96,1024]{1,0:T(8,128)S(1)}, u32[]{:S(2)}, u32[]{:S(2)}) collective-permute-start(f32[96,1024]{1,0:T(8,128)S(1)} %all_gather.3.refs_0_), channel_id=1, source_target_pairs={{0,96},{32,128},{64,160},{96,192},{128,224},{160,256},{192,288},{2... | collective-permute-start | bytes 1179656 | tf_op jit(solution)/shard_map/ppermute | solution.py:107
  53.7 4.5 %collective-permute-start = (f32[96,1024]{1,0:T(8,128)S(1)}, f32[96,1024]{1,0:T(8,128)S(1)}, u32[]{:S(2)}, u32[]{:S(2)}) collective-permute-start(f32[96,1024]{1,0:T(8,128)S(1)} %all_gather.3.refs_0_), channel_id=1, source_target_pairs={{0,672},{32,704},{64,736},{96,0},{128,32},{160,64},{192,96},{224,1... | collective-permute-start | bytes 1179656 | tf_op jit(solution)/shard_map/ppermute | solution.py:108
  58.2 7.3 %collective-permute-done.3.refs_7_ = f32[96,1024]{1,0:T(8,128)S(1)} collective-permute-done((f32[96,1024]{1,0:T(8,128)S(1)}, f32[96,1024]{1,0:T(8,128)S(1)}, u32[]{:S(2)}, u32[]{:S(2)}) %collective-permute-start.3) | collective-permute-done | bytes 393248 | tf_op jit(solution)/shard_map/ppermute | solution.py:107
  65.5 1.9 %collective-permute-start.4 = (f32[96,1024]{1,0:T(8,128)S(1)}, f32[96,1024]{1,0:T(8,128)S(1)}, u32[]{:S(2)}, u32[]{:S(2)}) collective-permute-start(f32[96,1024]{1,0:T(8,128)S(1)} %collective-permute-done.3.refs_7_), channel_id=1, source_target_pairs={{0,96},{32,128},{64,160},{96,192},{128,224},{160,256},{192,288},{2... | collective-permute-start | bytes 1179656 | tf_op jit(solution)/shard_map/ppermute | solution.py:107
  67.4 0.0 collective-permute-done.refs_1_
  67.5 5.1 %collective-permute-start.1 = (f32[96,1024]{1,0:T(8,128)S(1)}, f32[96,1024]{1,0:T(8,128)S(1)}, u32[]{:S(2)}, u32[]{:S(2)}) collective-permute-start(f32[96,1024]{1,0:T(8,128)S(1)} %collective-permute-done.refs_1_), channel_id=1, source_target_pairs={{0,672},{32,704},{64,736},{96,0},{128,32},{160,64},{192,96},{224,1... | collective-permute-start | bytes 1179656 | tf_op jit(solution)/shard_map/ppermute | solution.py:108
  72.6 6.5 %collective-permute-done.4.refs_6_ = f32[96,1024]{1,0:T(8,128)S(1)} collective-permute-done((f32[96,1024]{1,0:T(8,128)S(1)}, f32[96,1024]{1,0:T(8,128)S(1)}, u32[]{:S(2)}, u32[]{:S(2)}) %collective-permute-start.4) | collective-permute-done | bytes 393248 | tf_op jit(solution)/shard_map/ppermute | solution.py:107
  79.1 1.9 %collective-permute-start.5 = (f32[96,1024]{1,0:T(8,128)S(1)}, f32[96,1024]{1,0:T(8,128)}, u32[]{:S(2)}, u32[]{:S(2)}) collective-permute-start(f32[96,1024]{1,0:T(8,128)S(1)} %collective-permute-done.4.refs_6_), channel_id=1, source_target_pairs={{0,96},{32,128},{64,160},{96,192},{128,224},{160,256},{192,288},{2... | collective-permute-start | bytes 1179656 | tf_op jit(solution)/shard_map/ppermute | solution.py:107
  81.0 0.0 collective-permute-done.1.refs_2_
  81.0 5.1 %collective-permute-start.2 = (f32[96,1024]{1,0:T(8,128)S(1)}, f32[96,1024]{1,0:T(8,128)}, u32[]{:S(2)}, u32[]{:S(2)}) collective-permute-start(f32[96,1024]{1,0:T(8,128)S(1)} %collective-permute-done.1.refs_2_), channel_id=1, source_target_pairs={{0,672},{32,704},{64,736},{96,0},{128,32},{160,64},{192,96},{224,1... | collective-permute-start | bytes 1179656 | tf_op jit(solution)/shard_map/ppermute | solution.py:108
  86.2 5.7 %collective-permute-done.5.refs_5_ = f32[96,1024]{1,0:T(8,128)} collective-permute-done((f32[96,1024]{1,0:T(8,128)S(1)}, f32[96,1024]{1,0:T(8,128)}, u32[]{:S(2)}, u32[]{:S(2)}) %collective-permute-start.5) | collective-permute-done | bytes 393248 | tf_op jit(solution)/shard_map/ppermute | solution.py:107
  91.9 1.9 %collective-permute-start.6 = (f32[96,1024]{1,0:T(8,128)}, f32[96,1024]{1,0:T(8,128)}, u32[]{:S(2)}, u32[]{:S(2)}) collective-permute-start(f32[96,1024]{1,0:T(8,128)} %collective-permute-done.5.refs_5_), channel_id=1, source_target_pairs={{0,96},{32,128},{64,160},{96,192},{128,224},{160,256},{192,288},{2... | collective-permute-start | bytes 1179656 | tf_op jit(solution)/shard_map/ppermute | solution.py:110
  93.8 0.1 pad_add_fusion.place
  93.9 12.5 %all-to-all-done.1.pieces = f32[32,24,512]{2,1,0:T(8,128)S(1)} async-done(((f32[32,24,512]{2,1,0:T(8,128)}), f32[32,24,512]{2,1,0:T(8,128)S(1)}, u32[]{:S(2)}, u32[]{:S(2)}) %all-to-all-start.1) | async-done | bytes 1572896 | tf_op jit(solution)/shard_map/all_to_all | solution.py:132
  106.4 1.5 shard_map.56
  107.9 0.0 collective-permute-done.2.refs_3_
  107.9 0.0 collective-permute-done.6.refs_4_
  107.9 3.3 %shard_map.57 = (f32[256,1024]{1,0:T(8,128)S(1)}, bf16[768,1024]{1,0:T(8,128)(2,1)S(1)}, bf16[768,1024]{1,0:T(8,128)(2,1)S(1)}) custom-call(s32[2]{0:T(128)S(1)} %pad_add_fusion.place, bf16[512,768]{1,0:T(8,128)(2,1)S(1)} %get-tuple-element.13.high, bf16[512,768]{1,0:T(8,128)(2,1)S(1)} %get-tuple-element.14.low, f32[96,1024]{1,0:T(8,128)S(1)} %all_gather.3.refs_0_, ...), custom_call_target="tpu_custom_call" | custom-call | flops 1207959552 | bytes 6291456 | tf_op jit(solution)/shard_map/pallas_call | solution.py:91
  111.2 1.9 %collective-permute-start.7 = (f32[256,1024]{1,0:T(8,128)S(1)}, f32[256,1024]{1,0:T(8,128)S(1)}, u32[]{:S(2)}, u32[]{:S(2)}) collective-permute-start(f32[256,1024]{1,0:T(8,128)S(1)} %get-tuple-element.18), channel_id=1, source_target_pairs={{0,1},{1,0},{2,3},{3,2},{4,5},{5,4},{6,7},{7,6},{8,9},{9,8},{10,11... | collective-permute-start | bytes 3145736 | tf_op jit(solution)/shard_map/ppermute | solution.py:154
  113.1 1.4 shard_map.58
  114.5 1.2 collective-permute-done.7
  115.8 0.1 add.7
  115.9 18.7 %all_to_all.35 = f32[4,64,1024]{2,1,0:T(8,128)S(1)} all-to-all(f32[4,64,1024]{2,1,0:T(8,128)S(1)} %bitcast.8), channel_id=1, replica_groups={{0,8,16,24},{1,9,17,25},{2,10,18,26},{3,11,19,27},{4,12,20,28},{5,13,21..., dimensions={0} | all-to-all | bytes 2097152 | tf_op jit(solution)/shard_map/all_to_all | solution.py:157
  134.6 0.1 reduce_sum.18
  134.7 22.1 %all_to_all.36 = f32[4,16,1024]{2,1,0:T(8,128)S(1)} all-to-all(f32[4,16,1024]{2,1,0:T(8,128)S(1)} %bitcast.10), channel_id=1, replica_groups={{0,2,4,6},{1,3,5,7},{8,10,12,14},{9,11,13,15},{16,18,20,22},{17,19,21,2..., dimensions={0} | all-to-all | bytes 524288 | tf_op jit(solution)/shard_map/all_to_all | solution.py:159
  156.8 0.6 reduce_sum.19
Async XLA Ops:
  1.7 30.2 %all-to-all-start = ((f32[32,1,1024]{2,1,0:T(1,128)}), f32[32,1,1024]{2,1,0:T(1,128)S(1)}, u32[]{:S(2)}, u32[]{:S(2)}) async-start(f32[32,1,1024]{2,1,0:T(1,128)} %all_to_all.23), calls=%async_computation | async-start | bytes 262144 | tf_op jit(solution)/shard_map/all_to_all | solution.py:117
  19.0 1.4 copy-start
  20.4 0.7 copy-start.1
  21.1 0.7 copy-start.2
  24.6 8.1 %copy-start.3 = (s32[32]{0:T(128)S(1)}, s32[32]{0:T(128)}, u32[]{:S(2)}) copy-start(s32[32]{0:T(128)} %param.9) | copy-start | bytes 388
  46.2 60.2 %all-to-all-start.1 = ((f32[32,24,512]{2,1,0:T(8,128)}), f32[32,24,512]{2,1,0:T(8,128)S(1)}, u32[]{:S(2)}, u32[]{:S(2)}) async-start(f32[32,24,512]{2,1,0:T(8,128)} %shard_map.55), calls=%async_computation.1 | async-start | bytes 3145728 | tf_op jit(solution)/shard_map/all_to_all | solution.py:132
  51.1 14.4 %collective-permute-start.3 = (f32[96,1024]{1,0:T(8,128)S(1)}, f32[96,1024]{1,0:T(8,128)S(1)}, u32[]{:S(2)}, u32[]{:S(2)}) collective-permute-start(f32[96,1024]{1,0:T(8,128)S(1)} %all_gather.3.refs_0_), channel_id=1, source_target_pairs={{0,96},{32,128},{64,160},{96,192},{128,224},{160,256},{192,288},{2... | collective-permute-start | bytes 1179656 | tf_op jit(solution)/shard_map/ppermute | solution.py:107
  53.7 13.7 %collective-permute-start = (f32[96,1024]{1,0:T(8,128)S(1)}, f32[96,1024]{1,0:T(8,128)S(1)}, u32[]{:S(2)}, u32[]{:S(2)}) collective-permute-start(f32[96,1024]{1,0:T(8,128)S(1)} %all_gather.3.refs_0_), channel_id=1, source_target_pairs={{0,672},{32,704},{64,736},{96,0},{128,32},{160,64},{192,96},{224,1... | collective-permute-start | bytes 1179656 | tf_op jit(solution)/shard_map/ppermute | solution.py:108
  65.5 13.6 %collective-permute-start.4 = (f32[96,1024]{1,0:T(8,128)S(1)}, f32[96,1024]{1,0:T(8,128)S(1)}, u32[]{:S(2)}, u32[]{:S(2)}) collective-permute-start(f32[96,1024]{1,0:T(8,128)S(1)} %collective-permute-done.3.refs_7_), channel_id=1, source_target_pairs={{0,96},{32,128},{64,160},{96,192},{128,224},{160,256},{192,288},{2... | collective-permute-start | bytes 1179656 | tf_op jit(solution)/shard_map/ppermute | solution.py:107
  67.5 13.6 %collective-permute-start.1 = (f32[96,1024]{1,0:T(8,128)S(1)}, f32[96,1024]{1,0:T(8,128)S(1)}, u32[]{:S(2)}, u32[]{:S(2)}) collective-permute-start(f32[96,1024]{1,0:T(8,128)S(1)} %collective-permute-done.refs_1_), channel_id=1, source_target_pairs={{0,672},{32,704},{64,736},{96,0},{128,32},{160,64},{192,96},{224,1... | collective-permute-start | bytes 1179656 | tf_op jit(solution)/shard_map/ppermute | solution.py:108
  79.1 12.8 %collective-permute-start.5 = (f32[96,1024]{1,0:T(8,128)S(1)}, f32[96,1024]{1,0:T(8,128)}, u32[]{:S(2)}, u32[]{:S(2)}) collective-permute-start(f32[96,1024]{1,0:T(8,128)S(1)} %collective-permute-done.4.refs_6_), channel_id=1, source_target_pairs={{0,96},{32,128},{64,160},{96,192},{128,224},{160,256},{192,288},{2... | collective-permute-start | bytes 1179656 | tf_op jit(solution)/shard_map/ppermute | solution.py:107
  81.0 26.8 %collective-permute-start.2 = (f32[96,1024]{1,0:T(8,128)S(1)}, f32[96,1024]{1,0:T(8,128)}, u32[]{:S(2)}, u32[]{:S(2)}) collective-permute-start(f32[96,1024]{1,0:T(8,128)S(1)} %collective-permute-done.1.refs_2_), channel_id=1, source_target_pairs={{0,672},{32,704},{64,736},{96,0},{128,32},{160,64},{192,96},{224,1... | collective-permute-start | bytes 1179656 | tf_op jit(solution)/shard_map/ppermute | solution.py:108
  91.9 16.0 %collective-permute-start.6 = (f32[96,1024]{1,0:T(8,128)}, f32[96,1024]{1,0:T(8,128)}, u32[]{:S(2)}, u32[]{:S(2)}) collective-permute-start(f32[96,1024]{1,0:T(8,128)} %collective-permute-done.5.refs_5_), channel_id=1, source_target_pairs={{0,96},{32,128},{64,160},{96,192},{128,224},{160,256},{192,288},{2... | collective-permute-start | bytes 1179656 | tf_op jit(solution)/shard_map/ppermute | solution.py:110
  111.2 4.6 %collective-permute-start.7 = (f32[256,1024]{1,0:T(8,128)S(1)}, f32[256,1024]{1,0:T(8,128)S(1)}, u32[]{:S(2)}, u32[]{:S(2)}) collective-permute-start(f32[256,1024]{1,0:T(8,128)S(1)} %get-tuple-element.18), channel_id=1, source_target_pairs={{0,1},{1,0},{2,3},{3,2},{4,5},{5,4},{6,7},{7,6},{8,9},{9,8},{10,11... | collective-permute-start | bytes 3145736 | tf_op jit(solution)/shard_map/ppermute | solution.py:154

commit v5 on v4

v5 whole, which is shorter than its diff:
```python
import jax
import jax.numpy as jnp
from jax import lax
from jax.experimental import pallas as pl
from jax.experimental.pallas import tpu as pltpu
from jax.sharding import PartitionSpec as P

BW = 128
NO = 32
NX, NY, NZH, NZL, NC = 4, 8, 4, 3, 2
WIDE, NARROW = NY * NZL, NX * NZH * NC
LR = 32
SLAB = 512
DEPTH = 768
COLS = 1024
OUT = 16
HALF = SLAB // 2

ZH_GROUPS = [[x * 8 + zh * 2 + c for zh in range(NZH)] for x in range(NX) for c in range(NC)]
CORE_SWAP = [(n, n ^ 1) for n in range(NARROW)]
X_NEAR = [(n, n ^ 8) for n in range(NARROW)]
X_FAR = [(n, n ^ 16) for n in range(NARROW)]
VMEM = pl.BlockSpec(memory_space=pltpu.VMEM)
SMEM = pl.BlockSpec(memory_space=pltpu.SMEM)


def y_shift(step):
    return [(y * NZL + zl, (y + step) % NY * NZL + zl) for y in range(NY) for zl in range(NZL)]


def zl_shift(step):
    return [(y * NZL + zl, y * NZL + (zl + step) % NZL) for y in range(NY) for zl in range(NZL)]


def swap_ij(rows):
    count, cols = rows.shape
    return jnp.swapaxes(rows.reshape(count, NO, NO), 1, 2).reshape(count, cols)


def pieces_kernel(row_irrep, col_irrep, block, out, turned):
    for x in range(NX):
        for col in range(DEPTH // BW):
            keep = row_irrep[x] == col_irrep[col]
            values = jnp.where(keep, block[x * BW : (x + 1) * BW, col * BW : (col + 1) * BW], 0.0)
            turned[col * BW : (col + 1) * BW, :] = values.T
        lanes = slice(x % 2 * BW, (x % 2 + 1) * BW)
        for rest in range(LR // 2):
            to = x // 2 * 16 + rest
            for far in range(2):
                rows = slice(far * WIDE, (far + 1) * WIDE)
                out[to, rows, lanes] = turned[pl.ds(to ^ (16 * far), WIDE, stride=LR), :]


def split_kernel(place, plus, minus, pieces, high, low, turned):
    x, core = place[0] // 8, place[0] % 2
    for group in range(DEPTH // BW):
        lanes = slice(group * BW, (group + 1) * BW)
        tile = [pieces[:, far * WIDE + group * 4 + i, :] for i in range(4) for far in range(2)]
        tile = jnp.concatenate(tile, axis=0).T
        top = tile.astype(jnp.bfloat16)
        rest = (tile - top.astype(jnp.float32)).astype(jnp.bfloat16)
        for sign, pick in enumerate((plus, minus)):
            total = jnp.dot(rest, pick[...], preferred_element_type=jnp.float32)
            turned[...] = total + jnp.dot(top, pick[...], preferred_element_type=jnp.float32)
            for away in range(2):
                for near in range(2):
                    for zh in range(NZH):
                        start = lax.bitwise_xor(x % 2, near) * BW + zh * LR + lax.bitwise_xor(core, away) * OUT
                        values = turned[pl.ds(pl.multiple_of(start, OUT), OUT), :]
                        upper = values.astype(jnp.bfloat16)
                        to = away * HALF + sign * BW + near * NZH * OUT + zh * OUT
                        high[to : to + OUT, lanes] = upper
                        low[to : to + OUT, lanes] = (values - upper.astype(jnp.float32)).astype(jnp.bfloat16)


def upper_triangle(shape):
    column = lax.broadcasted_iota(jnp.int32, shape, len(shape) - 1)
    return column // NO <= column % NO


def three_pass(high, low, s_high, s_low, rows):
    total = jnp.dot(low[rows, :], s_high[...], preferred_element_type=jnp.float32)
    total += jnp.dot(high[rows, :], s_low[...], preferred_element_type=jnp.float32)
    total += jnp.dot(high[rows, :], s_high[...], preferred_element_type=jnp.float32)
    return jnp.where(upper_triangle((BW, COLS)), total[:BW], total[BW:])


def first_kernel(place, high, low, *refs):
    blocks, (other, s_high, s_low) = refs[:NY], refs[NY:]
    y, zl = place[1] // NZL, lax.rem(place[1], NZL)
    for step, block in enumerate(blocks):
        at = lax.rem(y + step, NY) * (NZL * LR)
        for slot in range(NZL):
            owner = lax.rem(zl + (0, NZL - 1, 1)[slot], NZL)
            to = pl.ds(pl.multiple_of(at + owner * LR, LR), LR)
            values = block[slot * LR : (slot + 1) * LR, :]
            top = values.astype(jnp.bfloat16)
            s_high[to, :] = top
            s_low[to, :] = (values - top.astype(jnp.float32)).astype(jnp.bfloat16)
    other[...] = three_pass(high, low, s_high, s_low, slice(HALF, SLAB))


def second_kernel(high, low, s_high, s_low, own):
    own[...] = three_pass(high, low, s_high, s_low, slice(0, HALF))


def call(kernel, out_shape, in_specs, args, flops, moved, scratch=()):
    outs = out_shape if isinstance(out_shape, list) else [out_shape]
    found = pl.pallas_call(
        kernel,
        out_shape=outs,
        in_specs=in_specs,
        out_specs=[VMEM] * len(outs),
        scratch_shapes=list(scratch),
        compiler_params=pltpu.CompilerParams(vmem_limit_bytes=32 << 20),
        cost_estimate=pl.CostEstimate(flops=flops, bytes_accessed=moved, transcendentals=0),
    )(*args)
    return found if isinstance(out_shape, list) else found[0]


def gather_y(block):
    up, down = block, block
    found = {0: block}
    for step in (1, 2, 3):
        up = lax.ppermute(up, "wide", y_shift(1))
        down = lax.ppermute(down, "wide", y_shift(-1))
        found[NY - step], found[step] = up, down
    found[4] = lax.ppermute(up, "wide", y_shift(1))
    return [found[d] for d in range(NY)]


def pairs_of(partner):
    n = jnp.arange(NARROW, dtype=jnp.int32)
    first = n < partner
    before = first[None, :] & (n[None, :] < jnp.minimum(n, partner)[:, None])
    pair = before.astype(jnp.int32).sum(1)
    plus = (pair[None, :] == jnp.arange(NARROW // 2, dtype=jnp.int32)[:, None]).astype(jnp.float32)
    return plus, jnp.where(first[None, :], plus, -plus)


def local(integrals, amplitudes, row_irrep, col_irrep, partner):
    place = jnp.stack([lax.axis_index("narrow"), lax.axis_index("wide")]).astype(jnp.int32)

    rows = lax.all_to_all(amplitudes, "narrow", 0, 0, tiled=True)
    pieces = call(
        pieces_kernel,
        jax.ShapeDtypeStruct((NARROW, 2 * WIDE, HALF), jnp.float32),
        [SMEM, SMEM, VMEM],
        (row_irrep, col_irrep, integrals),
        0,
        3 << 20,
        [pltpu.VMEM((DEPTH, BW), jnp.float32)],
    )
    plus, minus = pairs_of(partner)
    pieces, rows = lax.optimization_barrier((pieces, rows))
    swapped = swap_ij(rows)
    even = jnp.dot(plus, rows + swapped, precision=lax.Precision.HIGHEST)
    odd = jnp.dot(minus, rows - swapped, precision=lax.Precision.HIGHEST)
    packed = 0.5 * jnp.where(upper_triangle((1, COLS)), even, odd)

    block = jnp.concatenate([packed, lax.ppermute(packed, "narrow", X_FAR)], axis=0)
    before = lax.ppermute(block, "wide", zl_shift(1))
    after = lax.ppermute(block, "wide", zl_shift(-1))
    pieces, before, after = lax.optimization_barrier((pieces, before, after))
    pieces = lax.all_to_all(pieces, "narrow", 0, 0, tiled=True)
    found = gather_y(jnp.concatenate([block, before, after], axis=0))
    eight = jnp.eye(8, dtype=jnp.float32)
    high, low = call(
        split_kernel,
        [jax.ShapeDtypeStruct((SLAB, DEPTH), jnp.bfloat16)] * 2,
        [SMEM, VMEM, VMEM, VMEM],
        (place, jnp.kron(eight, plus.T).astype(jnp.bfloat16), jnp.kron(eight, minus.T).astype(jnp.bfloat16), pieces),
        0,
        3 << 20,
        [pltpu.VMEM((HALF, BW), jnp.float32)],
    )

    product = jax.ShapeDtypeStruct((BW, COLS), jnp.float32)
    flops = 6 * HALF * DEPTH * COLS
    theirs, s_high, s_low = call(
        first_kernel,
        [product] + [jax.ShapeDtypeStruct((DEPTH, COLS), jnp.bfloat16)] * 2,
        [SMEM] + [VMEM] * (2 + NY),
        (place, high, low, *found),
        flops,
        6 << 20,
    )
    arrived = lax.ppermute(theirs, "narrow", CORE_SWAP)
    mine = call(second_kernel, product, [VMEM] * 4, (high, low, s_high, s_low), flops, 6 << 20)
    chip = mine + arrived
    share = NZH * OUT
    chip = chip[:share] + lax.ppermute(chip[share:], "narrow", X_NEAR)
    over_z = lax.all_to_all(chip, "narrow", 0, 0, tiled=True, axis_index_groups=ZH_GROUPS)
    result = over_z.reshape(NZH, OUT, COLS).sum(0)
    turned = swap_ij(result)
    column = jnp.arange(COLS, dtype=jnp.int32)[None, :]
    i, j = column // NO, column % NO
    return jnp.where(i < j, result - turned, jnp.where(i > j, result + turned, result))


def solution(mesh):
    return jax.shard_map(
        local,
        mesh=mesh,
        in_specs=(P("wide", "narrow"), P(("narrow", "wide"), None), P("wide"), P("narrow"), P()),
        out_specs=P(("wide", "narrow"), None),
        check_vma=False,
    )
```

time: 158 us -> 160 us (1.013)
  the two profiles are of different devices: /device:TPU:32 before, /device:TPU:24 now
where the time goes in v5:
time: 160 us; the launch traced here: 159 us
  starting transfers between devices  75.6 us (47%)
  waiting for transfers between devices  56.5 us (35%)
  local copies, waits for them, and re-layouts  13.8 us (9%)
  Pallas kernels  9.43 us (6%)
  other arithmetic  3.41 us (2%)
    ppermute x3, waiting for transfers between devices, gather_y(): up = lax.ppermute(up, 'wide', y_shift(1))  18 us
    all_to_all x1, starting transfers between devices, local(): rows = lax.all_to_all(amplitudes, 'narrow', 0, 0, tiled=True)  17.4 us
    all_to_all x1, waiting for transfers between devices, local(): lax.all_to_all(chip, 'narrow', 0, 0, tiled=True, axis_index_groups=ZH_GRO...  16.6 us
    ppermute x3, starting transfers between devices, gather_y(): up = lax.ppermute(up, 'wide', y_shift(1))  15.9 us
    pallas_call x4, Pallas kernels, call(): pl.pallas_call(kernel, out_shape=outs, in_specs=in_specs, out_specs=[VMEM...  9.43 us
    all_to_all x1, starting transfers between devices, local(): lax.all_to_all(chip, 'narrow', 0, 0, tiled=True, axis_index_groups=ZH_GRO...  8.97 us
    ppermute x1, waiting for transfers between devices, local(): chip = chip[:share] + lax.ppermute(chip[share:], 'narrow', X_NEAR)  6.94 us
    all_to_all x1, waiting for transfers between devices, local(): rows = lax.all_to_all(amplitudes, 'narrow', 0, 0, tiled=True)  6.3 us
  transfers between devices with their start and end apart: 15, of which 10 were waited for; matrix products, arithmetic and copies ran while one was open for 5% of the time, Pallas kernels for 4%

profile of v5, /device:TPU:24, one launch (start us, length us, event | category | flops | bytes accessed | tf_op | source)
XLA Modules:
  0.0 159.5 jit_solution(422930173757466427)
XLA Ops:
  0.0 1.7 %all_to_all.17 = f32[32,1,1024]{2,1,0:T(1,128)} reshape(f32[32,1024]{1,0:T(8,128)} %param.6) | data formatting | bytes 262144 | tf_op jit(solution)/shard_map/all_to_all | solution.py:144
  1.7 17.4 %all-to-all-start = ((f32[32,1,1024]{2,1,0:T(1,128)}), f32[32,1,1024]{2,1,0:T(1,128)S(1)}, u32[]{:S(2)}, u32[]{:S(2)}) async-start(f32[32,1,1024]{2,1,0:T(1,128)} %all_to_all.17), calls=%async_computation | async-start | bytes 262144 | tf_op jit(solution)/shard_map/all_to_all | solution.py:144
  19.0 0.7 iota_compare_fusion.6
  19.7 1.4 copy-done
  21.1 0.7 copy-done.3
  21.8 0.7 copy-done.4
  22.4 2.9 %shard_map.55 = f32[32,48,256]{2,1,0:T(8,128)} custom-call(s32[4]{0:T(128)S(1)} %copy-done.3, s32[6]{0:T(128)S(1)} %copy-done.4, f32[512,768]{1,0:T(8,128)S(1)} %copy-done), custom_call_target="tpu_custom_call" | custom-call | bytes 3145728 | tf_op jit(solution)/shard_map/pallas_call | solution.py:109
  25.3 0.2 convert_reduce_fusion
  25.5 6.3 %all-to-all-done = f32[32,1,1024]{2,1,0:T(1,128)S(1)} async-done(((f32[32,1,1024]{2,1,0:T(1,128)}), f32[32,1,1024]{2,1,0:T(1,128)S(1)}, u32[]{:S(2)}, u32[]{:S(2)}) %all-to-all-start) | async-done | bytes 131104 | tf_op jit(solution)/shard_map/all_to_all | solution.py:144
  32.0 0.2 copy.16
  32.2 0.2 reshape.143
  32.5 0.2 fusion.2
  32.6 0.2 fusion
  32.9 3.3 %collective-permute-start = (f32[16,1024]{1,0:T(8,128)S(1)}, f32[16,1024]{1,0:T(8,128)S(1)}, u32[]{:S(2)}, u32[]{:S(2)}) collective-permute-start(f32[16,1024]{1,0:T(8,128)S(1)} %fusion), channel_id=1, source_target_pairs={{0,16},{1,17},{2,18},{3,19},{4,20},{5,21},{6,22},{7,23},{8,24},{9,... | collective-permute-start | bytes 196616 | tf_op jit(solution)/shard_map/ppermute | solution.py:161
  36.1 4.4 %collective-permute-done = f32[16,1024]{1,0:T(8,128)S(1)} collective-permute-done((f32[16,1024]{1,0:T(8,128)S(1)}, f32[16,1024]{1,0:T(8,128)S(1)}, u32[]{:S(2)}, u32[]{:S(2)}) %collective-permute-start) | collective-permute-done | bytes 65568 | tf_op jit(solution)/shard_map/ppermute | solution.py:161
  40.5 4.1 %collective-permute-start.1 = (f32[32,1024]{1,0:T(8,128)S(1)}, f32[32,1024]{1,0:T(8,128)S(1)}, u32[]{:S(2)}, u32[]{:S(2)}) collective-permute-start(f32[32,1024]{1,0:T(8,128)S(1)} %pad_maximum_fusion.1), channel_id=1, source_target_pairs={{0,32},{32,64},{64,0},{96,128},{128,160},{160,96},{192,224},{224,2... | collective-permute-start | bytes 393224 | tf_op jit(solution)/shard_map/ppermute | solution.py:162
  44.6 3.6 %collective-permute-start.2 = (f32[32,1024]{1,0:T(8,128)S(1)}, f32[32,1024]{1,0:T(8,128)S(1)}, u32[]{:S(2)}, u32[]{:S(2)}) collective-permute-start(f32[32,1024]{1,0:T(8,128)S(1)} %pad_maximum_fusion.1), channel_id=1, source_target_pairs={{0,64},{32,0},{64,32},{96,160},{128,96},{160,128},{192,256},{224,1... | collective-permute-start | bytes 393224 | tf_op jit(solution)/shard_map/ppermute | solution.py:163
  48.2 1.0 collective-permute-done.1
  49.2 2.8 %collective-permute-done.2 = f32[32,1024]{1,0:T(8,128)S(1)} collective-permute-done((f32[32,1024]{1,0:T(8,128)S(1)}, f32[32,1024]{1,0:T(8,128)S(1)}, u32[]{:S(2)}, u32[]{:S(2)}) %collective-permute-start.2) | collective-permute-done | bytes 131104 | tf_op jit(solution)/shard_map/ppermute | solution.py:163
  52.0 5.8 %all-to-all-start.1 = ((f32[32,48,256]{2,1,0:T(8,128)}), f32[32,48,256]{2,1,0:T(8,128)S(1)}, u32[]{:S(2)}, u32[]{:S(2)}) async-start(f32[32,48,256]{2,1,0:T(8,128)} %shard_map.55), calls=%async_computation.1 | async-start | bytes 3145728 | tf_op jit(solution)/shard_map/all_to_all | solution.py:165
  57.9 4.7 %collective-permute-start.6 = (f32[96,1024]{1,0:T(8,128)S(1)}, f32[96,1024]{1,0:T(8,128)S(1)}, u32[]{:S(2)}, u32[]{:S(2)}) collective-permute-start(f32[96,1024]{1,0:T(8,128)S(1)} %pad_maximum_fusion.refs_0_), channel_id=1, source_target_pairs={{0,96},{32,128},{64,160},{96,192},{128,224},{160,256},{192,288},{2... | collective-permute-start | bytes 1179656 | tf_op jit(solution)/shard_map/ppermute | solution.py:125
  62.6 1.9 %collective-permute-start.3 = (f32[96,1024]{1,0:T(8,128)S(1)}, f32[96,1024]{1,0:T(8,128)S(1)}, u32[]{:S(2)}, u32[]{:S(2)}) collective-permute-start(f32[96,1024]{1,0:T(8,128)S(1)} %pad_maximum_fusion.refs_0_), channel_id=1, source_target_pairs={{0,672},{32,704},{64,736},{96,0},{128,32},{160,64},{192,96},{224,1... | collective-permute-start | bytes 1179656 | tf_op jit(solution)/shard_map/ppermute | solution.py:126
  64.5 6.9 %collective-permute-done.6.refs_7_ = f32[96,1024]{1,0:T(8,128)S(1)} collective-permute-done((f32[96,1024]{1,0:T(8,128)S(1)}, f32[96,1024]{1,0:T(8,128)S(1)}, u32[]{:S(2)}, u32[]{:S(2)}) %collective-permute-start.6) | collective-permute-done | bytes 393248 | tf_op jit(solution)/shard_map/ppermute | solution.py:125
  71.4 5.6 %collective-permute-start.7 = (f32[96,1024]{1,0:T(8,128)S(1)}, f32[96,1024]{1,0:T(8,128)S(1)}, u32[]{:S(2)}, u32[]{:S(2)}) collective-permute-start(f32[96,1024]{1,0:T(8,128)S(1)} %collective-permute-done.6.refs_7_), channel_id=1, source_target_pairs={{0,96},{32,128},{64,160},{96,192},{128,224},{160,256},{192,288},{2... | collective-permute-start | bytes 1179656 | tf_op jit(solution)/shard_map/ppermute | solution.py:125
  77.0 1.9 %collective-permute-start.4 = (f32[96,1024]{1,0:T(8,128)S(1)}, f32[96,1024]{1,0:T(8,128)S(1)}, u32[]{:S(2)}, u32[]{:S(2)}) collective-permute-start(f32[96,1024]{1,0:T(8,128)S(1)} %collective-permute-done.3.refs_1_), channel_id=1, source_target_pairs={{0,672},{32,704},{64,736},{96,0},{128,32},{160,64},{192,96},{224,1... | collective-permute-start | bytes 1179656 | tf_op jit(solution)/shard_map/ppermute | solution.py:126
  78.9 6.0 %collective-permute-done.7.refs_6_ = f32[96,1024]{1,0:T(8,128)S(1)} collective-permute-done((f32[96,1024]{1,0:T(8,128)S(1)}, f32[96,1024]{1,0:T(8,128)S(1)}, u32[]{:S(2)}, u32[]{:S(2)}) %collective-permute-start.7) | collective-permute-done | bytes 393248 | tf_op jit(solution)/shard_map/ppermute | solution.py:125
  85.0 5.6 %collective-permute-start.8 = (f32[96,1024]{1,0:T(8,128)S(1)}, f32[96,1024]{1,0:T(8,128)}, u32[]{:S(2)}, u32[]{:S(2)}) collective-permute-start(f32[96,1024]{1,0:T(8,128)S(1)} %collective-permute-done.7.refs_6_), channel_id=1, source_target_pairs={{0,96},{32,128},{64,160},{96,192},{128,224},{160,256},{192,288},{2... | collective-permute-start | bytes 1179656 | tf_op jit(solution)/shard_map/ppermute | solution.py:125
  90.6 1.9 %collective-permute-start.5 = (f32[96,1024]{1,0:T(8,128)S(1)}, f32[96,1024]{1,0:T(8,128)}, u32[]{:S(2)}, u32[]{:S(2)}) collective-permute-start(f32[96,1024]{1,0:T(8,128)S(1)} %collective-permute-done.4.refs_2_), channel_id=1, source_target_pairs={{0,672},{32,704},{64,736},{96,0},{128,32},{160,64},{192,96},{224,1... | collective-permute-start | bytes 1179656 | tf_op jit(solution)/shard_map/ppermute | solution.py:126
  92.5 5.1 %collective-permute-done.8.refs_5_ = f32[96,1024]{1,0:T(8,128)} collective-permute-done((f32[96,1024]{1,0:T(8,128)S(1)}, f32[96,1024]{1,0:T(8,128)}, u32[]{:S(2)}, u32[]{:S(2)}) %collective-permute-start.8) | collective-permute-done | bytes 393248 | tf_op jit(solution)/shard_map/ppermute | solution.py:125
  97.6 5.7 %collective-permute-start.9 = (f32[96,1024]{1,0:T(8,128)}, f32[96,1024]{1,0:T(8,128)}, u32[]{:S(2)}, u32[]{:S(2)}) collective-permute-start(f32[96,1024]{1,0:T(8,128)} %collective-permute-done.8.refs_5_), channel_id=1, source_target_pairs={{0,96},{32,128},{64,160},{96,192},{128,224},{160,256},{192,288},{2... | collective-permute-start | bytes 1179656 | tf_op jit(solution)/shard_map/ppermute | solution.py:128
  103.3 1.0 multiply_convert_fusion
  104.3 1.8 %convert_element_type.40 = bf16[256,128]{0,1:T(8,128)(2,1)} reshape(bf16[8,32,8,16]{1,0,3,2:T(8,128)(2,1)} %get-tuple-element.26) | data formatting | bytes 131072 | tf_op jit(solution)/shard_map/convert_element_type | solution.py:172
  106.1 1.6 copy.17.plus
  107.7 1.8 %convert_element_type.42 = bf16[256,128]{0,1:T(8,128)(2,1)} reshape(bf16[8,32,8,16]{1,0,3,2:T(8,128)(2,1)} %get-tuple-element.25) | data formatting | bytes 131072 | tf_op jit(solution)/shard_map/convert_element_type | solution.py:172
  109.5 1.6 copy.18.minus
  111.1 0.8 copy-done.1
  112.0 0.8 copy-done.2
  112.8 2.1 %shard_map.56 = (bf16[512,768]{1,0:T(8,128)(2,1)S(1)}, bf16[512,768]{1,0:T(8,128)(2,1)S(1)}) custom-call(s32[2]{0:T(128)S(1)} %pad_add_fusion.place, bf16[256,128]{1,0:T(8,128)(2,1)S(1)} %copy-done.1, bf16[256,128]{1,0:T(8,128)(2,1)S(1)} %copy-done.2, f32[32,48,256]{2,1,0:T(8,128)S(1)} %all-to-all-done.1.pieces), custom_call_target="tpu_custom_call" | custom-call | bytes 3145728 | tf_op jit(solution)/shard_map/pallas_call | solution.py:109
  114.9 3.1 %shard_map.57 = (f32[128,1024]{1,0:T(8,128)S(1)}, bf16[768,1024]{1,0:T(8,128)(2,1)S(1)}, bf16[768,1024]{1,0:T(8,128)(2,1)S(1)}) custom-call(s32[2]{0:T(128)S(1)} %pad_add_fusion.place, bf16[512,768]{1,0:T(8,128)(2,1)S(1)} %get-tuple-element.18.high, bf16[512,768]{1,0:T(8,128)(2,1)S(1)} %get-tuple-element.19.low, f32[96,1024]{1,0:T(8,128)S(1)} %pad_maximum_fusion.refs_0_, ...), custom_call_target="tpu_custom_call" | custom-call | flops 1207959552 | bytes 6291456 | tf_op jit(solution)/shard_map/pallas_call | solution.py:109
  118.0 1.9 %collective-permute-start.10 = (f32[128,1024]{1,0:T(8,128)S(1)}, f32[128,1024]{1,0:T(8,128)S(1)}, u32[]{:S(2)}, u32[]{:S(2)}) collective-permute-start(f32[128,1024]{1,0:T(8,128)S(1)} %get-tuple-element.24), channel_id=1, source_target_pairs={{0,1},{1,0},{2,3},{3,2},{4,5},{5,4},{6,7},{7,6},{8,9},{9,8},{10,11... | collective-permute-start | bytes 1572872 | tf_op jit(solution)/shard_map/ppermute | solution.py:188
  119.9 1.4 shard_map.58
  121.3 0.5 collective-permute-done.10
  121.9 3.3 %collective-permute-start.11 = (f32[64,1024]{1,0:T(8,128)S(1)}, f32[64,1024]{1,0:T(8,128)S(1)}, u32[]{:S(2)}, u32[]{:S(2)}) collective-permute-start(f32[64,1024]{1,0:T(8,128)S(1)} %slice.9), channel_id=1, source_target_pairs={{0,8},{1,9},{2,10},{3,11},{4,12},{5,13},{6,14},{7,15},{8,0},{9,1},... | collective-permute-start | bytes 786440 | tf_op jit(solution)/shard_map/ppermute | solution.py:192
  125.2 6.9 %collective-permute-done.11 = f32[64,1024]{1,0:T(8,128)S(1)} collective-permute-done((f32[64,1024]{1,0:T(8,128)S(1)}, f32[64,1024]{1,0:T(8,128)S(1)}, u32[]{:S(2)}, u32[]{:S(2)}) %collective-permute-start.11) | collective-permute-done | bytes 262176 | tf_op jit(solution)/shard_map/ppermute | solution.py:192
  132.1 0.7 slice_add_fusion
  132.9 9.0 %all-to-all-start.2 = ((f32[4,16,1024]{2,1,0:T(8,128)}), f32[4,16,1024]{2,1,0:T(8,128)S(1)}, u32[]{:S(2)}, u32[]{:S(2)}) async-start(f32[4,16,1024]{2,1,0:T(8,128)} %bitcast.3), calls=%async_computation.2 | async-start | bytes 524288 | tf_op jit(solution)/shard_map/all_to_all | solution.py:193
  141.8 16.6 %all-to-all-done.2 = f32[4,16,1024]{2,1,0:T(8,128)S(1)} async-done(((f32[4,16,1024]{2,1,0:T(8,128)}), f32[4,16,1024]{2,1,0:T(8,128)S(1)}, u32[]{:S(2)}, u32[]{:S(2)}) %all-to-all-start.2) | async-done | bytes 262176 | tf_op jit(solution)/shard_map/all_to_all | solution.py:193
  158.8 0.6 fusion.4
  (29 shorter events, 0.8 us)
Async XLA Ops:
  1.7 30.2 %all-to-all-start = ((f32[32,1,1024]{2,1,0:T(1,128)}), f32[32,1,1024]{2,1,0:T(1,128)S(1)}, u32[]{:S(2)}, u32[]{:S(2)}) async-start(f32[32,1,1024]{2,1,0:T(1,128)} %all_to_all.17), calls=%async_computation | async-start | bytes 262144 | tf_op jit(solution)/shard_map/all_to_all | solution.py:144
  19.7 1.4 copy-start
  21.1 0.7 copy-start.3
  21.8 0.7 copy-start.4
  22.4 2.9 %copy-start.5 = (s32[32]{0:T(128)S(1)}, s32[32]{0:T(128)}, u32[]{:S(2)}) copy-start(s32[32]{0:T(128)} %param.9) | copy-start | bytes 388
  32.9 7.7 %collective-permute-start = (f32[16,1024]{1,0:T(8,128)S(1)}, f32[16,1024]{1,0:T(8,128)S(1)}, u32[]{:S(2)}, u32[]{:S(2)}) collective-permute-start(f32[16,1024]{1,0:T(8,128)S(1)} %fusion), channel_id=1, source_target_pairs={{0,16},{1,17},{2,18},{3,19},{4,20},{5,21},{6,22},{7,23},{8,24},{9,... | collective-permute-start | bytes 196616 | tf_op jit(solution)/shard_map/ppermute | solution.py:161
  40.5 8.7 %collective-permute-start.1 = (f32[32,1024]{1,0:T(8,128)S(1)}, f32[32,1024]{1,0:T(8,128)S(1)}, u32[]{:S(2)}, u32[]{:S(2)}) collective-permute-start(f32[32,1024]{1,0:T(8,128)S(1)} %pad_maximum_fusion.1), channel_id=1, source_target_pairs={{0,32},{32,64},{64,0},{96,128},{128,160},{160,96},{192,224},{224,2... | collective-permute-start | bytes 393224 | tf_op jit(solution)/shard_map/ppermute | solution.py:162
  44.6 7.4 %collective-permute-start.2 = (f32[32,1024]{1,0:T(8,128)S(1)}, f32[32,1024]{1,0:T(8,128)S(1)}, u32[]{:S(2)}, u32[]{:S(2)}) collective-permute-start(f32[32,1024]{1,0:T(8,128)S(1)} %pad_maximum_fusion.1), channel_id=1, source_target_pairs={{0,64},{32,0},{64,32},{96,160},{128,96},{160,128},{192,256},{224,1... | collective-permute-start | bytes 393224 | tf_op jit(solution)/shard_map/ppermute | solution.py:163
  52.0 59.1 %all-to-all-start.1 = ((f32[32,48,256]{2,1,0:T(8,128)}), f32[32,48,256]{2,1,0:T(8,128)S(1)}, u32[]{:S(2)}, u32[]{:S(2)}) async-start(f32[32,48,256]{2,1,0:T(8,128)} %shard_map.55), calls=%async_computation.1 | async-start | bytes 3145728 | tf_op jit(solution)/shard_map/all_to_all | solution.py:165
  57.9 13.5 %collective-permute-start.6 = (f32[96,1024]{1,0:T(8,128)S(1)}, f32[96,1024]{1,0:T(8,128)S(1)}, u32[]{:S(2)}, u32[]{:S(2)}) collective-permute-start(f32[96,1024]{1,0:T(8,128)S(1)} %pad_maximum_fusion.refs_0_), channel_id=1, source_target_pairs={{0,96},{32,128},{64,160},{96,192},{128,224},{160,256},{192,288},{2... | collective-permute-start | bytes 1179656 | tf_op jit(solution)/shard_map/ppermute | solution.py:125
  62.6 14.4 %collective-permute-start.3 = (f32[96,1024]{1,0:T(8,128)S(1)}, f32[96,1024]{1,0:T(8,128)S(1)}, u32[]{:S(2)}, u32[]{:S(2)}) collective-permute-start(f32[96,1024]{1,0:T(8,128)S(1)} %pad_maximum_fusion.refs_0_), channel_id=1, source_target_pairs={{0,672},{32,704},{64,736},{96,0},{128,32},{160,64},{192,96},{224,1... | collective-permute-start | bytes 1179656 | tf_op jit(solution)/shard_map/ppermute | solution.py:126
  71.4 13.6 %collective-permute-start.7 = (f32[96,1024]{1,0:T(8,128)S(1)}, f32[96,1024]{1,0:T(8,128)S(1)}, u32[]{:S(2)}, u32[]{:S(2)}) collective-permute-start(f32[96,1024]{1,0:T(8,128)S(1)} %collective-permute-done.6.refs_7_), channel_id=1, source_target_pairs={{0,96},{32,128},{64,160},{96,192},{128,224},{160,256},{192,288},{2... | collective-permute-start | bytes 1179656 | tf_op jit(solution)/shard_map/ppermute | solution.py:125
  77.0 13.6 %collective-permute-start.4 = (f32[96,1024]{1,0:T(8,128)S(1)}, f32[96,1024]{1,0:T(8,128)S(1)}, u32[]{:S(2)}, u32[]{:S(2)}) collective-permute-start(f32[96,1024]{1,0:T(8,128)S(1)} %collective-permute-done.3.refs_1_), channel_id=1, source_target_pairs={{0,672},{32,704},{64,736},{96,0},{128,32},{160,64},{192,96},{224,1... | collective-permute-start | bytes 1179656 | tf_op jit(solution)/shard_map/ppermute | solution.py:126
  85.0 12.7 %collective-permute-start.8 = (f32[96,1024]{1,0:T(8,128)S(1)}, f32[96,1024]{1,0:T(8,128)}, u32[]{:S(2)}, u32[]{:S(2)}) collective-permute-start(f32[96,1024]{1,0:T(8,128)S(1)} %collective-permute-done.7.refs_6_), channel_id=1, source_target_pairs={{0,96},{32,128},{64,160},{96,192},{128,224},{160,256},{192,288},{2... | collective-permute-start | bytes 1179656 | tf_op jit(solution)/shard_map/ppermute | solution.py:125
  90.6 24.3 %collective-permute-start.5 = (f32[96,1024]{1,0:T(8,128)S(1)}, f32[96,1024]{1,0:T(8,128)}, u32[]{:S(2)}, u32[]{:S(2)}) collective-permute-start(f32[96,1024]{1,0:T(8,128)S(1)} %collective-permute-done.4.refs_2_), channel_id=1, source_target_pairs={{0,672},{32,704},{64,736},{96,0},{128,32},{160,64},{192,96},{224,1... | collective-permute-start | bytes 1179656 | tf_op jit(solution)/shard_map/ppermute | solution.py:126
  97.6 17.3 %collective-permute-start.9 = (f32[96,1024]{1,0:T(8,128)}, f32[96,1024]{1,0:T(8,128)}, u32[]{:S(2)}, u32[]{:S(2)}) collective-permute-start(f32[96,1024]{1,0:T(8,128)} %collective-permute-done.8.refs_5_), channel_id=1, source_target_pairs={{0,96},{32,128},{64,160},{96,192},{128,224},{160,256},{192,288},{2... | collective-permute-start | bytes 1179656 | tf_op jit(solution)/shard_map/ppermute | solution.py:128
  111.1 0.8 copy-start.1
  112.0 0.8 copy-start.2
  118.0 3.8 %collective-permute-start.10 = (f32[128,1024]{1,0:T(8,128)S(1)}, f32[128,1024]{1,0:T(8,128)S(1)}, u32[]{:S(2)}, u32[]{:S(2)}) collective-permute-start(f32[128,1024]{1,0:T(8,128)S(1)} %get-tuple-element.24), channel_id=1, source_target_pairs={{0,1},{1,0},{2,3},{3,2},{4,5},{5,4},{6,7},{7,6},{8,9},{9,8},{10,11... | collective-permute-start | bytes 1572872 | tf_op jit(solution)/shard_map/ppermute | solution.py:188
  121.9 10.2 %collective-permute-start.11 = (f32[64,1024]{1,0:T(8,128)S(1)}, f32[64,1024]{1,0:T(8,128)S(1)}, u32[]{:S(2)}, u32[]{:S(2)}) collective-permute-start(f32[64,1024]{1,0:T(8,128)S(1)} %slice.9), channel_id=1, source_target_pairs={{0,8},{1,9},{2,10},{3,11},{4,12},{5,13},{6,14},{7,15},{8,0},{9,1},... | collective-permute-start | bytes 786440 | tf_op jit(solution)/shard_map/ppermute | solution.py:192
  132.9 25.5 %all-to-all-start.2 = ((f32[4,16,1024]{2,1,0:T(8,128)}), f32[4,16,1024]{2,1,0:T(8,128)S(1)}, u32[]{:S(2)}, u32[]{:S(2)}) async-start(f32[4,16,1024]{2,1,0:T(8,128)} %bitcast.3), calls=%async_computation.2 | async-start | bytes 524288 | tf_op jit(solution)/shard_map/all_to_all | solution.py:193

commit v6 on v5

--- a/solution.py
+++ b/solution.py
@@ -16,20 +16,22 @@
 OUT = 16
 HALF = SLAB // 2
 
-ZH_GROUPS = [[x * 8 + zh * 2 + c for zh in range(NZH)] for x in range(NX) for c in range(NC)]
+X_GROUPS = [[x * 8 + rest for x in range(NX)] for rest in range(8)]
 CORE_SWAP = [(n, n ^ 1) for n in range(NARROW)]
-X_NEAR = [(n, n ^ 8) for n in range(NARROW)]
-X_FAR = [(n, n ^ 16) for n in range(NARROW)]
+Z_FAR = [(n, n ^ 4) for n in range(NARROW)]
+SIX_GROUPS = [
+    [(y * NZL + zl) * NARROW + x * 8 + (pair * 2 + zh) * 2 + c for zh in range(2) for zl in range(NZL)]
+    for y in range(NY)
+    for x in range(NX)
+    for pair in range(2)
+    for c in range(NC)
+]
 VMEM = pl.BlockSpec(memory_space=pltpu.VMEM)
 SMEM = pl.BlockSpec(memory_space=pltpu.SMEM)
 
 
 def y_shift(step):
     return [(y * NZL + zl, (y + step) % NY * NZL + zl) for y in range(NY) for zl in range(NZL)]
-
-
-def zl_shift(step):
-    return [(y * NZL + zl, y * NZL + (zl + step) % NZL) for y in range(NY) for zl in range(NZL)]
 
 
 def swap_ij(rows):
@@ -41,21 +43,44 @@
     for x in range(NX):
         for col in range(DEPTH // BW):
             keep = row_irrep[x] == col_irrep[col]
-            values = jnp.where(keep, block[x * BW : (x + 1) * BW, col * BW : (col + 1) * BW], 0.0)
-            turned[col * BW : (col + 1) * BW, :] = values.T
-        lanes = slice(x % 2 * BW, (x % 2 + 1) * BW)
-        for rest in range(LR // 2):
-            to = x // 2 * 16 + rest
-            for far in range(2):
-                rows = slice(far * WIDE, (far + 1) * WIDE)
-                out[to, rows, lanes] = turned[pl.ds(to ^ (16 * far), WIDE, stride=LR), :]
-
-
-def split_kernel(place, plus, minus, pieces, high, low, turned):
-    x, core = place[0] // 8, place[0] % 2
+            values = jnp.where(keep, block[x * BW : (x + 1) * BW, col * BW : (col + 1) * BW], 0.0).T
+            even = [values[:, zh * LR : (zh + 1) * LR] for zh in (0, 2, 1, 3)]
+            turned[col * BW : (col + 1) * BW, :] = jnp.concatenate(even, axis=1)
+        lanes = slice(x * BW // 2, (x + 1) * BW // 2)
+        for to in range(NARROW):
+            odd = to // 2 % 2
+            for near in range(2):
+                rows = slice(near * WIDE, (near + 1) * WIDE)
+                column = to & ~2 | near * 2
+                found = turned[pl.ds(column, WIDE, stride=LR), :]
+                out[to, rows, lanes] = found[:, odd * (BW // 2) : (odd + 1) * (BW // 2)]
+
+
+def fill_pairs(partner, plus, minus, turned, ranks):
+    count = jnp.int32(0)
+    for n in range(NARROW):
+        ranks[n] = count
+        count = count + jnp.where(partner[n] > n, 1, 0)
+    lane = lax.broadcasted_iota(jnp.int32, (1, BW), 1)
+    for n in range(NARROW):
+        pair = ranks[jnp.minimum(partner[n], n)]
+        sign = jnp.where(partner[n] > n, 1.0, -1.0)
+        one = jnp.where(lane % (NARROW // 2) == pair, 1.0, 0.0)
+        turned[n : n + 1, :] = one
+        turned[NARROW + n : NARROW + n + 1, :] = one * sign
+    for group in range(8):
+        inside = lane // (NARROW // 2) == group
+        rows = slice(group * NARROW, (group + 1) * NARROW)
+        plus[rows, :] = jnp.where(inside, turned[:NARROW, :], 0.0).astype(jnp.bfloat16)
+        minus[rows, :] = jnp.where(inside, turned[NARROW : 2 * NARROW, :], 0.0).astype(jnp.bfloat16)
+
+
+def split_kernel(place, partner, pieces, high, low, turned, plus, minus, ranks):
+    fill_pairs(partner, plus, minus, turned, ranks)
+    far, core = place[0] // 4 % 2, place[0] % 2
     for group in range(DEPTH // BW):
         lanes = slice(group * BW, (group + 1) * BW)
-        tile = [pieces[:, far * WIDE + group * 4 + i, :] for i in range(4) for far in range(2)]
+        tile = [pieces[:, near * WIDE + group * 4 + i, :] for i in range(4) for near in range(2)]
         tile = jnp.concatenate(tile, axis=0).T
         top = tile.astype(jnp.bfloat16)
         rest = (tile - top.astype(jnp.float32)).astype(jnp.bfloat16)
@@ -63,12 +88,12 @@
             total = jnp.dot(rest, pick[...], preferred_element_type=jnp.float32)
             turned[...] = total + jnp.dot(top, pick[...], preferred_element_type=jnp.float32)
             for away in range(2):
-                for near in range(2):
-                    for zh in range(NZH):
-                        start = lax.bitwise_xor(x % 2, near) * BW + zh * LR + lax.bitwise_xor(core, away) * OUT
+                for x in range(NX):
+                    for across in range(2):
+                        start = x * (BW // 2) + lax.bitwise_xor(far, across) * LR + lax.bitwise_xor(core, away) * OUT
                         values = turned[pl.ds(pl.multiple_of(start, OUT), OUT), :]
                         upper = values.astype(jnp.bfloat16)
-                        to = away * HALF + sign * BW + near * NZH * OUT + zh * OUT
+                        to = away * HALF + sign * BW + x * LR + across * OUT
                         high[to : to + OUT, lanes] = upper
                         low[to : to + OUT, lanes] = (values - upper.astype(jnp.float32)).astype(jnp.bfloat16)
 
@@ -87,13 +112,14 @@
 
 def first_kernel(place, high, low, *refs):
     blocks, (other, s_high, s_low) = refs[:NY], refs[NY:]
-    y, zl = place[1] // NZL, lax.rem(place[1], NZL)
+    y = place[1] // NZL
+    half = NARROW // 2
     for step, block in enumerate(blocks):
         at = lax.rem(y + step, NY) * (NZL * LR)
-        for slot in range(NZL):
-            owner = lax.rem(zl + (0, NZL - 1, 1)[slot], NZL)
-            to = pl.ds(pl.multiple_of(at + owner * LR, LR), LR)
-            values = block[slot * LR : (slot + 1) * LR, :]
+        for zl in range(NZL):
+            to = pl.ds(pl.multiple_of(at + zl * LR, LR), LR)
+            values = [block[(near * NZL + zl) * half : (near * NZL + zl + 1) * half, :] for near in range(2)]
+            values = jnp.concatenate(values, axis=0)
             top = values.astype(jnp.bfloat16)
             s_high[to, :] = top
             s_low[to, :] = (values - top.astype(jnp.float32)).astype(jnp.bfloat16)
@@ -158,21 +184,19 @@
     odd = jnp.dot(minus, rows - swapped, precision=lax.Precision.HIGHEST)
     packed = 0.5 * jnp.where(upper_triangle((1, COLS)), even, odd)
 
-    block = jnp.concatenate([packed, lax.ppermute(packed, "narrow", X_FAR)], axis=0)
-    before = lax.ppermute(block, "wide", zl_shift(1))
-    after = lax.ppermute(block, "wide", zl_shift(-1))
-    pieces, before, after = lax.optimization_barrier((pieces, before, after))
+    block = lax.all_gather(packed, ("wide", "narrow"), axis=0, tiled=True, axis_index_groups=SIX_GROUPS)
+    pieces, block = lax.optimization_barrier((pieces, block))
     pieces = lax.all_to_all(pieces, "narrow", 0, 0, tiled=True)
-    found = gather_y(jnp.concatenate([block, before, after], axis=0))
-    eight = jnp.eye(8, dtype=jnp.float32)
+    found = gather_y(block)
     high, low = call(
         split_kernel,
         [jax.ShapeDtypeStruct((SLAB, DEPTH), jnp.bfloat16)] * 2,
-        [SMEM, VMEM, VMEM, VMEM],
-        (place, jnp.kron(eight, plus.T).astype(jnp.bfloat16), jnp.kron(eight, minus.T).astype(jnp.bfloat16), pieces),
+        [SMEM, SMEM, VMEM],
+        (place, partner, pieces),
         0,
         3 << 20,
-        [pltpu.VMEM((HALF, BW), jnp.float32)],
+        [pltpu.VMEM((HALF, BW), dtype) for dtype in (jnp.float32, jnp.bfloat16, jnp.bfloat16)]
+        + [pltpu.SMEM((NARROW,), jnp.int32)],
     )
 
     product = jax.ShapeDtypeStruct((BW, COLS), jnp.float32)
@@ -188,10 +212,9 @@
     arrived = lax.ppermute(theirs, "narrow", CORE_SWAP)
     mine = call(second_kernel, product, [VMEM] * 4, (high, low, s_high, s_low), flops, 6 << 20)
     chip = mine + arrived
-    share = NZH * OUT
-    chip = chip[:share] + lax.ppermute(chip[share:], "narrow", X_NEAR)
-    over_z = lax.all_to_all(chip, "narrow", 0, 0, tiled=True, axis_index_groups=ZH_GROUPS)
-    result = over_z.reshape(NZH, OUT, COLS).sum(0)
+    over_x = lax.all_to_all(chip, "narrow", 0, 0, tiled=True, axis_index_groups=X_GROUPS)
+    reduced = over_x.reshape(NX, 2 * OUT, COLS).sum(0)
+    result = reduced[:OUT] + lax.ppermute(reduced[OUT:], "narrow", Z_FAR)
     turned = swap_ij(result)
     column = jnp.arange(COLS, dtype=jnp.int32)[None, :]
     i, j = column // NO, column % NO

time: 160 us -> 165 us (1.031)
  the two profiles are of different devices: /device:TPU:24 before, /device:TPU:16 now
where the time goes in v6:
time: 165 us; the launch traced here: 164 us
  starting transfers between devices  57.1 us (35%)
  waiting for transfers between devices  45.6 us (28%)
  blocking collectives  42.7 us (26%)
  Pallas kernels  11.3 us (7%)
  local copies, waits for them, and re-layouts  5.38 us (3%)
  other arithmetic  1.7 us (1%)
    all_gather x1, blocking collectives, local(): lax.all_gather(packed, ('wide', 'narrow'), axis=0, tiled=True, axis_index...  30.2 us
    ppermute x3, waiting for transfers between devices, gather_y(): up = lax.ppermute(up, 'wide', y_shift(1))  18.2 us
    all_to_all x1, starting transfers between devices, local(): rows = lax.all_to_all(amplitudes, 'narrow', 0, 0, tiled=True)  17.4 us
    all_to_all x1, waiting for transfers between devices, local(): pieces = lax.all_to_all(pieces, 'narrow', 0, 0, tiled=True)  14.6 us
    all_to_all x1, blocking collectives, local(): lax.all_to_all(chip, 'narrow', 0, 0, tiled=True, axis_index_groups=X_GROUPS)  12.5 us
    ppermute x3, starting transfers between devices, gather_y(): up = lax.ppermute(up, 'wide', y_shift(1))  12.3 us
    pallas_call x4, Pallas kernels, call(): pl.pallas_call(kernel, out_shape=outs, in_specs=in_specs, out_specs=[VMEM...  11.3 us
    all_to_all x1, starting transfers between devices, local(): pieces = lax.all_to_all(pieces, 'narrow', 0, 0, tiled=True)  8.17 us
  transfers between devices with their start and end apart: 11, of which 9 were waited for; matrix products, arithmetic and copies ran while one was open for 1% of the time, Pallas kernels for 5%

profile of v6, /device:TPU:16, one launch (start us, length us, event | category | flops | bytes accessed | tf_op | source)
XLA Modules:
  0.0 164.4 jit_solution(16082915509793831432)
XLA Ops:
  0.0 1.6 all_to_all.17
  1.6 17.4 %all-to-all-start = ((f32[32,1,1024]{2,1,0:T(1,128)}), f32[32,1,1024]{2,1,0:T(1,128)S(1)}, u32[]{:S(2)}, u32[]{:S(2)}) async-start(f32[32,1,1024]{2,1,0:T(1,128)} %all_to_all.17), calls=%async_computation | async-start | bytes 262144 | tf_op jit(solution)/shard_map/all_to_all | solution.py:170
  19.0 0.7 iota_compare_fusion.4
  19.7 0.0 copy-start
  19.7 1.4 copy-done
  21.1 0.0 copy-start.1
  21.1 0.7 copy-done.1
  21.7 0.7 copy-done.2
  22.4 4.6 %shard_map.55 = f32[32,48,256]{2,1,0:T(8,128)} custom-call(s32[4]{0:T(128)S(1)} %copy-done.1, s32[6]{0:T(128)S(1)} %copy-done.2, f32[512,768]{1,0:T(8,128)S(1)} %copy-done), custom_call_target="tpu_custom_call" | custom-call | bytes 3145728 | tf_op jit(solution)/shard_map/pallas_call | solution.py:135
  27.0 0.0 copy-done.3
  27.0 0.2 convert_reduce_fusion
  27.2 4.6 %all-to-all-done = f32[32,1,1024]{2,1,0:T(1,128)S(1)} async-done(((f32[32,1,1024]{2,1,0:T(1,128)}), f32[32,1,1024]{2,1,0:T(1,128)S(1)}, u32[]{:S(2)}, u32[]{:S(2)}) %all-to-all-start) | async-done | bytes 131104 | tf_op jit(solution)/shard_map/all_to_all | solution.py:170
  31.8 0.2 reshape.80
  32.0 0.2 copy.10
  32.2 0.2 reshape.81
  32.4 0.2 fusion.2
  32.6 0.2 fusion
  32.8 30.2 %all_gather.3.refs_0_ = f32[96,1024]{1,0:T(8,128)S(1)} all-gather(f32[16,1024]{1,0:T(8,128)S(1)} %fusion), channel_id=1, replica_groups={{0,32,64,2,34,66},{1,33,65,3,35,67},{4,36,68,6,38,70},{5,37,69,7,39,71}..., dimensions={0}, use_global_device_ids=true | all-gather | bytes 458752 | tf_op jit(solution)/shard_map/all_gather | solution.py:187
  63.1 8.2 %all-to-all-start.1 = ((f32[32,48,256]{2,1,0:T(8,128)}), f32[32,48,256]{2,1,0:T(8,128)S(1)}, u32[]{:S(2)}, u32[]{:S(2)}) async-start(f32[32,48,256]{2,1,0:T(8,128)} %shard_map.55), calls=%async_computation.1 | async-start | bytes 3145728 | tf_op jit(solution)/shard_map/all_to_all | solution.py:189
  71.3 3.5 %collective-permute-start.3 = (f32[96,1024]{1,0:T(8,128)S(1)}, f32[96,1024]{1,0:T(8,128)S(1)}, u32[]{:S(2)}, u32[]{:S(2)}) collective-permute-start(f32[96,1024]{1,0:T(8,128)S(1)} %all_gather.3.refs_0_), channel_id=1, source_target_pairs={{0,96},{32,128},{64,160},{96,192},{128,224},{160,256},{192,288},{2... | collective-permute-start | bytes 1179656 | tf_op jit(solution)/shard_map/ppermute | solution.py:151
  74.8 2.3 %collective-permute-start = (f32[96,1024]{1,0:T(8,128)S(1)}, f32[96,1024]{1,0:T(8,128)S(1)}, u32[]{:S(2)}, u32[]{:S(2)}) collective-permute-start(f32[96,1024]{1,0:T(8,128)S(1)} %all_gather.3.refs_0_), channel_id=1, source_target_pairs={{0,672},{32,704},{64,736},{96,0},{128,32},{160,64},{192,96},{224,1... | collective-permute-start | bytes 1179656 | tf_op jit(solution)/shard_map/ppermute | solution.py:152
  77.1 7.3 %collective-permute-done.3.refs_7_ = f32[96,1024]{1,0:T(8,128)S(1)} collective-permute-done((f32[96,1024]{1,0:T(8,128)S(1)}, f32[96,1024]{1,0:T(8,128)S(1)}, u32[]{:S(2)}, u32[]{:S(2)}) %collective-permute-start.3) | collective-permute-done | bytes 393248 | tf_op jit(solution)/shard_map/ppermute | solution.py:151
  84.4 3.8 %collective-permute-start.4 = (f32[96,1024]{1,0:T(8,128)S(1)}, f32[96,1024]{1,0:T(8,128)S(1)}, u32[]{:S(2)}, u32[]{:S(2)}) collective-permute-start(f32[96,1024]{1,0:T(8,128)S(1)} %collective-permute-done.3.refs_7_), channel_id=1, source_target_pairs={{0,96},{32,128},{64,160},{96,192},{128,224},{160,256},{192,288},{2... | collective-permute-start | bytes 1179656 | tf_op jit(solution)/shard_map/ppermute | solution.py:151
  88.2 0.5 collective-permute-done.refs_1_
  88.7 1.9 %collective-permute-start.1 = (f32[96,1024]{1,0:T(8,128)S(1)}, f32[96,1024]{1,0:T(8,128)S(1)}, u32[]{:S(2)}, u32[]{:S(2)}) collective-permute-start(f32[96,1024]{1,0:T(8,128)S(1)} %collective-permute-done.refs_1_), channel_id=1, source_target_pairs={{0,672},{32,704},{64,736},{96,0},{128,32},{160,64},{192,96},{224,1... | collective-permute-start | bytes 1179656 | tf_op jit(solution)/shard_map/ppermute | solution.py:152
  90.6 6.2 %collective-permute-done.4.refs_6_ = f32[96,1024]{1,0:T(8,128)S(1)} collective-permute-done((f32[96,1024]{1,0:T(8,128)S(1)}, f32[96,1024]{1,0:T(8,128)S(1)}, u32[]{:S(2)}, u32[]{:S(2)}) %collective-permute-start.4) | collective-permute-done | bytes 393248 | tf_op jit(solution)/shard_map/ppermute | solution.py:151
  96.8 5.0 %collective-permute-start.5 = (f32[96,1024]{1,0:T(8,128)S(1)}, f32[96,1024]{1,0:T(8,128)}, u32[]{:S(2)}, u32[]{:S(2)}) collective-permute-start(f32[96,1024]{1,0:T(8,128)S(1)} %collective-permute-done.4.refs_6_), channel_id=1, source_target_pairs={{0,96},{32,128},{64,160},{96,192},{128,224},{160,256},{192,288},{2... | collective-permute-start | bytes 1179656 | tf_op jit(solution)/shard_map/ppermute | solution.py:151
  101.8 0.5 collective-permute-done.1.refs_2_
  102.3 1.9 %collective-permute-start.2 = (f32[96,1024]{1,0:T(8,128)S(1)}, f32[96,1024]{1,0:T(8,128)}, u32[]{:S(2)}, u32[]{:S(2)}) collective-permute-start(f32[96,1024]{1,0:T(8,128)S(1)} %collective-permute-done.1.refs_2_), channel_id=1, source_target_pairs={{0,672},{32,704},{64,736},{96,0},{128,32},{160,64},{192,96},{224,1... | collective-permute-start | bytes 1179656 | tf_op jit(solution)/shard_map/ppermute | solution.py:152
  104.2 4.7 %collective-permute-done.5.refs_5_ = f32[96,1024]{1,0:T(8,128)} collective-permute-done((f32[96,1024]{1,0:T(8,128)S(1)}, f32[96,1024]{1,0:T(8,128)}, u32[]{:S(2)}, u32[]{:S(2)}) %collective-permute-start.5) | collective-permute-done | bytes 393248 | tf_op jit(solution)/shard_map/ppermute | solution.py:151
  108.9 5.6 %collective-permute-start.6 = (f32[96,1024]{1,0:T(8,128)}, f32[96,1024]{1,0:T(8,128)}, u32[]{:S(2)}, u32[]{:S(2)}) collective-permute-start(f32[96,1024]{1,0:T(8,128)} %collective-permute-done.5.refs_5_), channel_id=1, source_target_pairs={{0,96},{32,128},{64,160},{96,192},{128,224},{160,256},{192,288},{2... | collective-permute-start | bytes 1179656 | tf_op jit(solution)/shard_map/ppermute | solution.py:154
  114.5 0.1 pad_add_fusion.place
  114.5 14.6 %all-to-all-done.1.pieces = f32[32,48,256]{2,1,0:T(8,128)S(1)} async-done(((f32[32,48,256]{2,1,0:T(8,128)}), f32[32,48,256]{2,1,0:T(8,128)S(1)}, u32[]{:S(2)}, u32[]{:S(2)}) %all-to-all-start.1) | async-done | bytes 1572896 | tf_op jit(solution)/shard_map/all_to_all | solution.py:189
  129.1 2.2 %shard_map.56 = (bf16[512,768]{1,0:T(8,128)(2,1)S(1)}, bf16[512,768]{1,0:T(8,128)(2,1)S(1)}) custom-call(s32[2]{0:T(128)S(1)} %pad_add_fusion.place, s32[32]{0:T(128)S(1)} %copy-done.3, f32[32,48,256]{2,1,0:T(8,128)S(1)} %all-to-all-done.1.pieces), custom_call_target="tpu_custom_call" | custom-call | bytes 3145728 | tf_op jit(solution)/shard_map/pallas_call | solution.py:135
  131.3 0.0 collective-permute-done.2.refs_3_
  131.3 0.0 collective-permute-done.6.refs_4_
  131.3 3.1 %shard_map.57 = (f32[128,1024]{1,0:T(8,128)S(1)}, bf16[768,1024]{1,0:T(8,128)(2,1)S(1)}, bf16[768,1024]{1,0:T(8,128)(2,1)S(1)}) custom-call(s32[2]{0:T(128)S(1)} %pad_add_fusion.place, bf16[512,768]{1,0:T(8,128)(2,1)S(1)} %get-tuple-element.17.high, bf16[512,768]{1,0:T(8,128)(2,1)S(1)} %get-tuple-element.18.low, f32[96,1024]{1,0:T(8,128)S(1)} %all_gather.3.refs_0_, ...), custom_call_target="tpu_custom_call" | custom-call | flops 1207959552 | bytes 6291456 | tf_op jit(solution)/shard_map/pallas_call | solution.py:135
  134.4 1.9 %collective-permute-start.7 = (f32[128,1024]{1,0:T(8,128)S(1)}, f32[128,1024]{1,0:T(8,128)S(1)}, u32[]{:S(2)}, u32[]{:S(2)}) collective-permute-start(f32[128,1024]{1,0:T(8,128)S(1)} %get-tuple-element.22), channel_id=1, source_target_pairs={{0,1},{1,0},{2,3},{3,2},{4,5},{5,4},{6,7},{7,6},{8,9},{9,8},{10,11... | collective-permute-start | bytes 1572872 | tf_op jit(solution)/shard_map/ppermute | solution.py:212
  136.4 1.4 shard_map.58
  137.8 0.5 collective-permute-done.7
  138.3 0.1 add.49
  138.3 12.5 %all_to_all.26 = f32[4,32,1024]{2,1,0:T(8,128)S(1)} all-to-all(f32[4,32,1024]{2,1,0:T(8,128)S(1)} %bitcast.11), channel_id=1, replica_groups={{0,8,16,24},{1,9,17,25},{2,10,18,26},{3,11,19,27},{4,12,20,28},{5,13,21..., dimensions={0} | all-to-all | bytes 1048576 | tf_op jit(solution)/shard_map/all_to_all | solution.py:215
  150.8 5.6 %collective-permute-start.8 = (f32[16,1024]{1,0:T(8,128)S(1)}, f32[16,1024]{1,0:T(8,128)S(1)}, u32[]{:S(2)}, u32[]{:S(2)}) collective-permute-start(f32[16,1024]{1,0:T(8,128)S(1)} %slice.9), channel_id=1, source_target_pairs={{0,4},{1,5},{2,6},{3,7},{4,0},{5,1},{6,2},{7,3},{8,12},{9,13},{10,... | collective-permute-start | bytes 196616 | tf_op jit(solution)/shard_map/ppermute | solution.py:217
  156.5 6.8 %collective-permute-done.8 = f32[16,1024]{1,0:T(8,128)S(1)} collective-permute-done((f32[16,1024]{1,0:T(8,128)S(1)}, f32[16,1024]{1,0:T(8,128)S(1)}, u32[]{:S(2)}, u32[]{:S(2)}) %collective-permute-start.8) | collective-permute-done | bytes 65568 | tf_op jit(solution)/shard_map/ppermute | solution.py:217
  163.3 0.1 reshape.82
  163.4 0.1 copy.11
  163.6 0.1 reshape.83
  163.7 0.6 fusion.4
  (9 shorter events, 0.1 us)
Async XLA Ops:
  1.6 30.2 %all-to-all-start = ((f32[32,1,1024]{2,1,0:T(1,128)}), f32[32,1,1024]{2,1,0:T(1,128)S(1)}, u32[]{:S(2)}, u32[]{:S(2)}) async-start(f32[32,1,1024]{2,1,0:T(1,128)} %all_to_all.17), calls=%async_computation | async-start | bytes 262144 | tf_op jit(solution)/shard_map/all_to_all | solution.py:170
  19.7 1.4 copy-start
  21.1 0.7 copy-start.1
  21.7 0.7 copy-start.2
  22.4 4.6 %copy-start.3 = (s32[32]{0:T(128)S(1)}, s32[32]{0:T(128)}, u32[]{:S(2)}) copy-start(s32[32]{0:T(128)} %partner.1) | copy-start | bytes 388
  63.1 66.0 %all-to-all-start.1 = ((f32[32,48,256]{2,1,0:T(8,128)}), f32[32,48,256]{2,1,0:T(8,128)S(1)}, u32[]{:S(2)}, u32[]{:S(2)}) async-start(f32[32,48,256]{2,1,0:T(8,128)} %shard_map.55), calls=%async_computation.1 | async-start | bytes 3145728 | tf_op jit(solution)/shard_map/all_to_all | solution.py:189
  71.3 13.2 %collective-permute-start.3 = (f32[96,1024]{1,0:T(8,128)S(1)}, f32[96,1024]{1,0:T(8,128)S(1)}, u32[]{:S(2)}, u32[]{:S(2)}) collective-permute-start(f32[96,1024]{1,0:T(8,128)S(1)} %all_gather.3.refs_0_), channel_id=1, source_target_pairs={{0,96},{32,128},{64,160},{96,192},{128,224},{160,256},{192,288},{2... | collective-permute-start | bytes 1179656 | tf_op jit(solution)/shard_map/ppermute | solution.py:151
  74.8 14.0 %collective-permute-start = (f32[96,1024]{1,0:T(8,128)S(1)}, f32[96,1024]{1,0:T(8,128)S(1)}, u32[]{:S(2)}, u32[]{:S(2)}) collective-permute-start(f32[96,1024]{1,0:T(8,128)S(1)} %all_gather.3.refs_0_), channel_id=1, source_target_pairs={{0,672},{32,704},{64,736},{96,0},{128,32},{160,64},{192,96},{224,1... | collective-permute-start | bytes 1179656 | tf_op jit(solution)/shard_map/ppermute | solution.py:152
  84.4 12.4 %collective-permute-start.4 = (f32[96,1024]{1,0:T(8,128)S(1)}, f32[96,1024]{1,0:T(8,128)S(1)}, u32[]{:S(2)}, u32[]{:S(2)}) collective-permute-start(f32[96,1024]{1,0:T(8,128)S(1)} %collective-permute-done.3.refs_7_), channel_id=1, source_target_pairs={{0,96},{32,128},{64,160},{96,192},{128,224},{160,256},{192,288},{2... | collective-permute-start | bytes 1179656 | tf_op jit(solution)/shard_map/ppermute | solution.py:151
  88.7 13.6 %collective-permute-start.1 = (f32[96,1024]{1,0:T(8,128)S(1)}, f32[96,1024]{1,0:T(8,128)S(1)}, u32[]{:S(2)}, u32[]{:S(2)}) collective-permute-start(f32[96,1024]{1,0:T(8,128)S(1)} %collective-permute-done.refs_1_), channel_id=1, source_target_pairs={{0,672},{32,704},{64,736},{96,0},{128,32},{160,64},{192,96},{224,1... | collective-permute-start | bytes 1179656 | tf_op jit(solution)/shard_map/ppermute | solution.py:152
  96.8 12.1 %collective-permute-start.5 = (f32[96,1024]{1,0:T(8,128)S(1)}, f32[96,1024]{1,0:T(8,128)}, u32[]{:S(2)}, u32[]{:S(2)}) collective-permute-start(f32[96,1024]{1,0:T(8,128)S(1)} %collective-permute-done.4.refs_6_), channel_id=1, source_target_pairs={{0,96},{32,128},{64,160},{96,192},{128,224},{160,256},{192,288},{2... | collective-permute-start | bytes 1179656 | tf_op jit(solution)/shard_map/ppermute | solution.py:151
  102.3 29.0 %collective-permute-start.2 = (f32[96,1024]{1,0:T(8,128)S(1)}, f32[96,1024]{1,0:T(8,128)}, u32[]{:S(2)}, u32[]{:S(2)}) collective-permute-start(f32[96,1024]{1,0:T(8,128)S(1)} %collective-permute-done.1.refs_2_), channel_id=1, source_target_pairs={{0,672},{32,704},{64,736},{96,0},{128,32},{160,64},{192,96},{224,1... | collective-permute-start | bytes 1179656 | tf_op jit(solution)/shard_map/ppermute | solution.py:152
  108.9 22.5 %collective-permute-start.6 = (f32[96,1024]{1,0:T(8,128)}, f32[96,1024]{1,0:T(8,128)}, u32[]{:S(2)}, u32[]{:S(2)}) collective-permute-start(f32[96,1024]{1,0:T(8,128)} %collective-permute-done.5.refs_5_), channel_id=1, source_target_pairs={{0,96},{32,128},{64,160},{96,192},{128,224},{160,256},{192,288},{2... | collective-permute-start | bytes 1179656 | tf_op jit(solution)/shard_map/ppermute | solution.py:154
  134.4 3.8 %collective-permute-start.7 = (f32[128,1024]{1,0:T(8,128)S(1)}, f32[128,1024]{1,0:T(8,128)S(1)}, u32[]{:S(2)}, u32[]{:S(2)}) collective-permute-start(f32[128,1024]{1,0:T(8,128)S(1)} %get-tuple-element.22), channel_id=1, source_target_pairs={{0,1},{1,0},{2,3},{3,2},{4,5},{5,4},{6,7},{7,6},{8,9},{9,8},{10,11... | collective-permute-start | bytes 1572872 | tf_op jit(solution)/shard_map/ppermute | solution.py:212
  150.8 12.5 %collective-permute-start.8 = (f32[16,1024]{1,0:T(8,128)S(1)}, f32[16,1024]{1,0:T(8,128)S(1)}, u32[]{:S(2)}, u32[]{:S(2)}) collective-permute-start(f32[16,1024]{1,0:T(8,128)S(1)} %slice.9), channel_id=1, source_target_pairs={{0,4},{1,5},{2,6},{3,7},{4,0},{5,1},{6,2},{7,3},{8,12},{9,13},{10,... | collective-permute-start | bytes 196616 | tf_op jit(solution)/shard_map/ppermute | solution.py:217

commit v7 on v6

--- a/solution.py
+++ b/solution.py
@@ -18,20 +18,17 @@
 
 X_GROUPS = [[x * 8 + rest for x in range(NX)] for rest in range(8)]
 CORE_SWAP = [(n, n ^ 1) for n in range(NARROW)]
-Z_FAR = [(n, n ^ 4) for n in range(NARROW)]
-SIX_GROUPS = [
-    [(y * NZL + zl) * NARROW + x * 8 + (pair * 2 + zh) * 2 + c for zh in range(2) for zl in range(NZL)]
-    for y in range(NY)
-    for x in range(NX)
-    for pair in range(2)
-    for c in range(NC)
-]
+Z_NEAR = [(n, n ^ 2) for n in range(NARROW)]
 VMEM = pl.BlockSpec(memory_space=pltpu.VMEM)
 SMEM = pl.BlockSpec(memory_space=pltpu.SMEM)
 
 
 def y_shift(step):
     return [(y * NZL + zl, (y + step) % NY * NZL + zl) for y in range(NY) for zl in range(NZL)]
+
+
+def zl_shift(step):
+    return [(y * NZL + zl, y * NZL + (zl + step) % NZL) for y in range(NY) for zl in range(NZL)]
 
 
 def swap_ij(rows):
@@ -43,17 +40,16 @@
     for x in range(NX):
         for col in range(DEPTH // BW):
             keep = row_irrep[x] == col_irrep[col]
-            values = jnp.where(keep, block[x * BW : (x + 1) * BW, col * BW : (col + 1) * BW], 0.0).T
-            even = [values[:, zh * LR : (zh + 1) * LR] for zh in (0, 2, 1, 3)]
-            turned[col * BW : (col + 1) * BW, :] = jnp.concatenate(even, axis=1)
+            values = jnp.where(keep, block[x * BW : (x + 1) * BW, col * BW : (col + 1) * BW], 0.0)
+            turned[col * BW : (col + 1) * BW, :] = values.T
         lanes = slice(x * BW // 2, (x + 1) * BW // 2)
         for to in range(NARROW):
-            odd = to // 2 % 2
+            upper = to // 4 % 2
             for near in range(2):
                 rows = slice(near * WIDE, (near + 1) * WIDE)
-                column = to & ~2 | near * 2
+                column = to & ~4 | near * 4
                 found = turned[pl.ds(column, WIDE, stride=LR), :]
-                out[to, rows, lanes] = found[:, odd * (BW // 2) : (odd + 1) * (BW // 2)]
+                out[to, rows, lanes] = found[:, upper * (BW // 2) : (upper + 1) * (BW // 2)]
 
 
 def fill_pairs(partner, plus, minus, turned, ranks):
@@ -77,7 +73,7 @@
 
 def split_kernel(place, partner, pieces, high, low, turned, plus, minus, ranks):
     fill_pairs(partner, plus, minus, turned, ranks)
-    far, core = place[0] // 4 % 2, place[0] % 2
+    odd, core = place[0] // 2 % 2, place[0] % 2
     for group in range(DEPTH // BW):
         lanes = slice(group * BW, (group + 1) * BW)
         tile = [pieces[:, near * WIDE + group * 4 + i, :] for i in range(4) for near in range(2)]
@@ -90,7 +86,7 @@
             for away in range(2):
                 for x in range(NX):
                     for across in range(2):
-                        start = x * (BW // 2) + lax.bitwise_xor(far, across) * LR + lax.bitwise_xor(core, away) * OUT
+                        start = x * (BW // 2) + lax.bitwise_xor(odd, across) * LR + lax.bitwise_xor(core, away) * OUT
                         values = turned[pl.ds(pl.multiple_of(start, OUT), OUT), :]
                         upper = values.astype(jnp.bfloat16)
                         to = away * HALF + sign * BW + x * LR + across * OUT
@@ -112,14 +108,13 @@
 
 def first_kernel(place, high, low, *refs):
     blocks, (other, s_high, s_low) = refs[:NY], refs[NY:]
-    y = place[1] // NZL
-    half = NARROW // 2
+    y, zl = place[1] // NZL, lax.rem(place[1], NZL)
     for step, block in enumerate(blocks):
         at = lax.rem(y + step, NY) * (NZL * LR)
-        for zl in range(NZL):
-            to = pl.ds(pl.multiple_of(at + zl * LR, LR), LR)
-            values = [block[(near * NZL + zl) * half : (near * NZL + zl + 1) * half, :] for near in range(2)]
-            values = jnp.concatenate(values, axis=0)
+        for slot in range(NZL):
+            owner = lax.rem(zl + (0, NZL - 1, 1)[slot], NZL)
+            to = pl.ds(pl.multiple_of(at + owner * LR, LR), LR)
+            values = block[slot * LR : (slot + 1) * LR, :]
             top = values.astype(jnp.bfloat16)
             s_high[to, :] = top
             s_low[to, :] = (values - top.astype(jnp.float32)).astype(jnp.bfloat16)
@@ -156,18 +151,21 @@
 
 
 def pairs_of(partner):
-    n = jnp.arange(NARROW, dtype=jnp.int32)
-    first = n < partner
-    before = first[None, :] & (n[None, :] < jnp.minimum(n, partner)[:, None])
-    pair = before.astype(jnp.int32).sum(1)
-    plus = (pair[None, :] == jnp.arange(NARROW // 2, dtype=jnp.int32)[:, None]).astype(jnp.float32)
-    return plus, jnp.where(first[None, :], plus, -plus)
+    m = jnp.arange(NARROW, dtype=jnp.int32)
+    n = jnp.concatenate([m, m])
+    other = jnp.concatenate([partner, partner])
+    before = (m < partner)[None, :] & (m[None, :] < jnp.minimum(n, other)[:, None])
+    pair = before.astype(jnp.int32).sum(1) + jnp.arange(2 * NARROW, dtype=jnp.int32) // NARROW * (NARROW // 2)
+    plus = (pair[None, :] == m[:, None]).astype(jnp.float32)
+    return plus, jnp.where((n < other)[None, :], plus, -plus)
 
 
 def local(integrals, amplitudes, row_irrep, col_irrep, partner):
     place = jnp.stack([lax.axis_index("narrow"), lax.axis_index("wide")]).astype(jnp.int32)
 
-    rows = lax.all_to_all(amplitudes, "narrow", 0, 0, tiled=True)
+    both = amplitudes.reshape(NX, 1, 2, 4, COLS).swapaxes(2, 3)
+    both = jnp.broadcast_to(both, (NX, 2, 4, 2, COLS)).reshape(NARROW, 2, COLS)
+    rows = lax.all_to_all(both, "narrow", 0, 0, tiled=True).swapaxes(0, 1).reshape(2 * NARROW, COLS)
     pieces = call(
         pieces_kernel,
         jax.ShapeDtypeStruct((NARROW, 2 * WIDE, HALF), jnp.float32),
@@ -182,12 +180,13 @@
     swapped = swap_ij(rows)
     even = jnp.dot(plus, rows + swapped, precision=lax.Precision.HIGHEST)
     odd = jnp.dot(minus, rows - swapped, precision=lax.Precision.HIGHEST)
-    packed = 0.5 * jnp.where(upper_triangle((1, COLS)), even, odd)
-
-    block = lax.all_gather(packed, ("wide", "narrow"), axis=0, tiled=True, axis_index_groups=SIX_GROUPS)
-    pieces, block = lax.optimization_barrier((pieces, block))
+    block = 0.5 * jnp.where(upper_triangle((1, COLS)), even, odd)
+
+    before = lax.ppermute(block, "wide", zl_shift(1))
+    after = lax.ppermute(block, "wide", zl_shift(-1))
+    pieces, before, after = lax.optimization_barrier((pieces, before, after))
     pieces = lax.all_to_all(pieces, "narrow", 0, 0, tiled=True)
-    found = gather_y(block)
+    found = gather_y(jnp.concatenate([block, before, after], axis=0))
     high, low = call(
         split_kernel,
         [jax.ShapeDtypeStruct((SLAB, DEPTH), jnp.bfloat16)] * 2,
@@ -214,7 +213,7 @@
     chip = mine + arrived
     over_x = lax.all_to_all(chip, "narrow", 0, 0, tiled=True, axis_index_groups=X_GROUPS)
     reduced = over_x.reshape(NX, 2 * OUT, COLS).sum(0)
-    result = reduced[:OUT] + lax.ppermute(reduced[OUT:], "narrow", Z_FAR)
+    result = reduced[:OUT] + lax.ppermute(reduced[OUT:], "narrow", Z_NEAR)
     turned = swap_ij(result)
     column = jnp.arange(COLS, dtype=jnp.int32)[None, :]
     i, j = column // NO, column % NO

time: 165 us -> 147 us (0.89)
  the two profiles are of different devices: /device:TPU:16 before, /device:TPU:112 now
where the time goes in v7:
time: 147 us
  waiting for transfers between devices  63.1 us (43%)
  starting transfers between devices  51.3 us (35%)
  blocking collectives  12.5 us (9%)
  Pallas kernels  11.5 us (8%)
  local copies, waits for them, and re-layouts  5.72 us (4%)
  other arithmetic  1.88 us (1%)
    all_to_all x1, waiting for transfers between devices, local(): pieces = lax.all_to_all(pieces, 'narrow', 0, 0, tiled=True)  20.6 us
    ppermute x3, waiting for transfers between devices, gather_y(): up = lax.ppermute(up, 'wide', y_shift(1))  20.1 us
    all_to_all x1, starting transfers between devices, local(): lax.all_to_all(both, 'narrow', 0, 0, tiled=True).swapaxes(0, 1)  16.5 us
    all_to_all x1, blocking collectives, local(): lax.all_to_all(chip, 'narrow', 0, 0, tiled=True, axis_index_groups=X_GROUPS)  12.5 us
    pallas_call x4, Pallas kernels, call(): pl.pallas_call(kernel, out_shape=outs, in_specs=in_specs, out_specs=[VMEM...  11.5 us
    ppermute x3, starting transfers between devices, gather_y(): down = lax.ppermute(down, 'wide', y_shift(-1))  9.93 us
    all_to_all x1, waiting for transfers between devices, local(): lax.all_to_all(both, 'narrow', 0, 0, tiled=True).swapaxes(0, 1)  9.88 us
    ppermute x3, starting transfers between devices, gather_y(): up = lax.ppermute(up, 'wide', y_shift(1))  7.74 us
  transfers between devices with their start and end apart: 13, of which 9 were waited for; matrix products, arithmetic and copies ran while one was open for 1% of the time, Pallas kernels for 6%

profile of v7, /device:TPU:112, one launch (start us, length us, event | category | flops | bytes accessed | tf_op | source)
XLA Modules:
  0.0 146.7 jit_solution(13517813679731883158)
XLA Ops:
  0.0 0.9 reshape.148
  0.9 0.1 copy.22
  1.1 0.8 broadcast_in_dim.45
  1.8 16.5 %all-to-all-start = ((f32[32,2,1024]{2,1,0:T(2,128)}), f32[32,2,1024]{2,1,0:T(2,128)S(1)}, u32[]{:S(2)}, u32[]{:S(2)}) async-start(f32[32,2,1024]{2,1,0:T(2,128)} %bitcast.4), calls=%async_computation | async-start | bytes 524288 | tf_op jit(solution)/shard_map/all_to_all | solution.py:168
  18.3 0.8 fusion.23
  19.1 1.4 copy-done
  20.5 0.7 copy-done.1
  21.2 0.7 copy-done.2
  21.9 4.8 %shard_map.55 = f32[32,48,256]{2,1,0:T(8,128)} custom-call(s32[4]{0:T(128)S(1)} %copy-done.1, s32[6]{0:T(128)S(1)} %copy-done.2, f32[512,768]{1,0:T(8,128)S(1)} %copy-done), custom_call_target="tpu_custom_call" | custom-call | bytes 3145728 | tf_op jit(solution)/shard_map/pallas_call | solution.py:130
  26.7 0.1 fusion.22
  26.8 0.1 convert_reduce_fusion
  26.9 9.9 %all-to-all-done = f32[32,2,1024]{2,1,0:T(2,128)S(1)} async-done(((f32[32,2,1024]{2,1,0:T(2,128)}), f32[32,2,1024]{2,1,0:T(2,128)S(1)}, u32[]{:S(2)}, u32[]{:S(2)}) %all-to-all-start) | async-done | bytes 262176 | tf_op jit(solution)/shard_map/all_to_all | solution.py:168
  36.8 0.1 copy.23
  36.9 0.2 copy.24
  37.1 0.3 copy.25
  37.4 0.2 copy.26
  37.6 0.2 fusion.2
  37.8 0.3 fusion
  38.1 3.0 %collective-permute-start = (f32[32,1024]{1,0:T(8,128)S(1)}, f32[32,1024]{1,0:T(8,128)S(1)}, u32[]{:S(2)}, u32[]{:S(2)}) collective-permute-start(f32[32,1024]{1,0:T(8,128)S(1)} %fusion), channel_id=1, source_target_pairs={{0,32},{32,64},{64,0},{96,128},{128,160},{160,96},{192,224},{224,2... | collective-permute-start | bytes 393224 | tf_op jit(solution)/shard_map/ppermute | solution.py:185
  41.0 2.9 %collective-permute-start.1 = (f32[32,1024]{1,0:T(8,128)S(1)}, f32[32,1024]{1,0:T(8,128)S(1)}, u32[]{:S(2)}, u32[]{:S(2)}) collective-permute-start(f32[32,1024]{1,0:T(8,128)S(1)} %fusion), channel_id=1, source_target_pairs={{0,64},{32,0},{64,32},{96,160},{128,96},{160,128},{192,256},{224,1... | collective-permute-start | bytes 393224 | tf_op jit(solution)/shard_map/ppermute | solution.py:186
  44.0 2.1 %collective-permute-done = f32[32,1024]{1,0:T(8,128)S(1)} collective-permute-done((f32[32,1024]{1,0:T(8,128)S(1)}, f32[32,1024]{1,0:T(8,128)S(1)}, u32[]{:S(2)}, u32[]{:S(2)}) %collective-permute-start) | collective-permute-done | bytes 131104 | tf_op jit(solution)/shard_map/ppermute | solution.py:185
  46.1 2.4 %collective-permute-done.1 = f32[32,1024]{1,0:T(8,128)S(1)} collective-permute-done((f32[32,1024]{1,0:T(8,128)S(1)}, f32[32,1024]{1,0:T(8,128)S(1)}, u32[]{:S(2)}, u32[]{:S(2)}) %collective-permute-start.1) | collective-permute-done | bytes 131104 | tf_op jit(solution)/shard_map/ppermute | solution.py:186
  48.5 4.8 %all-to-all-start.1 = ((f32[32,48,256]{2,1,0:T(8,128)}), f32[32,48,256]{2,1,0:T(8,128)S(1)}, u32[]{:S(2)}, u32[]{:S(2)}) async-start(f32[32,48,256]{2,1,0:T(8,128)} %shard_map.55), calls=%async_computation.1 | async-start | bytes 3145728 | tf_op jit(solution)/shard_map/all_to_all | solution.py:188
  53.3 2.6 %collective-permute-start.5 = (f32[96,1024]{1,0:T(8,128)S(1)}, f32[96,1024]{1,0:T(8,128)S(1)}, u32[]{:S(2)}, u32[]{:S(2)}) collective-permute-start(f32[96,1024]{1,0:T(8,128)S(1)} %pad_maximum_fusion.refs_0_), channel_id=1, source_target_pairs={{0,96},{32,128},{64,160},{96,192},{128,224},{160,256},{192,288},{2... | collective-permute-start | bytes 1179656 | tf_op jit(solution)/shard_map/ppermute | solution.py:146
  55.9 3.3 %collective-permute-start.2 = (f32[96,1024]{1,0:T(8,128)S(1)}, f32[96,1024]{1,0:T(8,128)S(1)}, u32[]{:S(2)}, u32[]{:S(2)}) collective-permute-start(f32[96,1024]{1,0:T(8,128)S(1)} %pad_maximum_fusion.refs_0_), channel_id=1, source_target_pairs={{0,672},{32,704},{64,736},{96,0},{128,32},{160,64},{192,96},{224,1... | collective-permute-start | bytes 1179656 | tf_op jit(solution)/shard_map/ppermute | solution.py:147
  59.2 7.3 %collective-permute-done.5.refs_7_ = f32[96,1024]{1,0:T(8,128)S(1)} collective-permute-done((f32[96,1024]{1,0:T(8,128)S(1)}, f32[96,1024]{1,0:T(8,128)S(1)}, u32[]{:S(2)}, u32[]{:S(2)}) %collective-permute-start.5) | collective-permute-done | bytes 393248 | tf_op jit(solution)/shard_map/ppermute | solution.py:146
  66.5 2.6 %collective-permute-start.6 = (f32[96,1024]{1,0:T(8,128)S(1)}, f32[96,1024]{1,0:T(8,128)S(1)}, u32[]{:S(2)}, u32[]{:S(2)}) collective-permute-start(f32[96,1024]{1,0:T(8,128)S(1)} %collective-permute-done.5.refs_7_), channel_id=1, source_target_pairs={{0,96},{32,128},{64,160},{96,192},{128,224},{160,256},{192,288},{2... | collective-permute-start | bytes 1179656 | tf_op jit(solution)/shard_map/ppermute | solution.py:146
  69.1 3.3 %collective-permute-start.3 = (f32[96,1024]{1,0:T(8,128)S(1)}, f32[96,1024]{1,0:T(8,128)S(1)}, u32[]{:S(2)}, u32[]{:S(2)}) collective-permute-start(f32[96,1024]{1,0:T(8,128)S(1)} %collective-permute-done.2.refs_1_), channel_id=1, source_target_pairs={{0,672},{32,704},{64,736},{96,0},{128,32},{160,64},{192,96},{224,1... | collective-permute-start | bytes 1179656 | tf_op jit(solution)/shard_map/ppermute | solution.py:147
  72.4 6.5 %collective-permute-done.6.refs_6_ = f32[96,1024]{1,0:T(8,128)S(1)} collective-permute-done((f32[96,1024]{1,0:T(8,128)S(1)}, f32[96,1024]{1,0:T(8,128)S(1)}, u32[]{:S(2)}, u32[]{:S(2)}) %collective-permute-start.6) | collective-permute-done | bytes 393248 | tf_op jit(solution)/shard_map/ppermute | solution.py:146
  78.9 2.6 %collective-permute-start.7 = (f32[96,1024]{1,0:T(8,128)S(1)}, f32[96,1024]{1,0:T(8,128)}, u32[]{:S(2)}, u32[]{:S(2)}) collective-permute-start(f32[96,1024]{1,0:T(8,128)S(1)} %collective-permute-done.6.refs_6_), channel_id=1, source_target_pairs={{0,96},{32,128},{64,160},{96,192},{128,224},{160,256},{192,288},{2... | collective-permute-start | bytes 1179656 | tf_op jit(solution)/shard_map/ppermute | solution.py:146
  81.5 3.4 %collective-permute-start.4 = (f32[96,1024]{1,0:T(8,128)S(1)}, f32[96,1024]{1,0:T(8,128)}, u32[]{:S(2)}, u32[]{:S(2)}) collective-permute-start(f32[96,1024]{1,0:T(8,128)S(1)} %collective-permute-done.3.refs_2_), channel_id=1, source_target_pairs={{0,672},{32,704},{64,736},{96,0},{128,32},{160,64},{192,96},{224,1... | collective-permute-start | bytes 1179656 | tf_op jit(solution)/shard_map/ppermute | solution.py:147
  84.9 6.3 %collective-permute-done.7.refs_5_ = f32[96,1024]{1,0:T(8,128)} collective-permute-done((f32[96,1024]{1,0:T(8,128)S(1)}, f32[96,1024]{1,0:T(8,128)}, u32[]{:S(2)}, u32[]{:S(2)}) %collective-permute-start.7) | collective-permute-done | bytes 393248 | tf_op jit(solution)/shard_map/ppermute | solution.py:146
  91.2 2.6 %collective-permute-start.8 = (f32[96,1024]{1,0:T(8,128)}, f32[96,1024]{1,0:T(8,128)}, u32[]{:S(2)}, u32[]{:S(2)}) collective-permute-start(f32[96,1024]{1,0:T(8,128)} %collective-permute-done.7.refs_5_), channel_id=1, source_target_pairs={{0,96},{32,128},{64,160},{96,192},{128,224},{160,256},{192,288},{2... | collective-permute-start | bytes 1179656 | tf_op jit(solution)/shard_map/ppermute | solution.py:149
  93.8 0.1 pad_add_fusion.place
  93.9 20.6 %all-to-all-done.1.pieces = f32[32,48,256]{2,1,0:T(8,128)S(1)} async-done(((f32[32,48,256]{2,1,0:T(8,128)}), f32[32,48,256]{2,1,0:T(8,128)S(1)}, u32[]{:S(2)}, u32[]{:S(2)}) %all-to-all-start.1) | async-done | bytes 1572896 | tf_op jit(solution)/shard_map/all_to_all | solution.py:188
  114.5 2.2 %shard_map.56 = (bf16[512,768]{1,0:T(8,128)(2,1)S(1)}, bf16[512,768]{1,0:T(8,128)(2,1)S(1)}) custom-call(s32[2]{0:T(128)S(1)} %pad_add_fusion.place, s32[32]{0:T(128)S(1)} %copy-done.3, f32[32,48,256]{2,1,0:T(8,128)S(1)} %all-to-all-done.1.pieces), custom_call_target="tpu_custom_call" | custom-call | bytes 3145728 | tf_op jit(solution)/shard_map/pallas_call | solution.py:130
  116.7 3.1 %shard_map.57 = (f32[128,1024]{1,0:T(8,128)S(1)}, bf16[768,1024]{1,0:T(8,128)(2,1)S(1)}, bf16[768,1024]{1,0:T(8,128)(2,1)S(1)}) custom-call(s32[2]{0:T(128)S(1)} %pad_add_fusion.place, bf16[512,768]{1,0:T(8,128)(2,1)S(1)} %get-tuple-element.18.high, bf16[512,768]{1,0:T(8,128)(2,1)S(1)} %get-tuple-element.19.low, f32[96,1024]{1,0:T(8,128)S(1)} %pad_maximum_fusion.refs_0_, ...), custom_call_target="tpu_custom_call" | custom-call | flops 1207959552 | bytes 6291456 | tf_op jit(solution)/shard_map/pallas_call | solution.py:130
  119.8 1.9 %collective-permute-start.9 = (f32[128,1024]{1,0:T(8,128)S(1)}, f32[128,1024]{1,0:T(8,128)S(1)}, u32[]{:S(2)}, u32[]{:S(2)}) collective-permute-start(f32[128,1024]{1,0:T(8,128)S(1)} %get-tuple-element.24), channel_id=1, source_target_pairs={{0,1},{1,0},{2,3},{3,2},{4,5},{5,4},{6,7},{7,6},{8,9},{9,8},{10,11... | collective-permute-start | bytes 1572872 | tf_op jit(solution)/shard_map/ppermute | solution.py:211
  121.7 1.4 shard_map.58
  123.1 0.5 collective-permute-done.9
  123.6 0.1 add.62
  123.7 12.5 %all_to_all.19 = f32[4,32,1024]{2,1,0:T(8,128)S(1)} all-to-all(f32[4,32,1024]{2,1,0:T(8,128)S(1)} %bitcast.18), channel_id=1, replica_groups={{0,8,16,24},{1,9,17,25},{2,10,18,26},{3,11,19,27},{4,12,20,28},{5,13,21..., dimensions={0} | all-to-all | bytes 1048576 | tf_op jit(solution)/shard_map/all_to_all | solution.py:214
  136.2 1.9 %collective-permute-start.10 = (f32[16,1024]{1,0:T(8,128)S(1)}, f32[16,1024]{1,0:T(8,128)S(1)}, u32[]{:S(2)}, u32[]{:S(2)}) collective-permute-start(f32[16,1024]{1,0:T(8,128)S(1)} %slice.9), channel_id=1, source_target_pairs={{0,2},{1,3},{2,0},{3,1},{4,6},{5,7},{6,4},{7,5},{8,10},{9,11},{10,... | collective-permute-start | bytes 196616 | tf_op jit(solution)/shard_map/ppermute | solution.py:216
  138.1 7.5 %collective-permute-done.10 = f32[16,1024]{1,0:T(8,128)S(1)} collective-permute-done((f32[16,1024]{1,0:T(8,128)S(1)}, f32[16,1024]{1,0:T(8,128)S(1)}, u32[]{:S(2)}, u32[]{:S(2)}) %collective-permute-start.10) | collective-permute-done | bytes 65568 | tf_op jit(solution)/shard_map/ppermute | solution.py:216
  145.6 0.1 reshape.153
  145.8 0.1 copy.28
  145.9 0.1 reshape.154
  146.0 0.6 fusion.4
  (18 shorter events, 0.1 us)
Async XLA Ops:
  1.8 34.9 %all-to-all-start = ((f32[32,2,1024]{2,1,0:T(2,128)}), f32[32,2,1024]{2,1,0:T(2,128)S(1)}, u32[]{:S(2)}, u32[]{:S(2)}) async-start(f32[32,2,1024]{2,1,0:T(2,128)} %bitcast.4), calls=%async_computation | async-start | bytes 524288 | tf_op jit(solution)/shard_map/all_to_all | solution.py:168
  19.1 1.4 copy-start
  20.5 0.7 copy-start.1
  21.2 0.7 copy-start.2
  21.9 4.8 %copy-start.3 = (s32[32]{0:T(128)S(1)}, s32[32]{0:T(128)}, u32[]{:S(2)}) copy-start(s32[32]{0:T(128)} %partner.1) | copy-start | bytes 388
  38.1 8.0 %collective-permute-start = (f32[32,1024]{1,0:T(8,128)S(1)}, f32[32,1024]{1,0:T(8,128)S(1)}, u32[]{:S(2)}, u32[]{:S(2)}) collective-permute-start(f32[32,1024]{1,0:T(8,128)S(1)} %fusion), channel_id=1, source_target_pairs={{0,32},{32,64},{64,0},{96,128},{128,160},{160,96},{192,224},{224,2... | collective-permute-start | bytes 393224 | tf_op jit(solution)/shard_map/ppermute | solution.py:185
  41.0 7.5 %collective-permute-start.1 = (f32[32,1024]{1,0:T(8,128)S(1)}, f32[32,1024]{1,0:T(8,128)S(1)}, u32[]{:S(2)}, u32[]{:S(2)}) collective-permute-start(f32[32,1024]{1,0:T(8,128)S(1)} %fusion), channel_id=1, source_target_pairs={{0,64},{32,0},{64,32},{96,160},{128,96},{160,128},{192,256},{224,1... | collective-permute-start | bytes 393224 | tf_op jit(solution)/shard_map/ppermute | solution.py:186
  48.5 66.0 %all-to-all-start.1 = ((f32[32,48,256]{2,1,0:T(8,128)}), f32[32,48,256]{2,1,0:T(8,128)S(1)}, u32[]{:S(2)}, u32[]{:S(2)}) async-start(f32[32,48,256]{2,1,0:T(8,128)} %shard_map.55), calls=%async_computation.1 | async-start | bytes 3145728 | tf_op jit(solution)/shard_map/all_to_all | solution.py:188
  53.3 13.2 %collective-permute-start.5 = (f32[96,1024]{1,0:T(8,128)S(1)}, f32[96,1024]{1,0:T(8,128)S(1)}, u32[]{:S(2)}, u32[]{:S(2)}) collective-permute-start(f32[96,1024]{1,0:T(8,128)S(1)} %pad_maximum_fusion.refs_0_), channel_id=1, source_target_pairs={{0,96},{32,128},{64,160},{96,192},{128,224},{160,256},{192,288},{2... | collective-permute-start | bytes 1179656 | tf_op jit(solution)/shard_map/ppermute | solution.py:146
  55.9 13.2 %collective-permute-start.2 = (f32[96,1024]{1,0:T(8,128)S(1)}, f32[96,1024]{1,0:T(8,128)S(1)}, u32[]{:S(2)}, u32[]{:S(2)}) collective-permute-start(f32[96,1024]{1,0:T(8,128)S(1)} %pad_maximum_fusion.refs_0_), channel_id=1, source_target_pairs={{0,672},{32,704},{64,736},{96,0},{128,32},{160,64},{192,96},{224,1... | collective-permute-start | bytes 1179656 | tf_op jit(solution)/shard_map/ppermute | solution.py:147
  66.5 12.4 %collective-permute-start.6 = (f32[96,1024]{1,0:T(8,128)S(1)}, f32[96,1024]{1,0:T(8,128)S(1)}, u32[]{:S(2)}, u32[]{:S(2)}) collective-permute-start(f32[96,1024]{1,0:T(8,128)S(1)} %collective-permute-done.5.refs_7_), channel_id=1, source_target_pairs={{0,96},{32,128},{64,160},{96,192},{128,224},{160,256},{192,288},{2... | collective-permute-start | bytes 1179656 | tf_op jit(solution)/shard_map/ppermute | solution.py:146
  69.1 12.4 %collective-permute-start.3 = (f32[96,1024]{1,0:T(8,128)S(1)}, f32[96,1024]{1,0:T(8,128)S(1)}, u32[]{:S(2)}, u32[]{:S(2)}) collective-permute-start(f32[96,1024]{1,0:T(8,128)S(1)} %collective-permute-done.2.refs_1_), channel_id=1, source_target_pairs={{0,672},{32,704},{64,736},{96,0},{128,32},{160,64},{192,96},{224,1... | collective-permute-start | bytes 1179656 | tf_op jit(solution)/shard_map/ppermute | solution.py:147
  78.9 12.3 %collective-permute-start.7 = (f32[96,1024]{1,0:T(8,128)S(1)}, f32[96,1024]{1,0:T(8,128)}, u32[]{:S(2)}, u32[]{:S(2)}) collective-permute-start(f32[96,1024]{1,0:T(8,128)S(1)} %collective-permute-done.6.refs_6_), channel_id=1, source_target_pairs={{0,96},{32,128},{64,160},{96,192},{128,224},{160,256},{192,288},{2... | collective-permute-start | bytes 1179656 | tf_op jit(solution)/shard_map/ppermute | solution.py:146
  81.5 35.2 %collective-permute-start.4 = (f32[96,1024]{1,0:T(8,128)S(1)}, f32[96,1024]{1,0:T(8,128)}, u32[]{:S(2)}, u32[]{:S(2)}) collective-permute-start(f32[96,1024]{1,0:T(8,128)S(1)} %collective-permute-done.3.refs_2_), channel_id=1, source_target_pairs={{0,672},{32,704},{64,736},{96,0},{128,32},{160,64},{192,96},{224,1... | collective-permute-start | bytes 1179656 | tf_op jit(solution)/shard_map/ppermute | solution.py:147
  91.2 25.5 %collective-permute-start.8 = (f32[96,1024]{1,0:T(8,128)}, f32[96,1024]{1,0:T(8,128)}, u32[]{:S(2)}, u32[]{:S(2)}) collective-permute-start(f32[96,1024]{1,0:T(8,128)} %collective-permute-done.7.refs_5_), channel_id=1, source_target_pairs={{0,96},{32,128},{64,160},{96,192},{128,224},{160,256},{192,288},{2... | collective-permute-start | bytes 1179656 | tf_op jit(solution)/shard_map/ppermute | solution.py:149
  119.8 3.8 %collective-permute-start.9 = (f32[128,1024]{1,0:T(8,128)S(1)}, f32[128,1024]{1,0:T(8,128)S(1)}, u32[]{:S(2)}, u32[]{:S(2)}) collective-permute-start(f32[128,1024]{1,0:T(8,128)S(1)} %get-tuple-element.24), channel_id=1, source_target_pairs={{0,1},{1,0},{2,3},{3,2},{4,5},{5,4},{6,7},{7,6},{8,9},{9,8},{10,11... | collective-permute-start | bytes 1572872 | tf_op jit(solution)/shard_map/ppermute | solution.py:211
  136.2 9.4 %collective-permute-start.10 = (f32[16,1024]{1,0:T(8,128)S(1)}, f32[16,1024]{1,0:T(8,128)S(1)}, u32[]{:S(2)}, u32[]{:S(2)}) collective-permute-start(f32[16,1024]{1,0:T(8,128)S(1)} %slice.9), channel_id=1, source_target_pairs={{0,2},{1,3},{2,0},{3,1},{4,6},{5,7},{6,4},{7,5},{8,10},{9,11},{10,... | collective-permute-start | bytes 196616 | tf_op jit(solution)/shard_map/ppermute | solution.py:216

commit v8 on v7

--- a/solution.py
+++ b/solution.py
@@ -36,7 +36,7 @@
     return jnp.swapaxes(rows.reshape(count, NO, NO), 1, 2).reshape(count, cols)
 
 
-def pieces_kernel(row_irrep, col_irrep, block, out, turned):
+def pieces_kernel(place, row_irrep, col_irrep, block, out, turned):
     for x in range(NX):
         for col in range(DEPTH // BW):
             keep = row_irrep[x] == col_irrep[col]
@@ -48,7 +48,7 @@
             for near in range(2):
                 rows = slice(near * WIDE, (near + 1) * WIDE)
                 column = to & ~4 | near * 4
-                found = turned[pl.ds(column, WIDE, stride=LR), :]
+                found = turned[pl.ds(place[2] + column, WIDE, stride=LR), :]
                 out[to, rows, lanes] = found[:, upper * (BW // 2) : (upper + 1) * (BW // 2)]
 
 
@@ -106,8 +106,8 @@
     return jnp.where(upper_triangle((BW, COLS)), total[:BW], total[BW:])
 
 
-def first_kernel(place, high, low, *refs):
-    blocks, (other, s_high, s_low) = refs[:NY], refs[NY:]
+def parts_kernel(place, *refs):
+    blocks, (s_high, s_low) = refs[:NY], refs[NY:]
     y, zl = place[1] // NZL, lax.rem(place[1], NZL)
     for step, block in enumerate(blocks):
         at = lax.rem(y + step, NY) * (NZL * LR)
@@ -118,6 +118,9 @@
             top = values.astype(jnp.bfloat16)
             s_high[to, :] = top
             s_low[to, :] = (values - top.astype(jnp.float32)).astype(jnp.bfloat16)
+
+
+def first_kernel(high, low, s_high, s_low, other):
     other[...] = three_pass(high, low, s_high, s_low, slice(HALF, SLAB))
 
 
@@ -161,7 +164,7 @@
 
 
 def local(integrals, amplitudes, row_irrep, col_irrep, partner):
-    place = jnp.stack([lax.axis_index("narrow"), lax.axis_index("wide")]).astype(jnp.int32)
+    place = jnp.stack([lax.axis_index("narrow"), lax.axis_index("wide"), 0]).astype(jnp.int32)
 
     both = amplitudes.reshape(NX, 1, 2, 4, COLS).swapaxes(2, 3)
     both = jnp.broadcast_to(both, (NX, 2, 4, 2, COLS)).reshape(NARROW, 2, COLS)
@@ -169,8 +172,8 @@
     pieces = call(
         pieces_kernel,
         jax.ShapeDtypeStruct((NARROW, 2 * WIDE, HALF), jnp.float32),
-        [SMEM, SMEM, VMEM],
-        (row_irrep, col_irrep, integrals),
+        [SMEM, SMEM, SMEM, VMEM],
+        (place, row_irrep, col_irrep, integrals),
         0,
         3 << 20,
         [pltpu.VMEM((DEPTH, BW), jnp.float32)],
@@ -187,6 +190,15 @@
     pieces, before, after = lax.optimization_barrier((pieces, before, after))
     pieces = lax.all_to_all(pieces, "narrow", 0, 0, tiled=True)
     found = gather_y(jnp.concatenate([block, before, after], axis=0))
+    s_high, s_low = call(
+        parts_kernel,
+        [jax.ShapeDtypeStruct((DEPTH, COLS), jnp.bfloat16)] * 2,
+        [SMEM] + [VMEM] * NY,
+        (place, *found),
+        0,
+        6 << 20,
+    )
+    pieces, s_high, s_low = lax.optimization_barrier((pieces, s_high, s_low))
     high, low = call(
         split_kernel,
         [jax.ShapeDtypeStruct((SLAB, DEPTH), jnp.bfloat16)] * 2,
@@ -200,14 +212,7 @@
 
     product = jax.ShapeDtypeStruct((BW, COLS), jnp.float32)
     flops = 6 * HALF * DEPTH * COLS
-    theirs, s_high, s_low = call(
-        first_kernel,
-        [product] + [jax.ShapeDtypeStruct((DEPTH, COLS), jnp.bfloat16)] * 2,
-        [SMEM] + [VMEM] * (2 + NY),
-        (place, high, low, *found),
-        flops,
-        6 << 20,
-    )
+    theirs = call(first_kernel, product, [VMEM] * 4, (high, low, s_high, s_low), flops, 6 << 20)
     arrived = lax.ppermute(theirs, "narrow", CORE_SWAP)
     mine = call(second_kernel, product, [VMEM] * 4, (high, low, s_high, s_low), flops, 6 << 20)
     chip = mine + arrived

time: 147 us -> 146 us (level)
  the two profiles are of different devices: /device:TPU:112 before, /device:TPU:104 now
where the time goes in v8:
time: 146 us; the launch traced here: 145 us
  waiting for transfers between devices  59.9 us (41%)
  starting transfers between devices  51.9 us (36%)
  blocking collectives  12.5 us (9%)
  Pallas kernels  11.2 us (8%)
  local copies, waits for them, and re-layouts  6.85 us (5%)
  other arithmetic  1.85 us (1%)
    ppermute x3, waiting for transfers between devices, gather_y(): up = lax.ppermute(up, 'wide', y_shift(1))  20 us
    all_to_all x1, starting transfers between devices, local(): lax.all_to_all(both, 'narrow', 0, 0, tiled=True).swapaxes(0, 1)  16.5 us
    all_to_all x1, blocking collectives, local(): lax.all_to_all(chip, 'narrow', 0, 0, tiled=True, axis_index_groups=X_GROUPS)  12.5 us
    ppermute x3, starting transfers between devices, gather_y(): down = lax.ppermute(down, 'wide', y_shift(-1))  11.9 us
    pallas_call x5, Pallas kernels, call(): pl.pallas_call(kernel, out_shape=outs, in_specs=in_specs, out_specs=[VMEM...  11.2 us
    ppermute x1, waiting for transfers between devices, gather_y(): found[4] = lax.ppermute(up, 'wide', y_shift(1))  9.8 us
    all_to_all x1, waiting for transfers between devices, local(): lax.all_to_all(both, 'narrow', 0, 0, tiled=True).swapaxes(0, 1)  9.3 us
    all_to_all x1, waiting for transfers between devices, local(): pieces = lax.all_to_all(pieces, 'narrow', 0, 0, tiled=True)  8.31 us
  transfers between devices with their start and end apart: 13, of which 10 were waited for; matrix products, arithmetic and copies ran while one was open for 1% of the time, Pallas kernels for 5%

profile of v8, /device:TPU:104, one launch (start us, length us, event | category | flops | bytes accessed | tf_op | source)
XLA Modules:
  0.0 144.9 jit_solution(16768891245621987490)
XLA Ops:
  0.0 0.9 reshape.148
  0.9 0.1 copy.22
  1.1 0.8 broadcast_in_dim.45
  1.8 16.5 %all-to-all-start = ((f32[32,2,1024]{2,1,0:T(2,128)}), f32[32,2,1024]{2,1,0:T(2,128)S(1)}, u32[]{:S(2)}, u32[]{:S(2)}) async-start(f32[32,2,1024]{2,1,0:T(2,128)} %bitcast.4), calls=%async_computation | async-start | bytes 524288 | tf_op jit(solution)/shard_map/all_to_all | solution.py:171
  18.3 0.8 fusion.23
  19.2 1.4 copy-done.2
  20.6 0.7 copy-done.3
  21.3 0.7 copy-done.4
  21.9 5.3 %shard_map.55 = f32[32,48,256]{2,1,0:T(8,128)} custom-call(s32[3]{0:T(128)S(1)} %pad_add_fusion.place, s32[4]{0:T(128)S(1)} %copy-done.3, s32[6]{0:T(128)S(1)} %copy-done.4, f32[512,768]{1,0:T(8,128)S(1)} %copy-done.2), custom_call_target="tpu_custom_call" | custom-call | bytes 3145728 | tf_op jit(solution)/shard_map/pallas_call | solution.py:133
  27.3 0.1 convert_reduce_fusion
  27.4 9.3 %all-to-all-done = f32[32,2,1024]{2,1,0:T(2,128)S(1)} async-done(((f32[32,2,1024]{2,1,0:T(2,128)}), f32[32,2,1024]{2,1,0:T(2,128)S(1)}, u32[]{:S(2)}, u32[]{:S(2)}) %all-to-all-start) | async-done | bytes 262176 | tf_op jit(solution)/shard_map/all_to_all | solution.py:171
  36.8 0.1 copy.23
  36.8 0.2 copy.24
  37.0 0.3 copy.25
  37.4 0.2 copy.26
  37.5 0.2 fusion.2
  37.8 0.3 fusion
  38.1 3.0 %collective-permute-start = (f32[32,1024]{1,0:T(8,128)S(1)}, f32[32,1024]{1,0:T(8,128)S(1)}, u32[]{:S(2)}, u32[]{:S(2)}) collective-permute-start(f32[32,1024]{1,0:T(8,128)S(1)} %fusion), channel_id=1, source_target_pairs={{0,32},{32,64},{64,0},{96,128},{128,160},{160,96},{192,224},{224,2... | collective-permute-start | bytes 393224 | tf_op jit(solution)/shard_map/ppermute | solution.py:188
  41.0 2.9 %collective-permute-start.1 = (f32[32,1024]{1,0:T(8,128)S(1)}, f32[32,1024]{1,0:T(8,128)S(1)}, u32[]{:S(2)}, u32[]{:S(2)}) collective-permute-start(f32[32,1024]{1,0:T(8,128)S(1)} %fusion), channel_id=1, source_target_pairs={{0,64},{32,0},{64,32},{96,160},{128,96},{160,128},{192,256},{224,1... | collective-permute-start | bytes 393224 | tf_op jit(solution)/shard_map/ppermute | solution.py:189
  44.0 2.1 %collective-permute-done = f32[32,1024]{1,0:T(8,128)S(1)} collective-permute-done((f32[32,1024]{1,0:T(8,128)S(1)}, f32[32,1024]{1,0:T(8,128)S(1)}, u32[]{:S(2)}, u32[]{:S(2)}) %collective-permute-start) | collective-permute-done | bytes 131104 | tf_op jit(solution)/shard_map/ppermute | solution.py:188
  46.0 2.4 %collective-permute-done.1 = f32[32,1024]{1,0:T(8,128)S(1)} collective-permute-done((f32[32,1024]{1,0:T(8,128)S(1)}, f32[32,1024]{1,0:T(8,128)S(1)}, u32[]{:S(2)}, u32[]{:S(2)}) %collective-permute-start.1) | collective-permute-done | bytes 131104 | tf_op jit(solution)/shard_map/ppermute | solution.py:189
  48.5 4.8 %all-to-all-start.1 = ((f32[32,48,256]{2,1,0:T(8,128)}), f32[32,48,256]{2,1,0:T(8,128)S(1)}, u32[]{:S(2)}, u32[]{:S(2)}) async-start(f32[32,48,256]{2,1,0:T(8,128)} %shard_map.55), calls=%async_computation.1 | async-start | bytes 3145728 | tf_op jit(solution)/shard_map/all_to_all | solution.py:191
  53.3 2.6 %collective-permute-start.5 = (f32[96,1024]{1,0:T(8,128)S(1)}, f32[96,1024]{1,0:T(8,128)S(1)}, u32[]{:S(2)}, u32[]{:S(2)}) collective-permute-start(f32[96,1024]{1,0:T(8,128)S(1)} %pad_maximum_fusion.refs_0_), channel_id=1, source_target_pairs={{0,96},{32,128},{64,160},{96,192},{128,224},{160,256},{192,288},{2... | collective-permute-start | bytes 1179656 | tf_op jit(solution)/shard_map/ppermute | solution.py:149
  55.9 3.3 %collective-permute-start.2 = (f32[96,1024]{1,0:T(8,128)S(1)}, f32[96,1024]{1,0:T(8,128)S(1)}, u32[]{:S(2)}, u32[]{:S(2)}) collective-permute-start(f32[96,1024]{1,0:T(8,128)S(1)} %pad_maximum_fusion.refs_0_), channel_id=1, source_target_pairs={{0,672},{32,704},{64,736},{96,0},{128,32},{160,64},{192,96},{224,1... | collective-permute-start | bytes 1179656 | tf_op jit(solution)/shard_map/ppermute | solution.py:150
  59.2 7.3 %collective-permute-done.5.refs_7_ = f32[96,1024]{1,0:T(8,128)S(1)} collective-permute-done((f32[96,1024]{1,0:T(8,128)S(1)}, f32[96,1024]{1,0:T(8,128)S(1)}, u32[]{:S(2)}, u32[]{:S(2)}) %collective-permute-start.5) | collective-permute-done | bytes 393248 | tf_op jit(solution)/shard_map/ppermute | solution.py:149
  66.5 2.6 %collective-permute-start.6 = (f32[96,1024]{1,0:T(8,128)S(1)}, f32[96,1024]{1,0:T(8,128)S(1)}, u32[]{:S(2)}, u32[]{:S(2)}) collective-permute-start(f32[96,1024]{1,0:T(8,128)S(1)} %collective-permute-done.5.refs_7_), channel_id=1, source_target_pairs={{0,96},{32,128},{64,160},{96,192},{128,224},{160,256},{192,288},{2... | collective-permute-start | bytes 1179656 | tf_op jit(solution)/shard_map/ppermute | solution.py:149
  69.1 3.8 %collective-permute-start.3 = (f32[96,1024]{1,0:T(8,128)S(1)}, f32[96,1024]{1,0:T(8,128)S(1)}, u32[]{:S(2)}, u32[]{:S(2)}) collective-permute-start(f32[96,1024]{1,0:T(8,128)S(1)} %collective-permute-done.2.refs_1_), channel_id=1, source_target_pairs={{0,672},{32,704},{64,736},{96,0},{128,32},{160,64},{192,96},{224,1... | collective-permute-start | bytes 1179656 | tf_op jit(solution)/shard_map/ppermute | solution.py:150
  72.9 6.8 %collective-permute-done.6.refs_6_ = f32[96,1024]{1,0:T(8,128)S(1)} collective-permute-done((f32[96,1024]{1,0:T(8,128)S(1)}, f32[96,1024]{1,0:T(8,128)S(1)}, u32[]{:S(2)}, u32[]{:S(2)}) %collective-permute-start.6) | collective-permute-done | bytes 393248 | tf_op jit(solution)/shard_map/ppermute | solution.py:149
  79.7 1.9 %collective-permute-start.7 = (f32[96,1024]{1,0:T(8,128)S(1)}, f32[96,1024]{1,0:T(8,128)S(1)}, u32[]{:S(2)}, u32[]{:S(2)}) collective-permute-start(f32[96,1024]{1,0:T(8,128)S(1)} %collective-permute-done.6.refs_6_), channel_id=1, source_target_pairs={{0,96},{32,128},{64,160},{96,192},{128,224},{160,256},{192,288},{2... | collective-permute-start | bytes 1179656 | tf_op jit(solution)/shard_map/ppermute | solution.py:149
  81.6 4.9 %collective-permute-start.4 = (f32[96,1024]{1,0:T(8,128)S(1)}, f32[96,1024]{1,0:T(8,128)S(1)}, u32[]{:S(2)}, u32[]{:S(2)}) collective-permute-start(f32[96,1024]{1,0:T(8,128)S(1)} %collective-permute-done.3.refs_2_), channel_id=1, source_target_pairs={{0,672},{32,704},{64,736},{96,0},{128,32},{160,64},{192,96},{224,1... | collective-permute-start | bytes 1179656 | tf_op jit(solution)/shard_map/ppermute | solution.py:150
  86.5 5.9 %collective-permute-done.7.refs_5_ = f32[96,1024]{1,0:T(8,128)S(1)} collective-permute-done((f32[96,1024]{1,0:T(8,128)S(1)}, f32[96,1024]{1,0:T(8,128)S(1)}, u32[]{:S(2)}, u32[]{:S(2)}) %collective-permute-start.7) | collective-permute-done | bytes 393248 | tf_op jit(solution)/shard_map/ppermute | solution.py:149
  92.4 1.9 %collective-permute-start.8 = (f32[96,1024]{1,0:T(8,128)S(1)}, f32[96,1024]{1,0:T(8,128)S(1)}, u32[]{:S(2)}, u32[]{:S(2)}) collective-permute-start(f32[96,1024]{1,0:T(8,128)S(1)} %collective-permute-done.7.refs_5_), channel_id=1, source_target_pairs={{0,96},{32,128},{64,160},{96,192},{128,224},{160,256},{192,288},{2... | collective-permute-start | bytes 1179656 | tf_op jit(solution)/shard_map/ppermute | solution.py:152
  94.3 9.8 %collective-permute-done.8.refs_4_ = f32[96,1024]{1,0:T(8,128)S(1)} collective-permute-done((f32[96,1024]{1,0:T(8,128)S(1)}, f32[96,1024]{1,0:T(8,128)S(1)}, u32[]{:S(2)}, u32[]{:S(2)}) %collective-permute-start.8) | collective-permute-done | bytes 393248 | tf_op jit(solution)/shard_map/ppermute | solution.py:152
  104.1 0.9 shard_map.56
  105.0 1.1 copy-done
  106.2 8.3 %all-to-all-done.1.pieces = f32[32,48,256]{2,1,0:T(8,128)S(1)} async-done(((f32[32,48,256]{2,1,0:T(8,128)}), f32[32,48,256]{2,1,0:T(8,128)S(1)}, u32[]{:S(2)}, u32[]{:S(2)}) %all-to-all-start.1) | async-done | bytes 1572896 | tf_op jit(solution)/shard_map/all_to_all | solution.py:191
  114.5 2.2 %shard_map.57 = (bf16[512,768]{1,0:T(8,128)(2,1)S(1)}, bf16[512,768]{1,0:T(8,128)(2,1)S(1)}) custom-call(s32[3]{0:T(128)S(1)} %pad_add_fusion.place, s32[32]{0:T(128)S(1)} %copy-done.5, f32[32,48,256]{2,1,0:T(8,128)S(1)} %all-to-all-done.1.pieces), custom_call_target="tpu_custom_call" | custom-call | bytes 3145728 | tf_op jit(solution)/shard_map/pallas_call | solution.py:133
  116.7 1.4 shard_map.59
  118.1 1.9 %collective-permute-start.9 = (f32[128,1024]{1,0:T(8,128)S(1)}, f32[128,1024]{1,0:T(8,128)S(1)}, u32[]{:S(2)}, u32[]{:S(2)}) collective-permute-start(f32[128,1024]{1,0:T(8,128)S(1)} %shard_map.59), channel_id=1, source_target_pairs={{0,1},{1,0},{2,3},{3,2},{4,5},{5,4},{6,7},{7,6},{8,9},{9,8},{10,11... | collective-permute-start | bytes 1572872 | tf_op jit(solution)/shard_map/ppermute | solution.py:216
  120.0 1.4 shard_map.58
  121.4 0.5 collective-permute-done.9
  121.9 12.5 %all_to_all.19 = f32[4,32,1024]{2,1,0:T(8,128)S(1)} all-to-all(f32[4,32,1024]{2,1,0:T(8,128)S(1)} %bitcast.18), channel_id=1, replica_groups={{0,8,16,24},{1,9,17,25},{2,10,18,26},{3,11,19,27},{4,12,20,28},{5,13,21..., dimensions={0} | all-to-all | bytes 1048576 | tf_op jit(solution)/shard_map/all_to_all | solution.py:219
  134.4 1.9 %collective-permute-start.10 = (f32[16,1024]{1,0:T(8,128)S(1)}, f32[16,1024]{1,0:T(8,128)S(1)}, u32[]{:S(2)}, u32[]{:S(2)}) collective-permute-start(f32[16,1024]{1,0:T(8,128)S(1)} %slice.9), channel_id=1, source_target_pairs={{0,2},{1,3},{2,0},{3,1},{4,6},{5,7},{6,4},{7,5},{8,10},{9,11},{10,... | collective-permute-start | bytes 196616 | tf_op jit(solution)/shard_map/ppermute | solution.py:221
  136.4 7.5 %collective-permute-done.10 = f32[16,1024]{1,0:T(8,128)S(1)} collective-permute-done((f32[16,1024]{1,0:T(8,128)S(1)}, f32[16,1024]{1,0:T(8,128)S(1)}, u32[]{:S(2)}, u32[]{:S(2)}) %collective-permute-start.10) | collective-permute-done | bytes 65568 | tf_op jit(solution)/shard_map/ppermute | solution.py:221
  143.9 0.1 reshape.153
  144.0 0.1 copy.28
  144.1 0.1 reshape.154
  144.3 0.6 fusion.4
  (23 shorter events, 0.3 us)
Async XLA Ops:
  1.8 34.9 %all-to-all-start = ((f32[32,2,1024]{2,1,0:T(2,128)}), f32[32,2,1024]{2,1,0:T(2,128)S(1)}, u32[]{:S(2)}, u32[]{:S(2)}) async-start(f32[32,2,1024]{2,1,0:T(2,128)} %bitcast.4), calls=%async_computation | async-start | bytes 524288 | tf_op jit(solution)/shard_map/all_to_all | solution.py:171
  19.2 1.4 copy-start.2
  20.6 0.7 copy-start.3
  21.3 0.7 copy-start.4
  21.9 5.3 %copy-start.5 = (s32[32]{0:T(128)S(1)}, s32[32]{0:T(128)}, u32[]{:S(2)}) copy-start(s32[32]{0:T(128)} %partner.1) | copy-start | bytes 388
  38.1 8.0 %collective-permute-start = (f32[32,1024]{1,0:T(8,128)S(1)}, f32[32,1024]{1,0:T(8,128)S(1)}, u32[]{:S(2)}, u32[]{:S(2)}) collective-permute-start(f32[32,1024]{1,0:T(8,128)S(1)} %fusion), channel_id=1, source_target_pairs={{0,32},{32,64},{64,0},{96,128},{128,160},{160,96},{192,224},{224,2... | collective-permute-start | bytes 393224 | tf_op jit(solution)/shard_map/ppermute | solution.py:188
  41.0 7.5 %collective-permute-start.1 = (f32[32,1024]{1,0:T(8,128)S(1)}, f32[32,1024]{1,0:T(8,128)S(1)}, u32[]{:S(2)}, u32[]{:S(2)}) collective-permute-start(f32[32,1024]{1,0:T(8,128)S(1)} %fusion), channel_id=1, source_target_pairs={{0,64},{32,0},{64,32},{96,160},{128,96},{160,128},{192,256},{224,1... | collective-permute-start | bytes 393224 | tf_op jit(solution)/shard_map/ppermute | solution.py:189
  48.5 66.0 %all-to-all-start.1 = ((f32[32,48,256]{2,1,0:T(8,128)}), f32[32,48,256]{2,1,0:T(8,128)S(1)}, u32[]{:S(2)}, u32[]{:S(2)}) async-start(f32[32,48,256]{2,1,0:T(8,128)} %shard_map.55), calls=%async_computation.1 | async-start | bytes 3145728 | tf_op jit(solution)/shard_map/all_to_all | solution.py:191
  53.3 13.2 %collective-permute-start.5 = (f32[96,1024]{1,0:T(8,128)S(1)}, f32[96,1024]{1,0:T(8,128)S(1)}, u32[]{:S(2)}, u32[]{:S(2)}) collective-permute-start(f32[96,1024]{1,0:T(8,128)S(1)} %pad_maximum_fusion.refs_0_), channel_id=1, source_target_pairs={{0,96},{32,128},{64,160},{96,192},{128,224},{160,256},{192,288},{2... | collective-permute-start | bytes 1179656 | tf_op jit(solution)/shard_map/ppermute | solution.py:149
  55.9 13.2 %collective-permute-start.2 = (f32[96,1024]{1,0:T(8,128)S(1)}, f32[96,1024]{1,0:T(8,128)S(1)}, u32[]{:S(2)}, u32[]{:S(2)}) collective-permute-start(f32[96,1024]{1,0:T(8,128)S(1)} %pad_maximum_fusion.refs_0_), channel_id=1, source_target_pairs={{0,672},{32,704},{64,736},{96,0},{128,32},{160,64},{192,96},{224,1... | collective-permute-start | bytes 1179656 | tf_op jit(solution)/shard_map/ppermute | solution.py:150
  66.5 13.2 %collective-permute-start.6 = (f32[96,1024]{1,0:T(8,128)S(1)}, f32[96,1024]{1,0:T(8,128)S(1)}, u32[]{:S(2)}, u32[]{:S(2)}) collective-permute-start(f32[96,1024]{1,0:T(8,128)S(1)} %collective-permute-done.5.refs_7_), channel_id=1, source_target_pairs={{0,96},{32,128},{64,160},{96,192},{128,224},{160,256},{192,288},{2... | collective-permute-start | bytes 1179656 | tf_op jit(solution)/shard_map/ppermute | solution.py:149
  69.1 12.5 %collective-permute-start.3 = (f32[96,1024]{1,0:T(8,128)S(1)}, f32[96,1024]{1,0:T(8,128)S(1)}, u32[]{:S(2)}, u32[]{:S(2)}) collective-permute-start(f32[96,1024]{1,0:T(8,128)S(1)} %collective-permute-done.2.refs_1_), channel_id=1, source_target_pairs={{0,672},{32,704},{64,736},{96,0},{128,32},{160,64},{192,96},{224,1... | collective-permute-start | bytes 1179656 | tf_op jit(solution)/shard_map/ppermute | solution.py:150
  79.7 12.7 %collective-permute-start.7 = (f32[96,1024]{1,0:T(8,128)S(1)}, f32[96,1024]{1,0:T(8,128)S(1)}, u32[]{:S(2)}, u32[]{:S(2)}) collective-permute-start(f32[96,1024]{1,0:T(8,128)S(1)} %collective-permute-done.6.refs_6_), channel_id=1, source_target_pairs={{0,96},{32,128},{64,160},{96,192},{128,224},{160,256},{192,288},{2... | collective-permute-start | bytes 1179656 | tf_op jit(solution)/shard_map/ppermute | solution.py:149
  81.6 12.6 %collective-permute-start.4 = (f32[96,1024]{1,0:T(8,128)S(1)}, f32[96,1024]{1,0:T(8,128)S(1)}, u32[]{:S(2)}, u32[]{:S(2)}) collective-permute-start(f32[96,1024]{1,0:T(8,128)S(1)} %collective-permute-done.3.refs_2_), channel_id=1, source_target_pairs={{0,672},{32,704},{64,736},{96,0},{128,32},{160,64},{192,96},{224,1... | collective-permute-start | bytes 1179656 | tf_op jit(solution)/shard_map/ppermute | solution.py:150
  92.4 11.7 %collective-permute-start.8 = (f32[96,1024]{1,0:T(8,128)S(1)}, f32[96,1024]{1,0:T(8,128)S(1)}, u32[]{:S(2)}, u32[]{:S(2)}) collective-permute-start(f32[96,1024]{1,0:T(8,128)S(1)} %collective-permute-done.7.refs_5_), channel_id=1, source_target_pairs={{0,96},{32,128},{64,160},{96,192},{128,224},{160,256},{192,288},{2... | collective-permute-start | bytes 1179656 | tf_op jit(solution)/shard_map/ppermute | solution.py:152
  105.0 1.1 copy-start
  114.5 2.2 %copy-start.1 = (bf16[768,1024]{1,0:T(8,128)(2,1)S(1)}, bf16[768,1024]{1,0:T(8,128)(2,1)}, u32[]{:S(2)}) copy-start(bf16[768,1024]{1,0:T(8,128)(2,1)} %copy-done) | copy-start | bytes 4718596
  118.1 3.8 %collective-permute-start.9 = (f32[128,1024]{1,0:T(8,128)S(1)}, f32[128,1024]{1,0:T(8,128)S(1)}, u32[]{:S(2)}, u32[]{:S(2)}) collective-permute-start(f32[128,1024]{1,0:T(8,128)S(1)} %shard_map.59), channel_id=1, source_target_pairs={{0,1},{1,0},{2,3},{3,2},{4,5},{5,4},{6,7},{7,6},{8,9},{9,8},{10,11... | collective-permute-start | bytes 1572872 | tf_op jit(solution)/shard_map/ppermute | solution.py:216
  134.4 9.4 %collective-permute-start.10 = (f32[16,1024]{1,0:T(8,128)S(1)}, f32[16,1024]{1,0:T(8,128)S(1)}, u32[]{:S(2)}, u32[]{:S(2)}) collective-permute-start(f32[16,1024]{1,0:T(8,128)S(1)} %slice.9), channel_id=1, source_target_pairs={{0,2},{1,3},{2,0},{3,1},{4,6},{5,7},{6,4},{7,5},{8,10},{9,11},{10,... | collective-permute-start | bytes 196616 | tf_op jit(solution)/shard_map/ppermute | solution.py:221

commit v9 on v8

--- a/solution.py
+++ b/solution.py
@@ -36,20 +36,24 @@
     return jnp.swapaxes(rows.reshape(count, NO, NO), 1, 2).reshape(count, cols)
 
 
-def pieces_kernel(place, row_irrep, col_irrep, block, out, turned):
-    for x in range(NX):
-        for col in range(DEPTH // BW):
-            keep = row_irrep[x] == col_irrep[col]
-            values = jnp.where(keep, block[x * BW : (x + 1) * BW, col * BW : (col + 1) * BW], 0.0)
-            turned[col * BW : (col + 1) * BW, :] = values.T
-        lanes = slice(x * BW // 2, (x + 1) * BW // 2)
-        for to in range(NARROW):
-            upper = to // 4 % 2
-            for near in range(2):
-                rows = slice(near * WIDE, (near + 1) * WIDE)
-                column = to & ~4 | near * 4
-                found = turned[pl.ds(place[2] + column, WIDE, stride=LR), :]
-                out[to, rows, lanes] = found[:, upper * (BW // 2) : (upper + 1) * (BW // 2)]
+def pieces_kernel(row_irrep, col_irrep, block, out, turned, second):
+    for pair in range(NX // 2):
+        for x in range(2):
+            at = pair * 2 + x
+            for col in range(DEPTH // BW):
+                keep = row_irrep[at] == col_irrep[col]
+                values = jnp.where(keep, block[at * BW : (at + 1) * BW, col * BW : (col + 1) * BW], 0.0)
+                (turned, second)[x][col * BW : (col + 1) * BW, :] = values.T
+        lanes = slice(pair * BW, (pair + 1) * BW)
+        for near in range(2):
+            rows = slice(near * WIDE, (near + 1) * WIDE)
+            for k in range(LR):
+                if k // 4 % 2 != near:
+                    continue
+                found = [ref[pl.ds(k, WIDE, stride=LR), :] for ref in (turned, second)]
+                for upper in range(2):
+                    half = slice(upper * (BW // 2), (upper + 1) * (BW // 2))
+                    out[k & ~4 | upper * 4, rows, lanes] = jnp.concatenate([f[:, half] for f in found], axis=1)
 
 
 def fill_pairs(partner, plus, minus, turned, ranks):
@@ -164,7 +168,7 @@
 
 
 def local(integrals, amplitudes, row_irrep, col_irrep, partner):
-    place = jnp.stack([lax.axis_index("narrow"), lax.axis_index("wide"), 0]).astype(jnp.int32)
+    place = jnp.stack([lax.axis_index("narrow"), lax.axis_index("wide")]).astype(jnp.int32)
 
     both = amplitudes.reshape(NX, 1, 2, 4, COLS).swapaxes(2, 3)
     both = jnp.broadcast_to(both, (NX, 2, 4, 2, COLS)).reshape(NARROW, 2, COLS)
@@ -172,11 +176,11 @@
     pieces = call(
         pieces_kernel,
         jax.ShapeDtypeStruct((NARROW, 2 * WIDE, HALF), jnp.float32),
-        [SMEM, SMEM, SMEM, VMEM],
-        (place, row_irrep, col_irrep, integrals),
+        [SMEM, SMEM, VMEM],
+        (row_irrep, col_irrep, integrals),
         0,
         3 << 20,
-        [pltpu.VMEM((DEPTH, BW), jnp.float32)],
+        [pltpu.VMEM((DEPTH, BW), jnp.float32)] * 2,
     )
     plus, minus = pairs_of(partner)
     pieces, rows = lax.optimization_barrier((pieces, rows))

time: 146 us -> 149 us (1.021)
  the two profiles are of different devices: /device:TPU:104 before, /device:TPU:64 now
where the time goes in v9:
time: 149 us; the launch traced here: 148 us
  starting transfers between devices  58.7 us (39%)
  waiting for transfers between devices  45.3 us (30%)
  local copies, waits for them, and re-layouts  19.1 us (13%)
  blocking collectives  13.6 us (9%)
  Pallas kernels  9.16 us (6%)
  other arithmetic  1.85 us (1%)
    ppermute x3, waiting for transfers between devices, gather_y(): up = lax.ppermute(up, 'wide', y_shift(1))  17.4 us
    all_to_all x1, starting transfers between devices, local(): lax.all_to_all(both, 'narrow', 0, 0, tiled=True).swapaxes(0, 1)  16.5 us
    unnamed x40, local copies, waits for them, and re-layouts  16 us
    ppermute x3, starting transfers between devices, gather_y(): down = lax.ppermute(down, 'wide', y_shift(-1))  14.1 us
    all_to_all x1, blocking collectives, local(): lax.all_to_all(chip, 'narrow', 0, 0, tiled=True, axis_index_groups=X_GROUPS)  13.6 us
    all_to_all x1, waiting for transfers between devices, local(): lax.all_to_all(both, 'narrow', 0, 0, tiled=True).swapaxes(0, 1)  11.4 us
    pallas_call x5, Pallas kernels, call(): pl.pallas_call(kernel, out_shape=outs, in_specs=in_specs, out_specs=[VMEM...  9.16 us
    ppermute x1, waiting for transfers between devices, gather_y(): found[4] = lax.ppermute(up, 'wide', y_shift(1))  8.6 us
  transfers between devices with their start and end apart: 13, of which 9 were waited for; matrix products, arithmetic and copies ran while one was open for 1% of the time, Pallas kernels for 4%

profile of v9, /device:TPU:64, one launch (start us, length us, event | category | flops | bytes accessed | tf_op | source)
XLA Modules:
  0.0 148.4 jit_solution(17356069080965007736)
XLA Ops:
  0.0 0.9 reshape.148
  1.1 0.8 broadcast_in_dim.45
  1.9 16.5 %all-to-all-start = ((f32[32,2,1024]{2,1,0:T(2,128)}), f32[32,2,1024]{2,1,0:T(2,128)S(1)}, u32[]{:S(2)}, u32[]{:S(2)}) async-start(f32[32,2,1024]{2,1,0:T(2,128)} %bitcast.4), calls=%async_computation | async-start | bytes 524288 | tf_op jit(solution)/shard_map/all_to_all | solution.py:175
  18.4 0.8 fusion.23
  19.2 1.4 copy-done.2
  20.6 0.7 copy-done.17
  21.2 0.7 copy-done.18
  21.9 3.3 %shard_map.55 = f32[32,48,256]{2,1,0:T(8,128)} custom-call(s32[4]{0:T(128)S(1)} %copy-done.17, s32[6]{0:T(128)S(1)} %copy-done.18, f32[512,768]{1,0:T(8,128)S(1)} %copy-done.2), custom_call_target="tpu_custom_call" | custom-call | bytes 3145728 | tf_op jit(solution)/shard_map/pallas_call | solution.py:137
  25.4 11.4 %all-to-all-done = f32[32,2,1024]{2,1,0:T(2,128)S(1)} async-done(((f32[32,2,1024]{2,1,0:T(2,128)}), f32[32,2,1024]{2,1,0:T(2,128)S(1)}, u32[]{:S(2)}, u32[]{:S(2)}) %all-to-all-start) | async-done | bytes 262176 | tf_op jit(solution)/shard_map/all_to_all | solution.py:175
  38.1 3.0 %collective-permute-start = (f32[32,1024]{1,0:T(8,128)S(1)}, f32[32,1024]{1,0:T(8,128)S(1)}, u32[]{:S(2)}, u32[]{:S(2)}) collective-permute-start(f32[32,1024]{1,0:T(8,128)S(1)} %fusion), channel_id=1, source_target_pairs={{0,32},{32,64},{64,0},{96,128},{128,160},{160,96},{192,224},{224,2... | collective-permute-start | bytes 393224 | tf_op jit(solution)/shard_map/ppermute | solution.py:192
  41.1 2.9 %collective-permute-start.1 = (f32[32,1024]{1,0:T(8,128)S(1)}, f32[32,1024]{1,0:T(8,128)S(1)}, u32[]{:S(2)}, u32[]{:S(2)}) collective-permute-start(f32[32,1024]{1,0:T(8,128)S(1)} %fusion), channel_id=1, source_target_pairs={{0,64},{32,0},{64,32},{96,160},{128,96},{160,128},{192,256},{224,1... | collective-permute-start | bytes 393224 | tf_op jit(solution)/shard_map/ppermute | solution.py:193
  44.0 2.1 %collective-permute-done = f32[32,1024]{1,0:T(8,128)S(1)} collective-permute-done((f32[32,1024]{1,0:T(8,128)S(1)}, f32[32,1024]{1,0:T(8,128)S(1)}, u32[]{:S(2)}, u32[]{:S(2)}) %collective-permute-start) | collective-permute-done | bytes 131104 | tf_op jit(solution)/shard_map/ppermute | solution.py:192
  46.1 2.4 %collective-permute-done.1 = f32[32,1024]{1,0:T(8,128)S(1)} collective-permute-done((f32[32,1024]{1,0:T(8,128)S(1)}, f32[32,1024]{1,0:T(8,128)S(1)}, u32[]{:S(2)}, u32[]{:S(2)}) %collective-permute-start.1) | collective-permute-done | bytes 131104 | tf_op jit(solution)/shard_map/ppermute | solution.py:193
  48.5 4.8 %all-to-all-start.1 = ((f32[32,48,256]{2,1,0:T(8,128)}), f32[32,48,256]{2,1,0:T(8,128)S(1)}, u32[]{:S(2)}, u32[]{:S(2)}) async-start(f32[32,48,256]{2,1,0:T(8,128)} %shard_map.55), calls=%async_computation.1 | async-start | bytes 3145728 | tf_op jit(solution)/shard_map/all_to_all | solution.py:195
  53.4 3.5 %collective-permute-start.5 = (f32[96,1024]{1,0:T(8,128)S(1)}, f32[96,1024]{1,0:T(8,128)S(1)}, u32[]{:S(2)}, u32[]{:S(2)}) collective-permute-start(f32[96,1024]{1,0:T(8,128)S(1)} %pad_maximum_fusion.refs_0_), channel_id=1, source_target_pairs={{0,96},{32,128},{64,160},{96,192},{128,224},{160,256},{192,288},{2... | collective-permute-start | bytes 1179656 | tf_op jit(solution)/shard_map/ppermute | solution.py:153
  56.9 3.8 %collective-permute-start.2 = (f32[96,1024]{1,0:T(8,128)S(1)}, f32[96,1024]{1,0:T(8,128)S(1)}, u32[]{:S(2)}, u32[]{:S(2)}) collective-permute-start(f32[96,1024]{1,0:T(8,128)S(1)} %pad_maximum_fusion.refs_0_), channel_id=1, source_target_pairs={{0,672},{32,704},{64,736},{96,0},{128,32},{160,64},{192,96},{224,1... | collective-permute-start | bytes 1179656 | tf_op jit(solution)/shard_map/ppermute | solution.py:154
  60.7 7.6 %collective-permute-done.5.refs_7_ = f32[96,1024]{1,0:T(8,128)S(1)} collective-permute-done((f32[96,1024]{1,0:T(8,128)S(1)}, f32[96,1024]{1,0:T(8,128)S(1)}, u32[]{:S(2)}, u32[]{:S(2)}) %collective-permute-start.5) | collective-permute-done | bytes 393248 | tf_op jit(solution)/shard_map/ppermute | solution.py:153
  68.3 1.9 %collective-permute-start.6 = (f32[96,1024]{1,0:T(8,128)S(1)}, f32[96,1024]{1,0:T(8,128)S(1)}, u32[]{:S(2)}, u32[]{:S(2)}) collective-permute-start(f32[96,1024]{1,0:T(8,128)S(1)} %collective-permute-done.5.refs_7_), channel_id=1, source_target_pairs={{0,96},{32,128},{64,160},{96,192},{128,224},{160,256},{192,288},{2... | collective-permute-start | bytes 1179656 | tf_op jit(solution)/shard_map/ppermute | solution.py:153
  70.2 0.7 copy-done.3
  71.0 5.1 %collective-permute-start.3 = (f32[96,1024]{1,0:T(8,128)S(1)}, f32[96,1024]{1,0:T(8,128)S(1)}, u32[]{:S(2)}, u32[]{:S(2)}) collective-permute-start(f32[96,1024]{1,0:T(8,128)S(1)} %collective-permute-done.2.refs_1_), channel_id=1, source_target_pairs={{0,672},{32,704},{64,736},{96,0},{128,32},{160,64},{192,96},{224,1... | collective-permute-start | bytes 1179656 | tf_op jit(solution)/shard_map/ppermute | solution.py:154
  76.1 0.7 copy-done.5
  76.8 5.3 %collective-permute-done.6.refs_6_ = f32[96,1024]{1,0:T(8,128)S(1)} collective-permute-done((f32[96,1024]{1,0:T(8,128)S(1)}, f32[96,1024]{1,0:T(8,128)S(1)}, u32[]{:S(2)}, u32[]{:S(2)}) %collective-permute-start.6) | collective-permute-done | bytes 393248 | tf_op jit(solution)/shard_map/ppermute | solution.py:153
  82.2 1.9 %collective-permute-start.7 = (f32[96,1024]{1,0:T(8,128)S(1)}, f32[96,1024]{1,0:T(8,128)S(1)}, u32[]{:S(2)}, u32[]{:S(2)}) collective-permute-start(f32[96,1024]{1,0:T(8,128)S(1)} %collective-permute-done.6.refs_6_), channel_id=1, source_target_pairs={{0,96},{32,128},{64,160},{96,192},{128,224},{160,256},{192,288},{2... | collective-permute-start | bytes 1179656 | tf_op jit(solution)/shard_map/ppermute | solution.py:153
  84.1 0.7 copy-done.7
  84.9 5.1 %collective-permute-start.4 = (f32[96,1024]{1,0:T(8,128)S(1)}, f32[96,1024]{1,0:T(8,128)S(1)}, u32[]{:S(2)}, u32[]{:S(2)}) collective-permute-start(f32[96,1024]{1,0:T(8,128)S(1)} %collective-permute-done.3.refs_2_), channel_id=1, source_target_pairs={{0,672},{32,704},{64,736},{96,0},{128,32},{160,64},{192,96},{224,1... | collective-permute-start | bytes 1179656 | tf_op jit(solution)/shard_map/ppermute | solution.py:154
  90.0 0.7 copy-done.9
  90.7 4.5 %collective-permute-done.7.refs_5_ = f32[96,1024]{1,0:T(8,128)S(1)} collective-permute-done((f32[96,1024]{1,0:T(8,128)S(1)}, f32[96,1024]{1,0:T(8,128)S(1)}, u32[]{:S(2)}, u32[]{:S(2)}) %collective-permute-start.7) | collective-permute-done | bytes 393248 | tf_op jit(solution)/shard_map/ppermute | solution.py:153
  95.2 1.9 %collective-permute-start.8 = (f32[96,1024]{1,0:T(8,128)S(1)}, f32[96,1024]{1,0:T(8,128)S(1)}, u32[]{:S(2)}, u32[]{:S(2)}) collective-permute-start(f32[96,1024]{1,0:T(8,128)S(1)} %collective-permute-done.7.refs_5_), channel_id=1, source_target_pairs={{0,96},{32,128},{64,160},{96,192},{128,224},{160,256},{192,288},{2... | collective-permute-start | bytes 1179656 | tf_op jit(solution)/shard_map/ppermute | solution.py:156
  97.1 0.7 copy-done.11
  98.0 0.7 copy-done.13
  98.7 8.6 %collective-permute-done.8.refs_4_ = f32[96,1024]{1,0:T(8,128)S(1)} collective-permute-done((f32[96,1024]{1,0:T(8,128)S(1)}, f32[96,1024]{1,0:T(8,128)S(1)}, u32[]{:S(2)}, u32[]{:S(2)}) %collective-permute-start.8) | collective-permute-done | bytes 393248 | tf_op jit(solution)/shard_map/ppermute | solution.py:156
  107.3 0.8 copy-done.15
  108.1 1.0 copy-done.4
  109.1 1.0 copy-done.6
  110.1 1.0 copy-done.8
  111.1 1.0 copy-done.10
  112.1 1.0 copy-done.12
  113.1 1.0 copy-done.14
  114.0 1.0 copy-done.16
  115.0 0.9 shard_map.56
  116.0 1.1 copy-done
  117.1 2.2 %shard_map.57 = (bf16[512,768]{1,0:T(8,128)(2,1)S(1)}, bf16[512,768]{1,0:T(8,128)(2,1)S(1)}) custom-call(s32[2]{0:T(128)S(1)} %pad_add_fusion.place, s32[32]{0:T(128)S(1)} %copy-done.19, f32[32,48,256]{2,1,0:T(8,128)S(1)} %all-to-all-done.1.pieces), custom_call_target="tpu_custom_call" | custom-call | bytes 3145728 | tf_op jit(solution)/shard_map/pallas_call | solution.py:137
  119.3 1.4 shard_map.59
  120.7 1.9 %collective-permute-start.9 = (f32[128,1024]{1,0:T(8,128)S(1)}, f32[128,1024]{1,0:T(8,128)S(1)}, u32[]{:S(2)}, u32[]{:S(2)}) collective-permute-start(f32[128,1024]{1,0:T(8,128)S(1)} %shard_map.59), channel_id=1, source_target_pairs={{0,1},{1,0},{2,3},{3,2},{4,5},{5,4},{6,7},{7,6},{8,9},{9,8},{10,11... | collective-permute-start | bytes 1572872 | tf_op jit(solution)/shard_map/ppermute | solution.py:220
  122.7 1.4 shard_map.58
  124.6 13.6 %all_to_all.19 = f32[4,32,1024]{2,1,0:T(8,128)S(1)} all-to-all(f32[4,32,1024]{2,1,0:T(8,128)S(1)} %bitcast.18), channel_id=1, replica_groups={{0,8,16,24},{1,9,17,25},{2,10,18,26},{3,11,19,27},{4,12,20,28},{5,13,21..., dimensions={0} | all-to-all | bytes 1048576 | tf_op jit(solution)/shard_map/all_to_all | solution.py:223
  138.2 6.4 %collective-permute-start.10 = (f32[16,1024]{1,0:T(8,128)S(1)}, f32[16,1024]{1,0:T(8,128)S(1)}, u32[]{:S(2)}, u32[]{:S(2)}) collective-permute-start(f32[16,1024]{1,0:T(8,128)S(1)} %slice.9), channel_id=1, source_target_pairs={{0,2},{1,3},{2,0},{3,1},{4,6},{5,7},{6,4},{7,5},{8,10},{9,11},{10,... | collective-permute-start | bytes 196616 | tf_op jit(solution)/shard_map/ppermute | solution.py:225
  144.6 2.8 %collective-permute-done.10 = f32[16,1024]{1,0:T(8,128)S(1)} collective-permute-done((f32[16,1024]{1,0:T(8,128)S(1)}, f32[16,1024]{1,0:T(8,128)S(1)}, u32[]{:S(2)}, u32[]{:S(2)}) %collective-permute-start.10) | collective-permute-done | bytes 65568 | tf_op jit(solution)/shard_map/ppermute | solution.py:225
  (51 shorter events, 3.4 us)
Async XLA Ops:
  1.9 34.9 %all-to-all-start = ((f32[32,2,1024]{2,1,0:T(2,128)}), f32[32,2,1024]{2,1,0:T(2,128)S(1)}, u32[]{:S(2)}, u32[]{:S(2)}) async-start(f32[32,2,1024]{2,1,0:T(2,128)} %bitcast.4), calls=%async_computation | async-start | bytes 524288 | tf_op jit(solution)/shard_map/all_to_all | solution.py:175
  19.2 1.4 copy-start.2
  20.6 0.7 copy-start.17
  21.2 0.7 copy-start.18
  21.9 3.3 %copy-start.19 = (s32[32]{0:T(128)S(1)}, s32[32]{0:T(128)}, u32[]{:S(2)}) copy-start(s32[32]{0:T(128)} %partner.1) | copy-start | bytes 388
  38.1 8.0 %collective-permute-start = (f32[32,1024]{1,0:T(8,128)S(1)}, f32[32,1024]{1,0:T(8,128)S(1)}, u32[]{:S(2)}, u32[]{:S(2)}) collective-permute-start(f32[32,1024]{1,0:T(8,128)S(1)} %fusion), channel_id=1, source_target_pairs={{0,32},{32,64},{64,0},{96,128},{128,160},{160,96},{192,224},{224,2... | collective-permute-start | bytes 393224 | tf_op jit(solution)/shard_map/ppermute | solution.py:192
  41.1 7.5 %collective-permute-start.1 = (f32[32,1024]{1,0:T(8,128)S(1)}, f32[32,1024]{1,0:T(8,128)S(1)}, u32[]{:S(2)}, u32[]{:S(2)}) collective-permute-start(f32[32,1024]{1,0:T(8,128)S(1)} %fusion), channel_id=1, source_target_pairs={{0,64},{32,0},{64,32},{96,160},{128,96},{160,128},{192,256},{224,1... | collective-permute-start | bytes 393224 | tf_op jit(solution)/shard_map/ppermute | solution.py:193
  48.5 68.6 %all-to-all-start.1 = ((f32[32,48,256]{2,1,0:T(8,128)}), f32[32,48,256]{2,1,0:T(8,128)S(1)}, u32[]{:S(2)}, u32[]{:S(2)}) async-start(f32[32,48,256]{2,1,0:T(8,128)} %shard_map.55), calls=%async_computation.1 | async-start | bytes 3145728 | tf_op jit(solution)/shard_map/all_to_all | solution.py:195
  53.4 14.9 %collective-permute-start.5 = (f32[96,1024]{1,0:T(8,128)S(1)}, f32[96,1024]{1,0:T(8,128)S(1)}, u32[]{:S(2)}, u32[]{:S(2)}) collective-permute-start(f32[96,1024]{1,0:T(8,128)S(1)} %pad_maximum_fusion.refs_0_), channel_id=1, source_target_pairs={{0,96},{32,128},{64,160},{96,192},{128,224},{160,256},{192,288},{2... | collective-permute-start | bytes 1179656 | tf_op jit(solution)/shard_map/ppermute | solution.py:153
  56.9 14.1 %collective-permute-start.2 = (f32[96,1024]{1,0:T(8,128)S(1)}, f32[96,1024]{1,0:T(8,128)S(1)}, u32[]{:S(2)}, u32[]{:S(2)}) collective-permute-start(f32[96,1024]{1,0:T(8,128)S(1)} %pad_maximum_fusion.refs_0_), channel_id=1, source_target_pairs={{0,672},{32,704},{64,736},{96,0},{128,32},{160,64},{192,96},{224,1... | collective-permute-start | bytes 1179656 | tf_op jit(solution)/shard_map/ppermute | solution.py:154
  68.3 13.9 %collective-permute-start.6 = (f32[96,1024]{1,0:T(8,128)S(1)}, f32[96,1024]{1,0:T(8,128)S(1)}, u32[]{:S(2)}, u32[]{:S(2)}) collective-permute-start(f32[96,1024]{1,0:T(8,128)S(1)} %collective-permute-done.5.refs_7_), channel_id=1, source_target_pairs={{0,96},{32,128},{64,160},{96,192},{128,224},{160,256},{192,288},{2... | collective-permute-start | bytes 1179656 | tf_op jit(solution)/shard_map/ppermute | solution.py:153
  70.2 0.7 copy-start.3
  71.0 13.9 %collective-permute-start.3 = (f32[96,1024]{1,0:T(8,128)S(1)}, f32[96,1024]{1,0:T(8,128)S(1)}, u32[]{:S(2)}, u32[]{:S(2)}) collective-permute-start(f32[96,1024]{1,0:T(8,128)S(1)} %collective-permute-done.2.refs_1_), channel_id=1, source_target_pairs={{0,672},{32,704},{64,736},{96,0},{128,32},{160,64},{192,96},{224,1... | collective-permute-start | bytes 1179656 | tf_op jit(solution)/shard_map/ppermute | solution.py:154
  76.1 0.8 copy-start.5
  82.2 13.0 %collective-permute-start.7 = (f32[96,1024]{1,0:T(8,128)S(1)}, f32[96,1024]{1,0:T(8,128)S(1)}, u32[]{:S(2)}, u32[]{:S(2)}) collective-permute-start(f32[96,1024]{1,0:T(8,128)S(1)} %collective-permute-done.6.refs_6_), channel_id=1, source_target_pairs={{0,96},{32,128},{64,160},{96,192},{128,224},{160,256},{192,288},{2... | collective-permute-start | bytes 1179656 | tf_op jit(solution)/shard_map/ppermute | solution.py:153
  84.1 0.7 copy-start.7
  84.9 13.1 %collective-permute-start.4 = (f32[96,1024]{1,0:T(8,128)S(1)}, f32[96,1024]{1,0:T(8,128)S(1)}, u32[]{:S(2)}, u32[]{:S(2)}) collective-permute-start(f32[96,1024]{1,0:T(8,128)S(1)} %collective-permute-done.3.refs_2_), channel_id=1, source_target_pairs={{0,672},{32,704},{64,736},{96,0},{128,32},{160,64},{192,96},{224,1... | collective-permute-start | bytes 1179656 | tf_op jit(solution)/shard_map/ppermute | solution.py:154
  90.0 0.8 copy-start.9
  95.2 12.1 %collective-permute-start.8 = (f32[96,1024]{1,0:T(8,128)S(1)}, f32[96,1024]{1,0:T(8,128)S(1)}, u32[]{:S(2)}, u32[]{:S(2)}) collective-permute-start(f32[96,1024]{1,0:T(8,128)S(1)} %collective-permute-done.7.refs_5_), channel_id=1, source_target_pairs={{0,96},{32,128},{64,160},{96,192},{128,224},{160,256},{192,288},{2... | collective-permute-start | bytes 1179656 | tf_op jit(solution)/shard_map/ppermute | solution.py:156
  97.1 0.8 copy-start.11
  98.0 0.7 copy-start.13
  107.3 0.8 copy-start.15
  108.1 1.0 copy-start.4
  109.1 1.0 copy-start.6
  110.1 1.0 copy-start.8
  111.1 1.0 copy-start.10
  112.1 1.0 copy-start.12
  113.0 1.0 copy-start.14
  114.0 1.0 copy-start.16
  116.0 1.1 copy-start
  117.1 2.2 %copy-start.1 = (bf16[768,1024]{1,0:T(8,128)(2,1)S(1)}, bf16[768,1024]{1,0:T(8,128)(2,1)}, u32[]{:S(2)}) copy-start(bf16[768,1024]{1,0:T(8,128)(2,1)} %copy-done) | copy-start | bytes 4718596
  120.7 3.8 %collective-permute-start.9 = (f32[128,1024]{1,0:T(8,128)S(1)}, f32[128,1024]{1,0:T(8,128)S(1)}, u32[]{:S(2)}, u32[]{:S(2)}) collective-permute-start(f32[128,1024]{1,0:T(8,128)S(1)} %shard_map.59), channel_id=1, source_target_pairs={{0,1},{1,0},{2,3},{3,2},{4,5},{5,4},{6,7},{7,6},{8,9},{9,8},{10,11... | collective-permute-start | bytes 1572872 | tf_op jit(solution)/shard_map/ppermute | solution.py:220
  138.2 9.2 %collective-permute-start.10 = (f32[16,1024]{1,0:T(8,128)S(1)}, f32[16,1024]{1,0:T(8,128)S(1)}, u32[]{:S(2)}, u32[]{:S(2)}) collective-permute-start(f32[16,1024]{1,0:T(8,128)S(1)} %slice.9), channel_id=1, source_target_pairs={{0,2},{1,3},{2,0},{3,1},{4,6},{5,7},{6,4},{7,5},{8,10},{9,11},{10,... | collective-permute-start | bytes 196616 | tf_op jit(solution)/shard_map/ppermute | solution.py:225

commit v10 on v9

--- a/solution.py
+++ b/solution.py
@@ -36,7 +36,7 @@
     return jnp.swapaxes(rows.reshape(count, NO, NO), 1, 2).reshape(count, cols)
 
 
-def pieces_kernel(row_irrep, col_irrep, block, out, turned, second):
+def pieces_kernel(place, row_irrep, col_irrep, block, out, turned, second):
     for pair in range(NX // 2):
         for x in range(2):
             at = pair * 2 + x
@@ -176,8 +176,8 @@
     pieces = call(
         pieces_kernel,
         jax.ShapeDtypeStruct((NARROW, 2 * WIDE, HALF), jnp.float32),
-        [SMEM, SMEM, VMEM],
-        (row_irrep, col_irrep, integrals),
+        [SMEM, SMEM, SMEM, VMEM],
+        (place, row_irrep, col_irrep, integrals),
         0,
         3 << 20,
         [pltpu.VMEM((DEPTH, BW), jnp.float32)] * 2,

time: 149 us -> 146 us (0.980)
  the two profiles are of different devices: /device:TPU:64 before, /device:TPU:80 now
where the time goes in v10:
time: 146 us; the launch traced here: 145 us
  waiting for transfers between devices  58.9 us (40%)
  starting transfers between devices  55 us (38%)
  blocking collectives  12.5 us (9%)
  Pallas kernels  9.15 us (6%)
  local copies, waits for them, and re-layouts  6.84 us (5%)
  other arithmetic  1.85 us (1%)
    ppermute x3, waiting for transfers between devices, gather_y(): up = lax.ppermute(up, 'wide', y_shift(1))  18.2 us
    all_to_all x1, starting transfers between devices, local(): lax.all_to_all(both, 'narrow', 0, 0, tiled=True).swapaxes(0, 1)  16.5 us
    all_to_all x1, blocking collectives, local(): lax.all_to_all(chip, 'narrow', 0, 0, tiled=True, axis_index_groups=X_GROUPS)  12.5 us
    ppermute x3, starting transfers between devices, gather_y(): up = lax.ppermute(up, 'wide', y_shift(1))  12.3 us
    all_to_all x1, waiting for transfers between devices, local(): lax.all_to_all(both, 'narrow', 0, 0, tiled=True).swapaxes(0, 1)  11.4 us
    all_to_all x1, waiting for transfers between devices, local(): pieces = lax.all_to_all(pieces, 'narrow', 0, 0, tiled=True)  9.73 us
    pallas_call x5, Pallas kernels, call(): pl.pallas_call(kernel, out_shape=outs, in_specs=in_specs, out_specs=[VMEM...  9.15 us
    ppermute x1, waiting for transfers between devices, local(): result = reduced[:OUT] + lax.ppermute(reduced[OUT:], 'narrow', Z_NEAR)  7.48 us
  transfers between devices with their start and end apart: 13, of which 13 were waited for; matrix products, arithmetic and copies ran while one was open for 1% of the time, Pallas kernels for 4%

profile of v10, /device:TPU:80, one launch (start us, length us, event | category | flops | bytes accessed | tf_op | source)
XLA Modules:
  0.0 144.9 jit_solution(13970495173846499970)
XLA Ops:
  0.0 0.9 reshape.148
  1.1 0.8 broadcast_in_dim.45
  1.8 16.5 %all-to-all-start = ((f32[32,2,1024]{2,1,0:T(2,128)}), f32[32,2,1024]{2,1,0:T(2,128)S(1)}, u32[]{:S(2)}, u32[]{:S(2)}) async-start(f32[32,2,1024]{2,1,0:T(2,128)} %bitcast.4), calls=%async_computation | async-start | bytes 524288 | tf_op jit(solution)/shard_map/all_to_all | solution.py:175
  18.4 0.8 fusion.23
  19.2 1.4 copy-done.2
  20.6 0.7 copy-done.3
  21.3 0.7 copy-done.4
  21.9 3.3 %shard_map.55 = f32[32,48,256]{2,1,0:T(8,128)} custom-call(s32[2]{0:T(128)S(1)} %pad_add_fusion.place, s32[4]{0:T(128)S(1)} %copy-done.3, s32[6]{0:T(128)S(1)} %copy-done.4, f32[512,768]{1,0:T(8,128)S(1)} %copy-done.2), custom_call_target="tpu_custom_call" | custom-call | bytes 3145728 | tf_op jit(solution)/shard_map/pallas_call | solution.py:137
  25.4 11.4 %all-to-all-done = f32[32,2,1024]{2,1,0:T(2,128)S(1)} async-done(((f32[32,2,1024]{2,1,0:T(2,128)}), f32[32,2,1024]{2,1,0:T(2,128)S(1)}, u32[]{:S(2)}, u32[]{:S(2)}) %all-to-all-start) | async-done | bytes 262176 | tf_op jit(solution)/shard_map/all_to_all | solution.py:175
  36.8 0.2 copy.24
  37.0 0.3 copy.25
  37.4 0.2 copy.26
  37.5 0.2 fusion.2
  37.8 0.3 fusion
  38.1 3.0 %collective-permute-start = (f32[32,1024]{1,0:T(8,128)S(1)}, f32[32,1024]{1,0:T(8,128)S(1)}, u32[]{:S(2)}, u32[]{:S(2)}) collective-permute-start(f32[32,1024]{1,0:T(8,128)S(1)} %fusion), channel_id=1, source_target_pairs={{0,32},{32,64},{64,0},{96,128},{128,160},{160,96},{192,224},{224,2... | collective-permute-start | bytes 393224 | tf_op jit(solution)/shard_map/ppermute | solution.py:192
  41.0 2.9 %collective-permute-start.1 = (f32[32,1024]{1,0:T(8,128)S(1)}, f32[32,1024]{1,0:T(8,128)S(1)}, u32[]{:S(2)}, u32[]{:S(2)}) collective-permute-start(f32[32,1024]{1,0:T(8,128)S(1)} %fusion), channel_id=1, source_target_pairs={{0,64},{32,0},{64,32},{96,160},{128,96},{160,128},{192,256},{224,1... | collective-permute-start | bytes 393224 | tf_op jit(solution)/shard_map/ppermute | solution.py:193
  44.0 2.1 %collective-permute-done = f32[32,1024]{1,0:T(8,128)S(1)} collective-permute-done((f32[32,1024]{1,0:T(8,128)S(1)}, f32[32,1024]{1,0:T(8,128)S(1)}, u32[]{:S(2)}, u32[]{:S(2)}) %collective-permute-start) | collective-permute-done | bytes 131104 | tf_op jit(solution)/shard_map/ppermute | solution.py:192
  46.0 2.4 %collective-permute-done.1 = f32[32,1024]{1,0:T(8,128)S(1)} collective-permute-done((f32[32,1024]{1,0:T(8,128)S(1)}, f32[32,1024]{1,0:T(8,128)S(1)}, u32[]{:S(2)}, u32[]{:S(2)}) %collective-permute-start.1) | collective-permute-done | bytes 131104 | tf_op jit(solution)/shard_map/ppermute | solution.py:193
  48.5 4.8 %all-to-all-start.1 = ((f32[32,48,256]{2,1,0:T(8,128)}), f32[32,48,256]{2,1,0:T(8,128)S(1)}, u32[]{:S(2)}, u32[]{:S(2)}) async-start(f32[32,48,256]{2,1,0:T(8,128)} %shard_map.55), calls=%async_computation.1 | async-start | bytes 3145728 | tf_op jit(solution)/shard_map/all_to_all | solution.py:195
  53.3 3.5 %collective-permute-start.5 = (f32[96,1024]{1,0:T(8,128)S(1)}, f32[96,1024]{1,0:T(8,128)S(1)}, u32[]{:S(2)}, u32[]{:S(2)}) collective-permute-start(f32[96,1024]{1,0:T(8,128)S(1)} %pad_maximum_fusion.refs_0_), channel_id=1, source_target_pairs={{0,96},{32,128},{64,160},{96,192},{128,224},{160,256},{192,288},{2... | collective-permute-start | bytes 1179656 | tf_op jit(solution)/shard_map/ppermute | solution.py:153
  56.8 2.4 %collective-permute-start.2 = (f32[96,1024]{1,0:T(8,128)S(1)}, f32[96,1024]{1,0:T(8,128)S(1)}, u32[]{:S(2)}, u32[]{:S(2)}) collective-permute-start(f32[96,1024]{1,0:T(8,128)S(1)} %pad_maximum_fusion.refs_0_), channel_id=1, source_target_pairs={{0,672},{32,704},{64,736},{96,0},{128,32},{160,64},{192,96},{224,1... | collective-permute-start | bytes 1179656 | tf_op jit(solution)/shard_map/ppermute | solution.py:154
  59.2 7.3 %collective-permute-done.5.refs_7_ = f32[96,1024]{1,0:T(8,128)S(1)} collective-permute-done((f32[96,1024]{1,0:T(8,128)S(1)}, f32[96,1024]{1,0:T(8,128)S(1)}, u32[]{:S(2)}, u32[]{:S(2)}) %collective-permute-start.5) | collective-permute-done | bytes 393248 | tf_op jit(solution)/shard_map/ppermute | solution.py:153
  66.5 3.8 %collective-permute-start.6 = (f32[96,1024]{1,0:T(8,128)S(1)}, f32[96,1024]{1,0:T(8,128)S(1)}, u32[]{:S(2)}, u32[]{:S(2)}) collective-permute-start(f32[96,1024]{1,0:T(8,128)S(1)} %collective-permute-done.5.refs_7_), channel_id=1, source_target_pairs={{0,96},{32,128},{64,160},{96,192},{128,224},{160,256},{192,288},{2... | collective-permute-start | bytes 1179656 | tf_op jit(solution)/shard_map/ppermute | solution.py:153
  70.3 0.5 collective-permute-done.2.refs_1_
  70.8 1.9 %collective-permute-start.3 = (f32[96,1024]{1,0:T(8,128)S(1)}, f32[96,1024]{1,0:T(8,128)S(1)}, u32[]{:S(2)}, u32[]{:S(2)}) collective-permute-start(f32[96,1024]{1,0:T(8,128)S(1)} %collective-permute-done.2.refs_1_), channel_id=1, source_target_pairs={{0,672},{32,704},{64,736},{96,0},{128,32},{160,64},{192,96},{224,1... | collective-permute-start | bytes 1179656 | tf_op jit(solution)/shard_map/ppermute | solution.py:154
  72.7 6.2 %collective-permute-done.6.refs_6_ = f32[96,1024]{1,0:T(8,128)S(1)} collective-permute-done((f32[96,1024]{1,0:T(8,128)S(1)}, f32[96,1024]{1,0:T(8,128)S(1)}, u32[]{:S(2)}, u32[]{:S(2)}) %collective-permute-start.6) | collective-permute-done | bytes 393248 | tf_op jit(solution)/shard_map/ppermute | solution.py:153
  78.9 5.0 %collective-permute-start.7 = (f32[96,1024]{1,0:T(8,128)S(1)}, f32[96,1024]{1,0:T(8,128)S(1)}, u32[]{:S(2)}, u32[]{:S(2)}) collective-permute-start(f32[96,1024]{1,0:T(8,128)S(1)} %collective-permute-done.6.refs_6_), channel_id=1, source_target_pairs={{0,96},{32,128},{64,160},{96,192},{128,224},{160,256},{192,288},{2... | collective-permute-start | bytes 1179656 | tf_op jit(solution)/shard_map/ppermute | solution.py:153
  83.9 0.5 collective-permute-done.3.refs_2_
  84.4 1.9 %collective-permute-start.4 = (f32[96,1024]{1,0:T(8,128)S(1)}, f32[96,1024]{1,0:T(8,128)S(1)}, u32[]{:S(2)}, u32[]{:S(2)}) collective-permute-start(f32[96,1024]{1,0:T(8,128)S(1)} %collective-permute-done.3.refs_2_), channel_id=1, source_target_pairs={{0,672},{32,704},{64,736},{96,0},{128,32},{160,64},{192,96},{224,1... | collective-permute-start | bytes 1179656 | tf_op jit(solution)/shard_map/ppermute | solution.py:154
  86.3 4.7 %collective-permute-done.7.refs_5_ = f32[96,1024]{1,0:T(8,128)S(1)} collective-permute-done((f32[96,1024]{1,0:T(8,128)S(1)}, f32[96,1024]{1,0:T(8,128)S(1)}, u32[]{:S(2)}, u32[]{:S(2)}) %collective-permute-start.7) | collective-permute-done | bytes 393248 | tf_op jit(solution)/shard_map/ppermute | solution.py:153
  90.9 5.6 %collective-permute-start.8 = (f32[96,1024]{1,0:T(8,128)S(1)}, f32[96,1024]{1,0:T(8,128)S(1)}, u32[]{:S(2)}, u32[]{:S(2)}) collective-permute-start(f32[96,1024]{1,0:T(8,128)S(1)} %collective-permute-done.7.refs_5_), channel_id=1, source_target_pairs={{0,96},{32,128},{64,160},{96,192},{128,224},{160,256},{192,288},{2... | collective-permute-start | bytes 1179656 | tf_op jit(solution)/shard_map/ppermute | solution.py:156
  96.5 0.5 collective-permute-done.4.refs_3_
  97.0 5.6 %collective-permute-done.8.refs_4_ = f32[96,1024]{1,0:T(8,128)S(1)} collective-permute-done((f32[96,1024]{1,0:T(8,128)S(1)}, f32[96,1024]{1,0:T(8,128)S(1)}, u32[]{:S(2)}, u32[]{:S(2)}) %collective-permute-start.8) | collective-permute-done | bytes 393248 | tf_op jit(solution)/shard_map/ppermute | solution.py:156
  102.7 0.9 shard_map.56
  103.6 1.1 copy-done
  104.7 9.7 %all-to-all-done.1.pieces = f32[32,48,256]{2,1,0:T(8,128)S(1)} async-done(((f32[32,48,256]{2,1,0:T(8,128)}), f32[32,48,256]{2,1,0:T(8,128)S(1)}, u32[]{:S(2)}, u32[]{:S(2)}) %all-to-all-start.1) | async-done | bytes 1572896 | tf_op jit(solution)/shard_map/all_to_all | solution.py:195
  114.5 2.2 %shard_map.57 = (bf16[512,768]{1,0:T(8,128)(2,1)S(1)}, bf16[512,768]{1,0:T(8,128)(2,1)S(1)}) custom-call(s32[2]{0:T(128)S(1)} %pad_add_fusion.place, s32[32]{0:T(128)S(1)} %copy-done.5, f32[32,48,256]{2,1,0:T(8,128)S(1)} %all-to-all-done.1.pieces), custom_call_target="tpu_custom_call" | custom-call | bytes 3145728 | tf_op jit(solution)/shard_map/pallas_call | solution.py:137
  116.7 1.4 shard_map.59
  118.1 1.9 %collective-permute-start.9 = (f32[128,1024]{1,0:T(8,128)S(1)}, f32[128,1024]{1,0:T(8,128)S(1)}, u32[]{:S(2)}, u32[]{:S(2)}) collective-permute-start(f32[128,1024]{1,0:T(8,128)S(1)} %shard_map.59), channel_id=1, source_target_pairs={{0,1},{1,0},{2,3},{3,2},{4,5},{5,4},{6,7},{7,6},{8,9},{9,8},{10,11... | collective-permute-start | bytes 1572872 | tf_op jit(solution)/shard_map/ppermute | solution.py:220
  120.0 1.4 shard_map.58
  121.4 0.5 collective-permute-done.9
  121.9 12.5 %all_to_all.19 = f32[4,32,1024]{2,1,0:T(8,128)S(1)} all-to-all(f32[4,32,1024]{2,1,0:T(8,128)S(1)} %bitcast.18), channel_id=1, replica_groups={{0,8,16,24},{1,9,17,25},{2,10,18,26},{3,11,19,27},{4,12,20,28},{5,13,21..., dimensions={0} | all-to-all | bytes 1048576 | tf_op jit(solution)/shard_map/all_to_all | solution.py:223
  134.4 1.9 %collective-permute-start.10 = (f32[16,1024]{1,0:T(8,128)S(1)}, f32[16,1024]{1,0:T(8,128)S(1)}, u32[]{:S(2)}, u32[]{:S(2)}) collective-permute-start(f32[16,1024]{1,0:T(8,128)S(1)} %slice.9), channel_id=1, source_target_pairs={{0,2},{1,3},{2,0},{3,1},{4,6},{5,7},{6,4},{7,5},{8,10},{9,11},{10,... | collective-permute-start | bytes 196616 | tf_op jit(solution)/shard_map/ppermute | solution.py:225
  136.4 7.5 %collective-permute-done.10 = f32[16,1024]{1,0:T(8,128)S(1)} collective-permute-done((f32[16,1024]{1,0:T(8,128)S(1)}, f32[16,1024]{1,0:T(8,128)S(1)}, u32[]{:S(2)}, u32[]{:S(2)}) %collective-permute-start.10) | collective-permute-done | bytes 65568 | tf_op jit(solution)/shard_map/ppermute | solution.py:225
  143.9 0.1 reshape.153
  144.0 0.1 copy.28
  144.1 0.1 reshape.154
  144.3 0.6 fusion.4
  (23 shorter events, 0.6 us)
Async XLA Ops:
  1.8 34.9 %all-to-all-start = ((f32[32,2,1024]{2,1,0:T(2,128)}), f32[32,2,1024]{2,1,0:T(2,128)S(1)}, u32[]{:S(2)}, u32[]{:S(2)}) async-start(f32[32,2,1024]{2,1,0:T(2,128)} %bitcast.4), calls=%async_computation | async-start | bytes 524288 | tf_op jit(solution)/shard_map/all_to_all | solution.py:175
  19.2 1.4 copy-start.2
  20.6 0.7 copy-start.3
  21.3 0.7 copy-start.4
  21.9 3.3 %copy-start.5 = (s32[32]{0:T(128)S(1)}, s32[32]{0:T(128)}, u32[]{:S(2)}) copy-start(s32[32]{0:T(128)} %partner.1) | copy-start | bytes 388
  38.1 8.0 %collective-permute-start = (f32[32,1024]{1,0:T(8,128)S(1)}, f32[32,1024]{1,0:T(8,128)S(1)}, u32[]{:S(2)}, u32[]{:S(2)}) collective-permute-start(f32[32,1024]{1,0:T(8,128)S(1)} %fusion), channel_id=1, source_target_pairs={{0,32},{32,64},{64,0},{96,128},{128,160},{160,96},{192,224},{224,2... | collective-permute-start | bytes 393224 | tf_op jit(solution)/shard_map/ppermute | solution.py:192
  41.0 7.5 %collective-permute-start.1 = (f32[32,1024]{1,0:T(8,128)S(1)}, f32[32,1024]{1,0:T(8,128)S(1)}, u32[]{:S(2)}, u32[]{:S(2)}) collective-permute-start(f32[32,1024]{1,0:T(8,128)S(1)} %fusion), channel_id=1, source_target_pairs={{0,64},{32,0},{64,32},{96,160},{128,96},{160,128},{192,256},{224,1... | collective-permute-start | bytes 393224 | tf_op jit(solution)/shard_map/ppermute | solution.py:193
  48.5 66.0 %all-to-all-start.1 = ((f32[32,48,256]{2,1,0:T(8,128)}), f32[32,48,256]{2,1,0:T(8,128)S(1)}, u32[]{:S(2)}, u32[]{:S(2)}) async-start(f32[32,48,256]{2,1,0:T(8,128)} %shard_map.55), calls=%async_computation.1 | async-start | bytes 3145728 | tf_op jit(solution)/shard_map/all_to_all | solution.py:195
  53.3 13.2 %collective-permute-start.5 = (f32[96,1024]{1,0:T(8,128)S(1)}, f32[96,1024]{1,0:T(8,128)S(1)}, u32[]{:S(2)}, u32[]{:S(2)}) collective-permute-start(f32[96,1024]{1,0:T(8,128)S(1)} %pad_maximum_fusion.refs_0_), channel_id=1, source_target_pairs={{0,96},{32,128},{64,160},{96,192},{128,224},{160,256},{192,288},{2... | collective-permute-start | bytes 1179656 | tf_op jit(solution)/shard_map/ppermute | solution.py:153
  56.8 14.0 %collective-permute-start.2 = (f32[96,1024]{1,0:T(8,128)S(1)}, f32[96,1024]{1,0:T(8,128)S(1)}, u32[]{:S(2)}, u32[]{:S(2)}) collective-permute-start(f32[96,1024]{1,0:T(8,128)S(1)} %pad_maximum_fusion.refs_0_), channel_id=1, source_target_pairs={{0,672},{32,704},{64,736},{96,0},{128,32},{160,64},{192,96},{224,1... | collective-permute-start | bytes 1179656 | tf_op jit(solution)/shard_map/ppermute | solution.py:154
  66.5 12.4 %collective-permute-start.6 = (f32[96,1024]{1,0:T(8,128)S(1)}, f32[96,1024]{1,0:T(8,128)S(1)}, u32[]{:S(2)}, u32[]{:S(2)}) collective-permute-start(f32[96,1024]{1,0:T(8,128)S(1)} %collective-permute-done.5.refs_7_), channel_id=1, source_target_pairs={{0,96},{32,128},{64,160},{96,192},{128,224},{160,256},{192,288},{2... | collective-permute-start | bytes 1179656 | tf_op jit(solution)/shard_map/ppermute | solution.py:153
  70.8 13.6 %collective-permute-start.3 = (f32[96,1024]{1,0:T(8,128)S(1)}, f32[96,1024]{1,0:T(8,128)S(1)}, u32[]{:S(2)}, u32[]{:S(2)}) collective-permute-start(f32[96,1024]{1,0:T(8,128)S(1)} %collective-permute-done.2.refs_1_), channel_id=1, source_target_pairs={{0,672},{32,704},{64,736},{96,0},{128,32},{160,64},{192,96},{224,1... | collective-permute-start | bytes 1179656 | tf_op jit(solution)/shard_map/ppermute | solution.py:154
  78.9 12.1 %collective-permute-start.7 = (f32[96,1024]{1,0:T(8,128)S(1)}, f32[96,1024]{1,0:T(8,128)S(1)}, u32[]{:S(2)}, u32[]{:S(2)}) collective-permute-start(f32[96,1024]{1,0:T(8,128)S(1)} %collective-permute-done.6.refs_6_), channel_id=1, source_target_pairs={{0,96},{32,128},{64,160},{96,192},{128,224},{160,256},{192,288},{2... | collective-permute-start | bytes 1179656 | tf_op jit(solution)/shard_map/ppermute | solution.py:153
  84.4 12.7 %collective-permute-start.4 = (f32[96,1024]{1,0:T(8,128)S(1)}, f32[96,1024]{1,0:T(8,128)S(1)}, u32[]{:S(2)}, u32[]{:S(2)}) collective-permute-start(f32[96,1024]{1,0:T(8,128)S(1)} %collective-permute-done.3.refs_2_), channel_id=1, source_target_pairs={{0,672},{32,704},{64,736},{96,0},{128,32},{160,64},{192,96},{224,1... | collective-permute-start | bytes 1179656 | tf_op jit(solution)/shard_map/ppermute | solution.py:154
  90.9 11.7 %collective-permute-start.8 = (f32[96,1024]{1,0:T(8,128)S(1)}, f32[96,1024]{1,0:T(8,128)S(1)}, u32[]{:S(2)}, u32[]{:S(2)}) collective-permute-start(f32[96,1024]{1,0:T(8,128)S(1)} %collective-permute-done.7.refs_5_), channel_id=1, source_target_pairs={{0,96},{32,128},{64,160},{96,192},{128,224},{160,256},{192,288},{2... | collective-permute-start | bytes 1179656 | tf_op jit(solution)/shard_map/ppermute | solution.py:156
  103.6 1.1 copy-start
  114.5 2.2 %copy-start.1 = (bf16[768,1024]{1,0:T(8,128)(2,1)S(1)}, bf16[768,1024]{1,0:T(8,128)(2,1)}, u32[]{:S(2)}) copy-start(bf16[768,1024]{1,0:T(8,128)(2,1)} %copy-done) | copy-start | bytes 4718596
  118.1 3.8 %collective-permute-start.9 = (f32[128,1024]{1,0:T(8,128)S(1)}, f32[128,1024]{1,0:T(8,128)S(1)}, u32[]{:S(2)}, u32[]{:S(2)}) collective-permute-start(f32[128,1024]{1,0:T(8,128)S(1)} %shard_map.59), channel_id=1, source_target_pairs={{0,1},{1,0},{2,3},{3,2},{4,5},{5,4},{6,7},{7,6},{8,9},{9,8},{10,11... | collective-permute-start | bytes 1572872 | tf_op jit(solution)/shard_map/ppermute | solution.py:220
  134.4 9.4 %collective-permute-start.10 = (f32[16,1024]{1,0:T(8,128)S(1)}, f32[16,1024]{1,0:T(8,128)S(1)}, u32[]{:S(2)}, u32[]{:S(2)}) collective-permute-start(f32[16,1024]{1,0:T(8,128)S(1)} %slice.9), channel_id=1, source_target_pairs={{0,2},{1,3},{2,0},{3,1},{4,6},{5,7},{6,4},{7,5},{8,10},{9,11},{10,... | collective-permute-start | bytes 196616 | tf_op jit(solution)/shard_map/ppermute | solution.py:225

commit v11 on v10

--- a/solution.py
+++ b/solution.py
@@ -34,6 +34,14 @@
 def swap_ij(rows):
     count, cols = rows.shape
     return jnp.swapaxes(rows.reshape(count, NO, NO), 1, 2).reshape(count, cols)
+
+
+def rows_kernel(rows, out):
+    for x in range(NX):
+        for upper in range(2):
+            half = rows[x * 8 + upper * 4 : x * 8 + upper * 4 + 4, :]
+            out[x * 8 : x * 8 + 4, upper, :] = half
+            out[x * 8 + 4 : x * 8 + 8, upper, :] = half
 
 
 def pieces_kernel(place, row_irrep, col_irrep, block, out, turned, second):
@@ -170,8 +178,7 @@
 def local(integrals, amplitudes, row_irrep, col_irrep, partner):
     place = jnp.stack([lax.axis_index("narrow"), lax.axis_index("wide")]).astype(jnp.int32)
 
-    both = amplitudes.reshape(NX, 1, 2, 4, COLS).swapaxes(2, 3)
-    both = jnp.broadcast_to(both, (NX, 2, 4, 2, COLS)).reshape(NARROW, 2, COLS)
+    both = call(rows_kernel, jax.ShapeDtypeStruct((NARROW, 2, COLS), jnp.float32), [VMEM], (amplitudes,), 0, 3 << 17)
     rows = lax.all_to_all(both, "narrow", 0, 0, tiled=True).swapaxes(0, 1).reshape(2 * NARROW, COLS)
     pieces = call(
         pieces_kernel,

time: 146 us -> 145 us (level)
  the two profiles are of different devices: /device:TPU:80 before, /device:TPU:104 now
where the time goes in v11:
time: 145 us
  waiting for transfers between devices  62 us (43%)
  starting transfers between devices  51.9 us (36%)
  blocking collectives  12.5 us (9%)
  Pallas kernels  9.9 us (7%)
  local copies, waits for them, and re-layouts  5.92 us (4%)
  other arithmetic  1.85 us (1%)
    ppermute x3, waiting for transfers between devices, gather_y(): up = lax.ppermute(up, 'wide', y_shift(1))  20 us
    all_to_all x1, starting transfers between devices, local(): lax.all_to_all(both, 'narrow', 0, 0, tiled=True).swapaxes(0, 1)  16.5 us
    all_to_all x1, blocking collectives, local(): lax.all_to_all(chip, 'narrow', 0, 0, tiled=True, axis_index_groups=X_GROUPS)  12.5 us
    ppermute x3, starting transfers between devices, gather_y(): down = lax.ppermute(down, 'wide', y_shift(-1))  11.9 us
    all_to_all x1, waiting for transfers between devices, local(): lax.all_to_all(both, 'narrow', 0, 0, tiled=True).swapaxes(0, 1)  11.4 us
    pallas_call x6, Pallas kernels, call(): pl.pallas_call(kernel, out_shape=outs, in_specs=in_specs, out_specs=[VMEM...  9.9 us
    ppermute x1, waiting for transfers between devices, gather_y(): found[4] = lax.ppermute(up, 'wide', y_shift(1))  9.8 us
    all_to_all x1, waiting for transfers between devices, local(): pieces = lax.all_to_all(pieces, 'narrow', 0, 0, tiled=True)  8.31 us
  transfers between devices with their start and end apart: 13, of which 10 were waited for; matrix products, arithmetic and copies ran while one was open for 1% of the time, Pallas kernels for 4%

profile of v11, /device:TPU:104, one launch (start us, length us, event | category | flops | bytes accessed | tf_op | source)
XLA Modules:
  0.0 144.7 jit_solution(11227883765639603837)
XLA Ops:
  0.0 0.9 copy-done.3
  0.9 0.7 shard_map.56
  1.6 16.5 %all-to-all-start = ((f32[32,2,1024]{2,1,0:T(2,128)}), f32[32,2,1024]{2,1,0:T(2,128)S(1)}, u32[]{:S(2)}, u32[]{:S(2)}) async-start(f32[32,2,1024]{2,1,0:T(2,128)} %shard_map.56), calls=%async_computation | async-start | bytes 524288 | tf_op jit(solution)/shard_map/all_to_all | solution.py:182
  18.2 0.8 fusion.23
  19.0 1.4 copy-done.2
  20.4 0.7 copy-done.4
  21.1 0.7 copy-done.5
  21.7 3.3 %shard_map.55 = f32[32,48,256]{2,1,0:T(8,128)} custom-call(s32[2]{0:T(128)S(1)} %pad_add_fusion.place, s32[4]{0:T(128)S(1)} %copy-done.4, s32[6]{0:T(128)S(1)} %copy-done.5, f32[512,768]{1,0:T(8,128)S(1)} %copy-done.2), custom_call_target="tpu_custom_call" | custom-call | bytes 3145728 | tf_op jit(solution)/shard_map/pallas_call | solution.py:145
  25.0 0.1 fusion.22
  25.1 0.1 convert_reduce_fusion
  25.2 11.4 %all-to-all-done = f32[32,2,1024]{2,1,0:T(2,128)S(1)} async-done(((f32[32,2,1024]{2,1,0:T(2,128)}), f32[32,2,1024]{2,1,0:T(2,128)S(1)}, u32[]{:S(2)}, u32[]{:S(2)}) %all-to-all-start) | async-done | bytes 262176 | tf_op jit(solution)/shard_map/all_to_all | solution.py:182
  36.6 0.1 copy.14
  36.6 0.2 copy.15
  36.9 0.3 copy.16
  37.2 0.2 copy.17
  37.4 0.2 fusion.2
  37.6 0.3 fusion
  37.9 3.0 %collective-permute-start = (f32[32,1024]{1,0:T(8,128)S(1)}, f32[32,1024]{1,0:T(8,128)S(1)}, u32[]{:S(2)}, u32[]{:S(2)}) collective-permute-start(f32[32,1024]{1,0:T(8,128)S(1)} %fusion), channel_id=1, source_target_pairs={{0,32},{32,64},{64,0},{96,128},{128,160},{160,96},{192,224},{224,2... | collective-permute-start | bytes 393224 | tf_op jit(solution)/shard_map/ppermute | solution.py:199
  40.8 2.9 %collective-permute-start.1 = (f32[32,1024]{1,0:T(8,128)S(1)}, f32[32,1024]{1,0:T(8,128)S(1)}, u32[]{:S(2)}, u32[]{:S(2)}) collective-permute-start(f32[32,1024]{1,0:T(8,128)S(1)} %fusion), channel_id=1, source_target_pairs={{0,64},{32,0},{64,32},{96,160},{128,96},{160,128},{192,256},{224,1... | collective-permute-start | bytes 393224 | tf_op jit(solution)/shard_map/ppermute | solution.py:200
  43.8 2.1 %collective-permute-done = f32[32,1024]{1,0:T(8,128)S(1)} collective-permute-done((f32[32,1024]{1,0:T(8,128)S(1)}, f32[32,1024]{1,0:T(8,128)S(1)}, u32[]{:S(2)}, u32[]{:S(2)}) %collective-permute-start) | collective-permute-done | bytes 131104 | tf_op jit(solution)/shard_map/ppermute | solution.py:199
  45.8 2.4 %collective-permute-done.1 = f32[32,1024]{1,0:T(8,128)S(1)} collective-permute-done((f32[32,1024]{1,0:T(8,128)S(1)}, f32[32,1024]{1,0:T(8,128)S(1)}, u32[]{:S(2)}, u32[]{:S(2)}) %collective-permute-start.1) | collective-permute-done | bytes 131104 | tf_op jit(solution)/shard_map/ppermute | solution.py:200
  48.3 4.8 %all-to-all-start.1 = ((f32[32,48,256]{2,1,0:T(8,128)}), f32[32,48,256]{2,1,0:T(8,128)S(1)}, u32[]{:S(2)}, u32[]{:S(2)}) async-start(f32[32,48,256]{2,1,0:T(8,128)} %shard_map.55), calls=%async_computation.1 | async-start | bytes 3145728 | tf_op jit(solution)/shard_map/all_to_all | solution.py:202
  53.1 2.6 %collective-permute-start.5 = (f32[96,1024]{1,0:T(8,128)S(1)}, f32[96,1024]{1,0:T(8,128)S(1)}, u32[]{:S(2)}, u32[]{:S(2)}) collective-permute-start(f32[96,1024]{1,0:T(8,128)S(1)} %pad_maximum_fusion.refs_0_), channel_id=1, source_target_pairs={{0,96},{32,128},{64,160},{96,192},{128,224},{160,256},{192,288},{2... | collective-permute-start | bytes 1179656 | tf_op jit(solution)/shard_map/ppermute | solution.py:161
  55.7 3.3 %collective-permute-start.2 = (f32[96,1024]{1,0:T(8,128)S(1)}, f32[96,1024]{1,0:T(8,128)S(1)}, u32[]{:S(2)}, u32[]{:S(2)}) collective-permute-start(f32[96,1024]{1,0:T(8,128)S(1)} %pad_maximum_fusion.refs_0_), channel_id=1, source_target_pairs={{0,672},{32,704},{64,736},{96,0},{128,32},{160,64},{192,96},{224,1... | collective-permute-start | bytes 1179656 | tf_op jit(solution)/shard_map/ppermute | solution.py:162
  59.0 7.3 %collective-permute-done.5.refs_7_ = f32[96,1024]{1,0:T(8,128)S(1)} collective-permute-done((f32[96,1024]{1,0:T(8,128)S(1)}, f32[96,1024]{1,0:T(8,128)S(1)}, u32[]{:S(2)}, u32[]{:S(2)}) %collective-permute-start.5) | collective-permute-done | bytes 393248 | tf_op jit(solution)/shard_map/ppermute | solution.py:161
  66.3 2.6 %collective-permute-start.6 = (f32[96,1024]{1,0:T(8,128)S(1)}, f32[96,1024]{1,0:T(8,128)S(1)}, u32[]{:S(2)}, u32[]{:S(2)}) collective-permute-start(f32[96,1024]{1,0:T(8,128)S(1)} %collective-permute-done.5.refs_7_), channel_id=1, source_target_pairs={{0,96},{32,128},{64,160},{96,192},{128,224},{160,256},{192,288},{2... | collective-permute-start | bytes 1179656 | tf_op jit(solution)/shard_map/ppermute | solution.py:161
  68.9 3.8 %collective-permute-start.3 = (f32[96,1024]{1,0:T(8,128)S(1)}, f32[96,1024]{1,0:T(8,128)S(1)}, u32[]{:S(2)}, u32[]{:S(2)}) collective-permute-start(f32[96,1024]{1,0:T(8,128)S(1)} %collective-permute-done.2.refs_1_), channel_id=1, source_target_pairs={{0,672},{32,704},{64,736},{96,0},{128,32},{160,64},{192,96},{224,1... | collective-permute-start | bytes 1179656 | tf_op jit(solution)/shard_map/ppermute | solution.py:162
  72.7 6.8 %collective-permute-done.6.refs_6_ = f32[96,1024]{1,0:T(8,128)S(1)} collective-permute-done((f32[96,1024]{1,0:T(8,128)S(1)}, f32[96,1024]{1,0:T(8,128)S(1)}, u32[]{:S(2)}, u32[]{:S(2)}) %collective-permute-start.6) | collective-permute-done | bytes 393248 | tf_op jit(solution)/shard_map/ppermute | solution.py:161
  79.5 1.9 %collective-permute-start.7 = (f32[96,1024]{1,0:T(8,128)S(1)}, f32[96,1024]{1,0:T(8,128)S(1)}, u32[]{:S(2)}, u32[]{:S(2)}) collective-permute-start(f32[96,1024]{1,0:T(8,128)S(1)} %collective-permute-done.6.refs_6_), channel_id=1, source_target_pairs={{0,96},{32,128},{64,160},{96,192},{128,224},{160,256},{192,288},{2... | collective-permute-start | bytes 1179656 | tf_op jit(solution)/shard_map/ppermute | solution.py:161
  81.4 4.9 %collective-permute-start.4 = (f32[96,1024]{1,0:T(8,128)S(1)}, f32[96,1024]{1,0:T(8,128)S(1)}, u32[]{:S(2)}, u32[]{:S(2)}) collective-permute-start(f32[96,1024]{1,0:T(8,128)S(1)} %collective-permute-done.3.refs_2_), channel_id=1, source_target_pairs={{0,672},{32,704},{64,736},{96,0},{128,32},{160,64},{192,96},{224,1... | collective-permute-start | bytes 1179656 | tf_op jit(solution)/shard_map/ppermute | solution.py:162
  86.3 5.9 %collective-permute-done.7.refs_5_ = f32[96,1024]{1,0:T(8,128)S(1)} collective-permute-done((f32[96,1024]{1,0:T(8,128)S(1)}, f32[96,1024]{1,0:T(8,128)S(1)}, u32[]{:S(2)}, u32[]{:S(2)}) %collective-permute-start.7) | collective-permute-done | bytes 393248 | tf_op jit(solution)/shard_map/ppermute | solution.py:161
  92.2 1.9 %collective-permute-start.8 = (f32[96,1024]{1,0:T(8,128)S(1)}, f32[96,1024]{1,0:T(8,128)S(1)}, u32[]{:S(2)}, u32[]{:S(2)}) collective-permute-start(f32[96,1024]{1,0:T(8,128)S(1)} %collective-permute-done.7.refs_5_), channel_id=1, source_target_pairs={{0,96},{32,128},{64,160},{96,192},{128,224},{160,256},{192,288},{2... | collective-permute-start | bytes 1179656 | tf_op jit(solution)/shard_map/ppermute | solution.py:164
  94.1 9.8 %collective-permute-done.8.refs_4_ = f32[96,1024]{1,0:T(8,128)S(1)} collective-permute-done((f32[96,1024]{1,0:T(8,128)S(1)}, f32[96,1024]{1,0:T(8,128)S(1)}, u32[]{:S(2)}, u32[]{:S(2)}) %collective-permute-start.8) | collective-permute-done | bytes 393248 | tf_op jit(solution)/shard_map/ppermute | solution.py:164
  103.9 0.9 shard_map.57
  104.8 1.1 copy-done
  106.0 8.3 %all-to-all-done.1.pieces = f32[32,48,256]{2,1,0:T(8,128)S(1)} async-done(((f32[32,48,256]{2,1,0:T(8,128)}), f32[32,48,256]{2,1,0:T(8,128)S(1)}, u32[]{:S(2)}, u32[]{:S(2)}) %all-to-all-start.1) | async-done | bytes 1572896 | tf_op jit(solution)/shard_map/all_to_all | solution.py:202
  114.3 2.2 %shard_map.58 = (bf16[512,768]{1,0:T(8,128)(2,1)S(1)}, bf16[512,768]{1,0:T(8,128)(2,1)S(1)}) custom-call(s32[2]{0:T(128)S(1)} %pad_add_fusion.place, s32[32]{0:T(128)S(1)} %copy-done.6, f32[32,48,256]{2,1,0:T(8,128)S(1)} %all-to-all-done.1.pieces), custom_call_target="tpu_custom_call" | custom-call | bytes 3145728 | tf_op jit(solution)/shard_map/pallas_call | solution.py:145
  116.5 1.4 shard_map.60
  117.9 1.9 %collective-permute-start.9 = (f32[128,1024]{1,0:T(8,128)S(1)}, f32[128,1024]{1,0:T(8,128)S(1)}, u32[]{:S(2)}, u32[]{:S(2)}) collective-permute-start(f32[128,1024]{1,0:T(8,128)S(1)} %shard_map.60), channel_id=1, source_target_pairs={{0,1},{1,0},{2,3},{3,2},{4,5},{5,4},{6,7},{7,6},{8,9},{9,8},{10,11... | collective-permute-start | bytes 1572872 | tf_op jit(solution)/shard_map/ppermute | solution.py:227
  119.8 1.4 shard_map.59
  121.2 0.5 collective-permute-done.9
  121.7 12.5 %all_to_all.19 = f32[4,32,1024]{2,1,0:T(8,128)S(1)} all-to-all(f32[4,32,1024]{2,1,0:T(8,128)S(1)} %bitcast.13), channel_id=1, replica_groups={{0,8,16,24},{1,9,17,25},{2,10,18,26},{3,11,19,27},{4,12,20,28},{5,13,21..., dimensions={0} | all-to-all | bytes 1048576 | tf_op jit(solution)/shard_map/all_to_all | solution.py:230
  134.2 1.9 %collective-permute-start.10 = (f32[16,1024]{1,0:T(8,128)S(1)}, f32[16,1024]{1,0:T(8,128)S(1)}, u32[]{:S(2)}, u32[]{:S(2)}) collective-permute-start(f32[16,1024]{1,0:T(8,128)S(1)} %slice.9), channel_id=1, source_target_pairs={{0,2},{1,3},{2,0},{3,1},{4,6},{5,7},{6,4},{7,5},{8,10},{9,11},{10,... | collective-permute-start | bytes 196616 | tf_op jit(solution)/shard_map/ppermute | solution.py:232
  136.2 7.5 %collective-permute-done.10 = f32[16,1024]{1,0:T(8,128)S(1)} collective-permute-done((f32[16,1024]{1,0:T(8,128)S(1)}, f32[16,1024]{1,0:T(8,128)S(1)}, u32[]{:S(2)}, u32[]{:S(2)}) %collective-permute-start.10) | collective-permute-done | bytes 65568 | tf_op jit(solution)/shard_map/ppermute | solution.py:232
  143.7 0.1 reshape.145
  143.8 0.1 copy.19
  143.9 0.1 reshape.146
  144.1 0.6 fusion.4
  (23 shorter events, 0.3 us)
Async XLA Ops:
  0.0 0.9 copy-start.3
  1.6 34.9 %all-to-all-start = ((f32[32,2,1024]{2,1,0:T(2,128)}), f32[32,2,1024]{2,1,0:T(2,128)S(1)}, u32[]{:S(2)}, u32[]{:S(2)}) async-start(f32[32,2,1024]{2,1,0:T(2,128)} %shard_map.56), calls=%async_computation | async-start | bytes 524288 | tf_op jit(solution)/shard_map/all_to_all | solution.py:182
  19.0 1.4 copy-start.2
  20.4 0.7 copy-start.4
  21.1 0.7 copy-start.5
  21.7 3.3 %copy-start.6 = (s32[32]{0:T(128)S(1)}, s32[32]{0:T(128)}, u32[]{:S(2)}) copy-start(s32[32]{0:T(128)} %partner.1) | copy-start | bytes 388
  37.9 8.0 %collective-permute-start = (f32[32,1024]{1,0:T(8,128)S(1)}, f32[32,1024]{1,0:T(8,128)S(1)}, u32[]{:S(2)}, u32[]{:S(2)}) collective-permute-start(f32[32,1024]{1,0:T(8,128)S(1)} %fusion), channel_id=1, source_target_pairs={{0,32},{32,64},{64,0},{96,128},{128,160},{160,96},{192,224},{224,2... | collective-permute-start | bytes 393224 | tf_op jit(solution)/shard_map/ppermute | solution.py:199
  40.8 7.5 %collective-permute-start.1 = (f32[32,1024]{1,0:T(8,128)S(1)}, f32[32,1024]{1,0:T(8,128)S(1)}, u32[]{:S(2)}, u32[]{:S(2)}) collective-permute-start(f32[32,1024]{1,0:T(8,128)S(1)} %fusion), channel_id=1, source_target_pairs={{0,64},{32,0},{64,32},{96,160},{128,96},{160,128},{192,256},{224,1... | collective-permute-start | bytes 393224 | tf_op jit(solution)/shard_map/ppermute | solution.py:200
  48.3 66.0 %all-to-all-start.1 = ((f32[32,48,256]{2,1,0:T(8,128)}), f32[32,48,256]{2,1,0:T(8,128)S(1)}, u32[]{:S(2)}, u32[]{:S(2)}) async-start(f32[32,48,256]{2,1,0:T(8,128)} %shard_map.55), calls=%async_computation.1 | async-start | bytes 3145728 | tf_op jit(solution)/shard_map/all_to_all | solution.py:202
  53.1 13.2 %collective-permute-start.5 = (f32[96,1024]{1,0:T(8,128)S(1)}, f32[96,1024]{1,0:T(8,128)S(1)}, u32[]{:S(2)}, u32[]{:S(2)}) collective-permute-start(f32[96,1024]{1,0:T(8,128)S(1)} %pad_maximum_fusion.refs_0_), channel_id=1, source_target_pairs={{0,96},{32,128},{64,160},{96,192},{128,224},{160,256},{192,288},{2... | collective-permute-start | bytes 1179656 | tf_op jit(solution)/shard_map/ppermute | solution.py:161
  55.7 13.2 %collective-permute-start.2 = (f32[96,1024]{1,0:T(8,128)S(1)}, f32[96,1024]{1,0:T(8,128)S(1)}, u32[]{:S(2)}, u32[]{:S(2)}) collective-permute-start(f32[96,1024]{1,0:T(8,128)S(1)} %pad_maximum_fusion.refs_0_), channel_id=1, source_target_pairs={{0,672},{32,704},{64,736},{96,0},{128,32},{160,64},{192,96},{224,1... | collective-permute-start | bytes 1179656 | tf_op jit(solution)/shard_map/ppermute | solution.py:162
  66.3 13.2 %collective-permute-start.6 = (f32[96,1024]{1,0:T(8,128)S(1)}, f32[96,1024]{1,0:T(8,128)S(1)}, u32[]{:S(2)}, u32[]{:S(2)}) collective-permute-start(f32[96,1024]{1,0:T(8,128)S(1)} %collective-permute-done.5.refs_7_), channel_id=1, source_target_pairs={{0,96},{32,128},{64,160},{96,192},{128,224},{160,256},{192,288},{2... | collective-permute-start | bytes 1179656 | tf_op jit(solution)/shard_map/ppermute | solution.py:161
  68.9 12.5 %collective-permute-start.3 = (f32[96,1024]{1,0:T(8,128)S(1)}, f32[96,1024]{1,0:T(8,128)S(1)}, u32[]{:S(2)}, u32[]{:S(2)}) collective-permute-start(f32[96,1024]{1,0:T(8,128)S(1)} %collective-permute-done.2.refs_1_), channel_id=1, source_target_pairs={{0,672},{32,704},{64,736},{96,0},{128,32},{160,64},{192,96},{224,1... | collective-permute-start | bytes 1179656 | tf_op jit(solution)/shard_map/ppermute | solution.py:162
  79.5 12.7 %collective-permute-start.7 = (f32[96,1024]{1,0:T(8,128)S(1)}, f32[96,1024]{1,0:T(8,128)S(1)}, u32[]{:S(2)}, u32[]{:S(2)}) collective-permute-start(f32[96,1024]{1,0:T(8,128)S(1)} %collective-permute-done.6.refs_6_), channel_id=1, source_target_pairs={{0,96},{32,128},{64,160},{96,192},{128,224},{160,256},{192,288},{2... | collective-permute-start | bytes 1179656 | tf_op jit(solution)/shard_map/ppermute | solution.py:161
  81.4 12.6 %collective-permute-start.4 = (f32[96,1024]{1,0:T(8,128)S(1)}, f32[96,1024]{1,0:T(8,128)S(1)}, u32[]{:S(2)}, u32[]{:S(2)}) collective-permute-start(f32[96,1024]{1,0:T(8,128)S(1)} %collective-permute-done.3.refs_2_), channel_id=1, source_target_pairs={{0,672},{32,704},{64,736},{96,0},{128,32},{160,64},{192,96},{224,1... | collective-permute-start | bytes 1179656 | tf_op jit(solution)/shard_map/ppermute | solution.py:162
  92.2 11.7 %collective-permute-start.8 = (f32[96,1024]{1,0:T(8,128)S(1)}, f32[96,1024]{1,0:T(8,128)S(1)}, u32[]{:S(2)}, u32[]{:S(2)}) collective-permute-start(f32[96,1024]{1,0:T(8,128)S(1)} %collective-permute-done.7.refs_5_), channel_id=1, source_target_pairs={{0,96},{32,128},{64,160},{96,192},{128,224},{160,256},{192,288},{2... | collective-permute-start | bytes 1179656 | tf_op jit(solution)/shard_map/ppermute | solution.py:164
  104.8 1.1 copy-start
  114.3 2.2 %copy-start.1 = (bf16[768,1024]{1,0:T(8,128)(2,1)S(1)}, bf16[768,1024]{1,0:T(8,128)(2,1)}, u32[]{:S(2)}) copy-start(bf16[768,1024]{1,0:T(8,128)(2,1)} %copy-done) | copy-start | bytes 4718596
  117.9 3.8 %collective-permute-start.9 = (f32[128,1024]{1,0:T(8,128)S(1)}, f32[128,1024]{1,0:T(8,128)S(1)}, u32[]{:S(2)}, u32[]{:S(2)}) collective-permute-start(f32[128,1024]{1,0:T(8,128)S(1)} %shard_map.60), channel_id=1, source_target_pairs={{0,1},{1,0},{2,3},{3,2},{4,5},{5,4},{6,7},{7,6},{8,9},{9,8},{10,11... | collective-permute-start | bytes 1572872 | tf_op jit(solution)/shard_map/ppermute | solution.py:227
  134.2 9.4 %collective-permute-start.10 = (f32[16,1024]{1,0:T(8,128)S(1)}, f32[16,1024]{1,0:T(8,128)S(1)}, u32[]{:S(2)}, u32[]{:S(2)}) collective-permute-start(f32[16,1024]{1,0:T(8,128)S(1)} %slice.9), channel_id=1, source_target_pairs={{0,2},{1,3},{2,0},{3,1},{4,6},{5,7},{6,4},{7,5},{8,10},{9,11},{10,... | collective-permute-start | bytes 196616 | tf_op jit(solution)/shard_map/ppermute | solution.py:232
